TPU v7x, 256 devices: a whole 4x4x8 slice. The times are simulated.
256 devices in a mesh: tok: 16 (over y, x_hi, core), lat: 16 (over x_lo, z).
Axes of the slice: x: 4 (x_hi: 2, x_lo: 2; x = x_hi * 2 + x_lo), y: 4, z: 8, core: 2. Of those that a mesh axis runs over, the one named last changes fastest.
Arguments:
- tokens: bfloat16 [1024, 3584], P('tok'), may hold values from -8 to 8
- dec_bias: float32 [3584], replicated, may hold values from -3 to 3
- enc_weight: bfloat16 [3584, 131072], P('tok', 'lat'), may hold values from -0.09375 to 0.09375
- enc_bias: float32 [131072], P('lat'), may hold values from -3 to -1
Outputs:
- gram: bfloat16 [4096, 131072], P('tok', 'lat')
All inputs are finite; a program needn't handle non-finite values.
Results may differ from a plain program's by a relative error of at most 0.0045.
Values may be sent and summed in bfloat16 or wider, within the bound.
No kernel may reach another device: no remote copies, remote signals or barrier semaphores. Data moves between devices by JAX's collectives and lax.ppermute only.
A program may use at most 128 MiB of HBM per device.

v0:
```python
import jax
import jax.numpy as jnp
from jax import lax
from jax.sharding import PartitionSpec as P

PANEL = 4096


def spread_2(shard, axis, root):
    mine = lax.axis_index(axis) == root
    return lax.psum(jnp.where(mine, shard, jnp.zeros_like(shard)), axis)


def encode(rows, weight, bias):
    pre = jnp.dot(rows, weight, preferred_element_type=jnp.float32) + bias
    return jnp.maximum(pre, 0.0).astype(jnp.bfloat16)


def per_device(tokens, dec_bias, enc_weight, enc_bias):
    tok_count = lax.axis_size("tok")
    here = lax.axis_index("tok")
    width_rows, slab = enc_weight.shape
    own_latents = slab // tok_count
    panel_share = PANEL // tok_count
    spread = enc_weight.reshape(width_rows, own_latents, tok_count).transpose(0, 2, 1)
    received = lax.all_to_all(spread, "tok", split_axis=1, concat_axis=0, tiled=True)
    own_weight = received.reshape(width_rows * tok_count, own_latents)
    own_bias = lax.dynamic_index_in_dim(
        enc_bias.reshape(own_latents, tok_count), here, axis=1, keepdims=False
    )
    centered = (tokens.astype(jnp.float32) - dec_bias).astype(jnp.bfloat16)
    activity = encode(lax.all_gather(centered, "tok", axis=0, tiled=True), own_weight, own_bias)
    leading = activity[:, :panel_share]
    total = activity.shape[0]
    columns = lax.all_gather(leading, "tok", axis=1, tiled=True)
    panel = spread_2(columns, "lat", 0)
    summed = lax.dot_general(
        panel, activity, (((0,), (0,)), ((), ())), preferred_element_type=jnp.float32
    )
    local_gram = (summed / total).astype(jnp.bfloat16)
    row_groups = panel_share // tok_count
    blocks = local_gram.reshape(tok_count, tok_count, row_groups, own_latents)
    moved = lax.all_to_all(blocks, "tok", split_axis=1, concat_axis=1, tiled=True)
    return moved.transpose(2, 0, 3, 1).reshape(panel_share, slab)


def solution(mesh):
    return jax.shard_map(
        per_device,
        mesh=mesh,
        in_specs=(P("tok", None), P(), P("tok", "lat"), P("lat")),
        out_specs=P("tok", "lat"),
        check_vma=False,
    )
```

profile of v0, /device:TPU:2, one launch (start us, length us, event | category | flops | bytes accessed | tf_op | source)
XLA Modules:
  0.0 561.5 jit_solution(6993315360342371203)
XLA Ops:
  6.5 0.0 all-gather.3.cloned.1.call-start
  6.5 1.9 subtract_convert_fusion
  8.4 0.0 all-gather.3.cloned.1.call-update
  8.5 6.2 %copy.9 = bf16[224,8192]{0,1:T(8,128)(2,1)} copy(bf16[224,8192]{1,0:T(8,128)(2,1)} %param.6) | data formatting | bytes 7340032 | tf_op args[2]
  14.7 7.9 %copy.10 = bf16[224,16,512]{2,0,1:T(8,128)(2,1)} copy(bf16[224,16,512]{0,1,2:T(8,128)(2,1)} %bitcast.17) | data formatting | bytes 7340032 | tf_op jit(solution)/shard_map/transpose | solution.py:25
  22.5 6.3 %all-to-all-start = ((bf16[224,16,512]{2,0,1:T(8,128)(2,1)}), bf16[224,16,512]{2,0,1:T(8,128)(2,1)}, u32[]{:S(2)}, u32[]{:S(2)}) async-start(bf16[224,16,512]{2,0,1:T(8,128)(2,1)} %copy.10), calls=%async_computation | async-start | bytes 7340032 | tf_op jit(solution)/shard_map/all_to_all | solution.py:26
  28.9 0.0 all-gather.5.cloned.1.call-start
  28.9 0.1 reshape.21
  29.1 0.2 dynamic-slice_reduce_fusion
  29.3 48.1 %all-to-all-done = bf16[224,16,512]{2,0,1:T(8,128)(2,1)} async-done(((bf16[224,16,512]{2,0,1:T(8,128)(2,1)}), bf16[224,16,512]{2,0,1:T(8,128)(2,1)}, u32[]{:S(2)}, u32[]{:S(2)}) %all-to-all-start) | async-done | bytes 3670048 | tf_op jit(solution)/shard_map/all_to_all | solution.py:26
  77.4 35.2 %all-gather.3.cloned.1.call-done = bf16[1024,3584]{1,0:T(8,128)(2,1)} async-done(((bf16[64,3584]{1,0:T(8,128)(2,1)}), bf16[1024,3584]{1,0:T(8,128)(2,1)}) %all-gather.3.cloned.1.call-update) | async-done | bytes 7340048 | tf_op jit(solution)/shard_map/all_gather | solution.py:32
  112.6 8.1 %maximum_convert_fusion = bf16[1024,512]{1,0:T(8,128)(2,1)S(1)} fusion(bf16[1024,3584]{1,0:T(8,128)(2,1)} %all-gather.3.cloned.1.call-done, bf16[3584,512]{1,0:T(8,128)(2,1)} %bitcast.4, f32[512]{0:T(512)S(1)} %dynamic-slice_reduce_fusion), kind=kOutput, calls=%fused_computation.2 | convolution fusion | flops 3759669248 | bytes 12060672 | tf_op jit(solution)/shard_map/dot_general | solution.py:15
  120.7 0.8 slice.4
  121.5 0.0 all-gather.5.cloned.1.call-update
  121.5 0.0 all-reduce.2.cloned.1.call-start
  121.6 80.1 %all-gather.5.cloned.1.call-done = bf16[1024,4096]{1,0:T(8,128)(2,1)} async-done(((bf16[1024,256]{1,0:T(8,128)(2,1)}), bf16[1024,4096]{1,0:T(8,128)(2,1)}) %all-gather.5.cloned.1.call-update) | async-done | bytes 8388624 | tf_op jit(solution)/shard_map/all_gather | solution.py:35
  201.7 3.8 broadcast_select_fusion
  205.5 0.0 all-reduce.2.cloned.1.call-update
  205.5 198.4 %all-reduce.2.cloned.1.call-done = bf16[1024,4096]{1,0:T(8,128)(2,1)} async-done(((bf16[1024,4096]{1,0:T(8,128)(2,1)}), bf16[1024,4096]{1,0:T(8,128)(2,1)}) %all-reduce.2.cloned.1.call-update) | async-done | bytes 8388624 | tf_op jit(solution)/shard_map/psum | solution.py:11
  403.9 8.4 %multiply_convert_fusion = bf16[4096,512]{1,0:T(8,128)(2,1)S(1)} fusion(bf16[1024,4096]{1,0:T(8,128)(2,1)} %all-reduce.2.cloned.1.call-done, bf16[1024,512]{1,0:T(8,128)(2,1)S(1)} %maximum_convert_fusion), kind=kOutput, calls=%fused_computation | convolution fusion | flops 4299161600 | bytes 13631488 | tf_op jit(solution)/shard_map/dot_general | solution.py:37
  412.3 0.6 copy.11
  412.9 57.8 %all_to_all.20 = bf16[16,16,16,512]{3,2,0,1:T(8,128)(2,1)} all-to-all(bf16[16,16,16,512]{3,2,0,1:T(8,128)(2,1)S(1)} %copy.11), channel_id=1, replica_groups=mesh['tok'=16,'lat'=16] {'tok'}, dimensions={1} | all-to-all | bytes 8388608 | tf_op jit(solution)/shard_map/all_to_all | solution.py:43
  470.7 26.7 %copy.12 = bf16[16,16,512,16]{3,2,1,0:T(8,128)(2,1)} copy(bf16[16,16,512,16]{2,0,1,3:T(8,128)(2,1)} %bitcast.16) | data formatting | bytes 8388608 | tf_op jit(solution)/shard_map/transpose | solution.py:44
  497.4 57.6 %reshape.23 = bf16[256,8192]{1,0:T(8,128)(2,1)} reshape(bf16[16,16,512,16]{3,2,1,0:T(8,128)(2,1)} %copy.12) | data formatting | bytes 8388608 | tf_op jit(solution)/shard_map/reshape | solution.py:44
  (2 shorter events, 0.0 us)
Async XLA Ops:
  6.5 106.1 %all-gather.3.cloned.1.call-start = ((), (), s32[]{:S(2)}) async-start(), calls=%async_computation.2 | async-start | bytes 7798784 | tf_op jit(solution)/shard_map/all_gather | solution.py:32
  22.5 6.4 %copy-start = (f32[8192]{0:T(1024)S(1)}, f32[8192]{0:T(1024)}, u32[]{:S(2)}) copy-start(f32[8192]{0:T(1024)} %param.7) | copy-start | bytes 98308
  22.5 54.8 %all-to-all-start = ((bf16[224,16,512]{2,0,1:T(8,128)(2,1)}), bf16[224,16,512]{2,0,1:T(8,128)(2,1)}, u32[]{:S(2)}, u32[]{:S(2)}) async-start(bf16[224,16,512]{2,0,1:T(8,128)(2,1)} %copy.10), calls=%async_computation | async-start | bytes 7340032 | tf_op jit(solution)/shard_map/all_to_all | solution.py:26
  28.9 172.8 %all-gather.5.cloned.1.call-start = ((), (), s32[]{:S(2)}) async-start(), calls=%async_computation.3 | async-start | bytes 8912896 | tf_op jit(solution)/shard_map/all_gather | solution.py:35
  121.5 282.3 %all-reduce.2.cloned.1.call-start = ((), (), s32[]{:S(2)}) async-start(), calls=%async_computation.4 | async-start | bytes 16777216 | tf_op jit(solution)/shard_map/psum | solution.py:11
Sparse Core Ops, SparseCore 0:
  10.1 102.4 all-gather.2
  121.6 79.9 all-gather.4
  205.6 198.2 all-reduce.1
where the time goes:
time: 564 us; the launch traced here: 562 us
  waiting for transfers between devices  362 us (64%)
  local copies, waits for them, and re-layouts  100 us (18%)
  blocking collectives  57.8 us (10%)
  matrix products  16.5 us (3%)
  between operations  13.2 us (2%)
  starting transfers between devices  6.4 us (1%)
  other arithmetic  5.66 us (1%)
    psum x1, waiting for transfers between devices, spread_2(): return lax.psum(jnp.where(mine, shard, jnp.zeros_like(shard)), axis)  198 us
    all_gather x1, waiting for transfers between devices, per_device(): columns = lax.all_gather(leading, 'tok', axis=1, tiled=True)  80.1 us
    all_to_all x1, blocking collectives, per_device(): lax.all_to_all(blocks, 'tok', split_axis=1, concat_axis=1, tiled=True)  57.8 us
    reshape x1, local copies, waits for them, and re-layouts, per_device(): return moved.transpose(2, 0, 3, 1).reshape(panel_share, slab)  57.6 us
    all_to_all x1, waiting for transfers between devices, per_device(): lax.all_to_all(spread, 'tok', split_axis=1, concat_axis=0, tiled=True)  48.1 us
    all_gather x1, waiting for transfers between devices, per_device(): lax.all_gather(centered, 'tok', axis=0, tiled=True)  35.2 us
    transpose x1, local copies, waits for them, and re-layouts, per_device(): return moved.transpose(2, 0, 3, 1).reshape(panel_share, slab)  26.7 us
  transfers between devices with their start and end apart: 4, of which 4 were waited for; matrix products, arithmetic and copies ran while one was open for 3% of the time, Pallas kernels for 0%

commit v1 on v0

v1 whole, which is shorter than its diff:
```python
import jax
import jax.numpy as jnp
from jax import lax
from jax.sharding import Mesh, PartitionSpec as P

AXES = ("y", "xh", "c", "xl", "z")
SIZES = (4, 2, 2, 2, 8)
PLANE = ("y", "xh")
TOK = ("y", "xh", "c")
LATENT = ("xl", "z")
CHIPS, CORES, XLO, DEPTH = 8, 2, 2, 8
SWAP = [(0, 1), (1, 0)]


def exchange(block, axes):
    return lax.all_to_all(block, axes, split_axis=0, concat_axis=0, tiled=True)


def spread(block, axes, count):
    copies = jnp.broadcast_to(block[None], (count,) + block.shape)
    return exchange(copies, axes)


def ring(block, step):
    return lax.ppermute(block, "z", [(i, (i + step) % DEPTH) for i in range(DEPTH)])


def per_device(tokens, dec_bias, enc_weight, enc_bias):
    own_tokens, width = tokens.shape
    rows, slab = enc_weight.shape
    half = slab // 2
    cols = half // CHIPS
    total = own_tokens * CHIPS * CORES
    core = lax.axis_index("c")
    chip = lax.axis_index("y") * 2 + lax.axis_index("xh")
    depth = lax.axis_index("z")

    centered = (tokens.astype(jnp.float32) - dec_bias).astype(jnp.bfloat16)
    by_core = centered.reshape(own_tokens, CHIPS, CORES, rows).transpose(2, 0, 1, 3)
    by_core = by_core.reshape(CORES, own_tokens, CHIPS * rows)
    keep = jnp.where(core == 0, by_core[0], by_core[1])
    give = jnp.where(core == 0, by_core[1], by_core[0])
    got = lax.ppermute(give, "c", SWAP)
    pair = jnp.where(core == 0, jnp.stack([keep, got]), jnp.stack([got, keep]))
    pair = pair.reshape(CORES * own_tokens, CHIPS * rows)
    batch = spread(pair, PLANE, CHIPS).reshape(total, CHIPS * rows)

    grouped = enc_weight.reshape(rows, 2, CHIPS, cols)
    acts = []
    for h in range(2):
        weight = exchange(grouped[:, h].transpose(1, 0, 2), PLANE)
        part = jnp.dot(batch, weight.reshape(CHIPS * rows, cols), preferred_element_type=jnp.float32)
        other = lax.ppermute(part, "c", SWAP)
        bias = lax.dynamic_slice_in_dim(enc_bias, h * half + chip * cols, cols)
        acts.append(jnp.maximum(part + other + bias, 0.0).astype(jnp.bfloat16))
    activity = jnp.concatenate(acts, axis=1)

    share = cols // CORES
    piece = share // (XLO * DEPTH)
    mine = jnp.where(core == 0, acts[0][:, :share], acts[0][:, share:]).T
    mine = mine.reshape(DEPTH, XLO, piece, total).transpose(1, 0, 2, 3)
    mine = mine.reshape(XLO * DEPTH, piece, total)
    held = exchange(mine, LATENT)[0]
    block = spread(held, ("y", "xh", "xl"), CHIPS * XLO)
    block = block.reshape(CHIPS, XLO * piece, total)

    strip = XLO * piece

    def gram(blocks):
        n = blocks.shape[0]
        out = lax.dot_general(
            blocks.reshape(-1, total), activity, (((1,), (0,)), ((), ())),
            preferred_element_type=jnp.float32,
        )
        out = (out / total).astype(jnp.bfloat16)
        return out.reshape(n, CHIPS, strip, 2 * cols)

    def send(blocks):
        n = len(blocks)
        out = gram(jnp.stack(blocks)).transpose(1, 0, 2, 3)
        out = exchange(out, PLANE)
        out = out.reshape(CHIPS, n, strip, 2, cols).transpose(1, 2, 3, 0, 4)
        return out.reshape(n, strip, slab)

    result = jnp.zeros((share, slab), jnp.bfloat16)

    def place(result, strips, offsets):
        for i, off in enumerate(offsets):
            start = lax.rem(depth + off + DEPTH, DEPTH) * strip
            result = lax.dynamic_update_slice_in_dim(result, strips[i], start, axis=0)
        return result

    up = down = block
    result = place(result, send([block]), [0])
    for step in range(1, DEPTH // 2):
        up, down = ring(up, 1), ring(down, -1)
        result = place(result, send([up, down]), [-step, step])
    cut = CHIPS // 2
    last = jnp.concatenate([ring(up[:cut], 1), ring(down[cut:], -1)])
    return place(result, send([last]), [DEPTH // 2])


def solution(mesh):
    fine = Mesh(mesh.devices.reshape(SIZES), AXES)
    return jax.shard_map(
        per_device,
        mesh=fine,
        in_specs=(P(TOK, None), P(), P(TOK, LATENT), P(LATENT)),
        out_specs=P(TOK, LATENT),
        check_vma=False,
    )
```

time: 564 us -> 287 us (0.51)
  waiting for transfers between devices: 362 us -> 131 us
  local copies, waits for them, and re-layouts: 100 us -> 41.9 us
  starting transfers between devices: 6.4 us -> 55.2 us
  blocking collectives: 57.8 us -> 24.8 us
  between operations: 13.2 us -> 0.52 us
    psum x1 -> x0, waiting for transfers between devices: 198 us -> none  [spread_2(): return lax.psum(jnp.where(mine, shard, jnp.zeros_like(shard)), axis)]
    all_gather x2 -> x0, waiting for transfers between devices: 115 us -> none  [the longest x1 80.1 us: per_device(): columns = lax.all_gather(leading, 'tok', axis=1, tiled=True)]
    all_to_all x1 -> x9, waiting for transfers between devices: 48.1 us -> 114 us  [exchange(): return lax.all_to_all(block, axes, split_axis=0, concat_axis=0, tiled=True)]
    reshape x3 -> x11, local copies, waits for them, and re-layouts: 58.4 us -> 8 us  [the longest x5 3.9 us: send(): out = out.reshape(CHIPS, n, strip, 2, cols).transpose(1, 2, 3, 0, 4)]
    all_to_all x1 -> x9, starting transfers between devices: 6.31 us -> 44.3 us  [exchange(): return lax.all_to_all(block, axes, split_axis=0, concat_axis=0, tiled=True)]
    all_to_all x1, blocking collectives: 57.8 us -> 24.8 us  [exchange(): return lax.all_to_all(block, axes, split_axis=0, concat_axis=0, tiled=True)]
    transpose x2 -> x5, local copies, waits for them, and re-layouts: 34.5 us -> 4.79 us  [the longest x3 3.91 us: per_device(): weight = exchange(grouped[:, h].transpose(1, 0, 2), PLANE)]
    ppermute x0 -> x11, waiting for transfers between devices: none -> 16.5 us  [the longest x8 15.3 us: ring(): lax.ppermute(block, 'z', [(i, (i + step) % DEPTH) for i in range(DEPTH)])]
  transfers between devices with their start and end apart: 4 -> 20, of which waited for: 4 -> 12; matrix products, arithmetic and copies ran while one was open for 3% -> 19% of each run, Pallas kernels for 0% -> 0%
where the time goes in v1:
time: 287 us; the launch traced here: 286 us
  waiting for transfers between devices  131 us (46%)
  starting transfers between devices  55.2 us (19%)
  local copies, waits for them, and re-layouts  41.9 us (15%)
  blocking collectives  24.8 us (9%)
  matrix products  21.8 us (8%)
  other arithmetic  10.6 us (4%)
    all_to_all x9, waiting for transfers between devices, exchange(): return lax.all_to_all(block, axes, split_axis=0, concat_axis=0, tiled=True)  114 us
    all_to_all x9, starting transfers between devices, exchange(): return lax.all_to_all(block, axes, split_axis=0, concat_axis=0, tiled=True)  44.3 us
    all_to_all x1, blocking collectives, exchange(): return lax.all_to_all(block, axes, split_axis=0, concat_axis=0, tiled=True)  24.8 us
    ppermute x8, waiting for transfers between devices, ring(): lax.ppermute(block, 'z', [(i, (i + step) % DEPTH) for i in range(DEPTH)])  15.3 us
    dot_general x5, matrix products, gram(): lax.dot_general(blocks.reshape(-1, total), activity, (((1,), (0,)), ((),...  11.1 us
    dot_general x2, matrix products, per_device(): jnp.dot(batch, weight.reshape(CHIPS * rows, cols), preferred_element_type...  10.7 us
    ppermute x8, starting transfers between devices, ring(): lax.ppermute(block, 'z', [(i, (i + step) % DEPTH) for i in range(DEPTH)])  10.6 us
    slice x9, local copies, waits for them, and re-layouts, place(): result = lax.dynamic_update_slice_in_dim(result, strips[i], start, axis=0)  8.73 us
  transfers between devices with their start and end apart: 20, of which 12 were waited for; matrix products, arithmetic and copies ran while one was open for 19% of the time, Pallas kernels for 0%

profile of v1, /device:TPU:2, one launch (start us, length us, event | category | flops | bytes accessed | tf_op | source)
XLA Modules:
  0.0 285.6 jit_solution(17557387341180120938)
XLA Ops:
  0.0 3.6 %copy.43 = bf16[28,8,16,512]{3,2,1,0:T(8,128)(2,1)S(1)} copy(bf16[28,8,16,512]{3,1,2,0:T(8,128)(2,1)} %bitcast.105) | data formatting | bytes 7340032
  5.7 6.2 %all-to-all-start.1 = ((bf16[8,224,512]{2,1,0:T(8,128)(2,1)}), bf16[8,224,512]{2,1,0:T(8,128)(2,1)}, u32[]{:S(2)}, u32[]{:S(2)}) async-start(bf16[8,224,512]{2,1,0:T(8,128)(2,1)} %copy.27), calls=%async_computation.1 | async-start | bytes 3670016 | tf_op jit(solution)/shard_map/all_to_all | solution.py:16
  14.8 22.8 %all-to-all-done.1 = bf16[8,224,512]{2,1,0:T(8,128)(2,1)} async-done(((bf16[8,224,512]{2,1,0:T(8,128)(2,1)}), bf16[8,224,512]{2,1,0:T(8,128)(2,1)}, u32[]{:S(2)}, u32[]{:S(2)}) %all-to-all-start.1) | async-done | bytes 1835040 | tf_op jit(solution)/shard_map/all_to_all | solution.py:16
  39.7 4.5 %all-to-all-start = ((bf16[8,128,1792]{2,1,0:T(8,128)(2,1)}), bf16[8,128,1792]{2,1,0:T(8,128)(2,1)}, u32[]{:S(2)}, u32[]{:S(2)}) async-start(bf16[8,128,1792]{2,1,0:T(8,128)(2,1)} %broadcast_in_dim.9), calls=%async_computation | async-start | bytes 7340032 | tf_op jit(solution)/shard_map/all_to_all | solution.py:16
  46.1 42.6 %all-to-all-done = bf16[8,128,1792]{2,1,0:T(8,128)(2,1)} async-done(((bf16[8,128,1792]{2,1,0:T(8,128)(2,1)}), bf16[8,128,1792]{2,1,0:T(8,128)(2,1)}, u32[]{:S(2)}, u32[]{:S(2)}) %all-to-all-start) | async-done | bytes 3670048 | tf_op jit(solution)/shard_map/all_to_all | solution.py:16
  88.6 3.6 %all-to-all-start.4 = ((bf16[8,224,512]{2,1,0:T(8,128)(2,1)}), bf16[8,224,512]{2,1,0:T(8,128)(2,1)S(1)}, u32[]{:S(2)}, u32[]{:S(2)}) async-start(bf16[8,224,512]{2,1,0:T(8,128)(2,1)} %copy.29), calls=%async_computation.4 | async-start | bytes 3670016 | tf_op jit(solution)/shard_map/all_to_all | solution.py:16
  92.2 6.0 %fusion.6 = f32[1024,512]{0,1:T(8,128)} fusion(bf16[1024,1792]{1,0:T(8,128)(2,1)} %bitcast.3, bf16[1792,512]{1,0:T(8,128)(2,1)} %bitcast.6), kind=kOutput, calls=%fused_computation.38 | convolution fusion | flops 1879048192 | bytes 7602176 | tf_op jit(solution)/shard_map/dot_general | solution.py:52
  98.3 18.9 %all-to-all-done.4 = bf16[8,224,512]{2,1,0:T(8,128)(2,1)S(1)} async-done(((bf16[8,224,512]{2,1,0:T(8,128)(2,1)}), bf16[8,224,512]{2,1,0:T(8,128)(2,1)S(1)}, u32[]{:S(2)}, u32[]{:S(2)}) %all-to-all-start.4) | async-done | bytes 1835040 | tf_op jit(solution)/shard_map/all_to_all | solution.py:16
  118.4 4.7 %fusion.7 = f32[1024,512]{0,1:T(8,128)S(1)} fusion(bf16[1024,1792]{1,0:T(8,128)(2,1)} %bitcast.3, bf16[1792,512]{1,0:T(8,128)(2,1)} %bitcast.111), kind=kOutput, calls=%fused_computation.39 | convolution fusion | flops 1879048192 | bytes 7602176 | tf_op jit(solution)/shard_map/dot_general | solution.py:52
  126.6 24.8 %all_to_all.50 = bf16[16,16,1024]{2,1,0:T(8,128)(2,1)S(1)} all-to-all(bf16[16,16,1024]{2,1,0:T(8,128)(2,1)S(1)} %bitcast.108), channel_id=1, replica_groups=mesh['y'=4,'xh'=2,'c'=2,'xl'=2,'z'=8] {'xl','z'}, dimensions={0} | all-to-all | bytes 1048576 | tf_op jit(solution)/shard_map/all_to_all | solution.py:16
  152.3 5.3 %all-to-all-start.3 = ((bf16[16,16,1024]{2,1,0:T(8,128)(2,1)}), bf16[16,16,1024]{2,1,0:T(8,128)(2,1)}, u32[]{:S(2)}, u32[]{:S(2)}) async-start(bf16[16,16,1024]{2,1,0:T(8,128)(2,1)} %broadcast_in_dim.21), calls=%async_computation.3 | async-start | bytes 1048576 | tf_op jit(solution)/shard_map/all_to_all | solution.py:16
  160.4 6.5 %all-to-all-done.3 = bf16[16,16,1024]{2,1,0:T(8,128)(2,1)} async-done(((bf16[16,16,1024]{2,1,0:T(8,128)(2,1)}), bf16[16,16,1024]{2,1,0:T(8,128)(2,1)}, u32[]{:S(2)}, u32[]{:S(2)}) %all-to-all-start.3) | async-done | bytes 524320 | tf_op jit(solution)/shard_map/all_to_all | solution.py:16
  173.1 3.5 %all-to-all-start.5 = ((bf16[8,1,32,1024]{3,2,1,0:T(8,128)(2,1)}), bf16[8,1,32,1024]{3,2,1,0:T(8,128)(2,1)S(1)}, u32[]{:S(2)}, u32[]{:S(2)}) async-start(bf16[8,1,32,1024]{3,2,1,0:T(8,128)(2,1)} %bitcast.17), calls=%async_computation.5 | async-start | bytes 1048576 | tf_op jit(solution)/shard_map/all_to_all | solution.py:16
  176.7 10.2 %all-to-all-done.5 = bf16[8,1,32,1024]{3,2,1,0:T(8,128)(2,1)S(1)} async-done(((bf16[8,1,32,1024]{3,2,1,0:T(8,128)(2,1)}), bf16[8,1,32,1024]{3,2,1,0:T(8,128)(2,1)S(1)}, u32[]{:S(2)}, u32[]{:S(2)}) %all-to-all-start.5) | async-done | bytes 524320 | tf_op jit(solution)/shard_map/all_to_all | solution.py:16
  192.9 3.6 %all-to-all-start.6 = ((bf16[8,2,32,1024]{3,2,1,0:T(8,128)(2,1)}), bf16[8,2,32,1024]{3,2,1,0:T(8,128)(2,1)S(1)}, u32[]{:S(2)}, u32[]{:S(2)}) async-start(bf16[8,2,32,1024]{3,2,1,0:T(8,128)(2,1)} %bitcast.99), calls=%async_computation.6 | async-start | bytes 2097152 | tf_op jit(solution)/shard_map/all_to_all | solution.py:16
  196.4 3.2 %collective-permute-start.6 = (bf16[8,32,1024]{2,1,0:T(8,128)(2,1)S(1)}, bf16[8,32,1024]{2,1,0:T(8,128)(2,1)}, u32[]{:S(2)}, u32[]{:S(2)}) collective-permute-start(bf16[8,32,1024]{2,1,0:T(8,128)(2,1)S(1)} %copy-done.5), channel_id=1, source_target_pairs={{0,7},{1,0},{2,1},{3,2},{4,3},{5,4},{6,5},{7,6},{8,15},{9,8},{10,9... | collective-permute-start | bytes 1572872 | tf_op jit(solution)/shard_map/ppermute | solution.py:25
  200.2 7.8 %collective-permute-done.6 = bf16[8,32,1024]{2,1,0:T(8,128)(2,1)} collective-permute-done((bf16[8,32,1024]{2,1,0:T(8,128)(2,1)S(1)}, bf16[8,32,1024]{2,1,0:T(8,128)(2,1)}, u32[]{:S(2)}, u32[]{:S(2)}) %collective-permute-start.6) | collective-permute-done | bytes 524320 | tf_op jit(solution)/shard_map/ppermute | solution.py:25
  208.0 3.7 %collective-permute-done.5 = bf16[8,32,1024]{2,1,0:T(8,128)(2,1)} collective-permute-done((bf16[8,32,1024]{2,1,0:T(8,128)(2,1)}, bf16[8,32,1024]{2,1,0:T(8,128)(2,1)}, u32[]{:S(2)}, u32[]{:S(2)}) %collective-permute-start.5) | collective-permute-done | bytes 524320 | tf_op jit(solution)/shard_map/ppermute | solution.py:25
  217.4 6.8 %all-to-all-start.7 = ((bf16[8,2,32,1024]{3,2,1,0:T(8,128)(2,1)}), bf16[8,2,32,1024]{3,2,1,0:T(8,128)(2,1)S(1)}, u32[]{:S(2)}, u32[]{:S(2)}) async-start(bf16[8,2,32,1024]{3,2,1,0:T(8,128)(2,1)} %bitcast.98), calls=%async_computation.7 | async-start | bytes 2097152 | tf_op jit(solution)/shard_map/all_to_all | solution.py:16
  241.1 3.6 %collective-permute-done.9 = bf16[4,32,1024]{2,1,0:T(8,128)(2,1)S(1)} collective-permute-done((bf16[4,32,1024]{2,1,0:T(8,128)(2,1)S(1)}, bf16[4,32,1024]{2,1,0:T(8,128)(2,1)S(1)}, u32[]{:S(2)}, u32[]{:S(2)}) %collective-permute-start.9) | collective-permute-done | bytes 262176 | tf_op jit(solution)/shard_map/ppermute | solution.py:25
  246.2 7.2 %all-to-all-start.9 = ((bf16[8,1,32,1024]{3,2,1,0:T(8,128)(2,1)}), bf16[8,1,32,1024]{3,2,1,0:T(8,128)(2,1)S(1)}, u32[]{:S(2)}, u32[]{:S(2)}) async-start(bf16[8,1,32,1024]{3,2,1,0:T(8,128)(2,1)} %bitcast.40), calls=%async_computation.9 | async-start | bytes 1048576 | tf_op jit(solution)/shard_map/all_to_all | solution.py:16
  259.6 4.1 %all-to-all-done.9 = bf16[8,1,32,1024]{3,2,1,0:T(8,128)(2,1)S(1)} async-done(((bf16[8,1,32,1024]{3,2,1,0:T(8,128)(2,1)}), bf16[8,1,32,1024]{3,2,1,0:T(8,128)(2,1)S(1)}, u32[]{:S(2)}, u32[]{:S(2)}) %all-to-all-start.9) | async-done | bytes 524320 | tf_op jit(solution)/shard_map/all_to_all | solution.py:16
  263.7 3.8 %all-to-all-start.8 = ((bf16[8,2,32,1024]{3,2,1,0:T(8,128)(2,1)}), bf16[8,2,32,1024]{3,2,1,0:T(8,128)(2,1)S(1)}, u32[]{:S(2)}, u32[]{:S(2)}) async-start(bf16[8,2,32,1024]{3,2,1,0:T(8,128)(2,1)} %bitcast.97), calls=%async_computation.8 | async-start | bytes 2097152 | tf_op jit(solution)/shard_map/all_to_all | solution.py:16
  270.9 9.2 %all-to-all-done.8 = bf16[8,2,32,1024]{3,2,1,0:T(8,128)(2,1)S(1)} async-done(((bf16[8,2,32,1024]{3,2,1,0:T(8,128)(2,1)}), bf16[8,2,32,1024]{3,2,1,0:T(8,128)(2,1)S(1)}, u32[]{:S(2)}, u32[]{:S(2)}) %all-to-all-start.8) | async-done | bytes 1048608 | tf_op jit(solution)/shard_map/all_to_all | solution.py:16
  (101 shorter events, 69.0 us)
Async XLA Ops:
  5.7 6.2 %copy-start.7 = (f32[3584]{0:T(1024)S(1)}, f32[3584]{0:T(1024)}, u32[]{:S(2)}) copy-start(f32[3584]{0:T(1024)} %param.5) | copy-start | bytes 43012
  5.7 31.9 %all-to-all-start.1 = ((bf16[8,224,512]{2,1,0:T(8,128)(2,1)}), bf16[8,224,512]{2,1,0:T(8,128)(2,1)}, u32[]{:S(2)}, u32[]{:S(2)}) async-start(bf16[8,224,512]{2,1,0:T(8,128)(2,1)} %copy.27), calls=%async_computation.1 | async-start | bytes 3670016 | tf_op jit(solution)/shard_map/all_to_all | solution.py:16
  13.2 1.6 collective-permute-start
  39.7 48.9 %all-to-all-start = ((bf16[8,128,1792]{2,1,0:T(8,128)(2,1)}), bf16[8,128,1792]{2,1,0:T(8,128)(2,1)}, u32[]{:S(2)}, u32[]{:S(2)}) async-start(bf16[8,128,1792]{2,1,0:T(8,128)(2,1)} %broadcast_in_dim.9), calls=%async_computation | async-start | bytes 7340032 | tf_op jit(solution)/shard_map/all_to_all | solution.py:16
  88.6 28.5 %all-to-all-start.4 = ((bf16[8,224,512]{2,1,0:T(8,128)(2,1)}), bf16[8,224,512]{2,1,0:T(8,128)(2,1)S(1)}, u32[]{:S(2)}, u32[]{:S(2)}) async-start(bf16[8,224,512]{2,1,0:T(8,128)(2,1)} %copy.29), calls=%async_computation.4 | async-start | bytes 3670016 | tf_op jit(solution)/shard_map/all_to_all | solution.py:16
  98.3 25.7 %collective-permute-start.1 = (f32[1024,512]{0,1:T(8,128)}, f32[1024,512]{0,1:T(8,128)}, u32[]{:S(2)}, u32[]{:S(2)}) collective-permute-start(f32[1024,512]{0,1:T(8,128)} %fusion.6), channel_id=1, source_target_pairs={{0,16},{16,0},{1,17},{17,1},{2,18},{18,2},{3,19},{19,3},{4,20},{20... | collective-permute-start | bytes 6291464 | tf_op jit(solution)/shard_map/ppermute | solution.py:53
  123.1 34.4 %collective-permute-start.2 = (f32[1024,512]{0,1:T(8,128)S(1)}, f32[1024,512]{0,1:T(8,128)}, u32[]{:S(2)}, u32[]{:S(2)}) collective-permute-start(f32[1024,512]{0,1:T(8,128)S(1)} %fusion.7), channel_id=1, source_target_pairs={{0,16},{16,0},{1,17},{17,1},{2,18},{18,2},{3,19},{19,3},{4,20},{20... | collective-permute-start | bytes 6291464 | tf_op jit(solution)/shard_map/ppermute | solution.py:53
  152.3 14.7 %all-to-all-start.3 = ((bf16[16,16,1024]{2,1,0:T(8,128)(2,1)}), bf16[16,16,1024]{2,1,0:T(8,128)(2,1)}, u32[]{:S(2)}, u32[]{:S(2)}) async-start(bf16[16,16,1024]{2,1,0:T(8,128)(2,1)} %broadcast_in_dim.21), calls=%async_computation.3 | async-start | bytes 1048576 | tf_op jit(solution)/shard_map/all_to_all | solution.py:16
  167.0 20.9 %collective-permute-start.4 = (bf16[8,32,1024]{2,1,0:T(8,128)(2,1)}, bf16[8,32,1024]{2,1,0:T(8,128)(2,1)S(1)}, u32[]{:S(2)}, u32[]{:S(2)}) collective-permute-start(bf16[8,32,1024]{2,1,0:T(8,128)(2,1)} %bitcast.19), channel_id=1, source_target_pairs={{0,7},{1,0},{2,1},{3,2},{4,3},{5,4},{6,5},{7,6},{8,15},{9,8},{10,9... | collective-permute-start | bytes 1572872 | tf_op jit(solution)/shard_map/ppermute | solution.py:25
  170.2 17.7 %collective-permute-start.3 = (bf16[8,32,1024]{2,1,0:T(8,128)(2,1)}, bf16[8,32,1024]{2,1,0:T(8,128)(2,1)}, u32[]{:S(2)}, u32[]{:S(2)}) collective-permute-start(bf16[8,32,1024]{2,1,0:T(8,128)(2,1)} %bitcast.19), channel_id=1, source_target_pairs={{0,1},{1,2},{2,3},{3,4},{4,5},{5,6},{6,7},{7,0},{8,9},{9,10},{10,1... | collective-permute-start | bytes 1572872 | tf_op jit(solution)/shard_map/ppermute | solution.py:25
  173.1 13.7 %all-to-all-start.5 = ((bf16[8,1,32,1024]{3,2,1,0:T(8,128)(2,1)}), bf16[8,1,32,1024]{3,2,1,0:T(8,128)(2,1)S(1)}, u32[]{:S(2)}, u32[]{:S(2)}) async-start(bf16[8,1,32,1024]{3,2,1,0:T(8,128)(2,1)} %bitcast.17), calls=%async_computation.5 | async-start | bytes 1048576 | tf_op jit(solution)/shard_map/all_to_all | solution.py:16
  192.9 24.6 %all-to-all-start.6 = ((bf16[8,2,32,1024]{3,2,1,0:T(8,128)(2,1)}), bf16[8,2,32,1024]{3,2,1,0:T(8,128)(2,1)S(1)}, u32[]{:S(2)}, u32[]{:S(2)}) async-start(bf16[8,2,32,1024]{3,2,1,0:T(8,128)(2,1)} %bitcast.99), calls=%async_computation.6 | async-start | bytes 2097152 | tf_op jit(solution)/shard_map/all_to_all | solution.py:16
  196.4 11.6 %collective-permute-start.6 = (bf16[8,32,1024]{2,1,0:T(8,128)(2,1)S(1)}, bf16[8,32,1024]{2,1,0:T(8,128)(2,1)}, u32[]{:S(2)}, u32[]{:S(2)}) collective-permute-start(bf16[8,32,1024]{2,1,0:T(8,128)(2,1)S(1)} %copy-done.5), channel_id=1, source_target_pairs={{0,7},{1,0},{2,1},{3,2},{4,3},{5,4},{6,5},{7,6},{8,15},{9,8},{10,9... | collective-permute-start | bytes 1572872 | tf_op jit(solution)/shard_map/ppermute | solution.py:25
  199.7 12.1 %collective-permute-start.5 = (bf16[8,32,1024]{2,1,0:T(8,128)(2,1)}, bf16[8,32,1024]{2,1,0:T(8,128)(2,1)}, u32[]{:S(2)}, u32[]{:S(2)}) collective-permute-start(bf16[8,32,1024]{2,1,0:T(8,128)(2,1)} %collective-permute-done.3), channel_id=1, source_target_pairs={{0,1},{1,2},{2,3},{3,4},{4,5},{5,6},{6,7},{7,0},{8,9},{9,10},{10,1... | collective-permute-start | bytes 1572872 | tf_op jit(solution)/shard_map/ppermute | solution.py:25
  200.1 12.9 %copy-start.2 = (bf16[1024,512]{0,1:T(8,128)(2,1)S(1)}, bf16[1024,512]{0,1:T(8,128)(2,1)}, u32[]{:S(2)}) copy-start(bf16[1024,512]{0,1:T(8,128)(2,1)} %maximum_convert_fusion) | copy-start | bytes 3145732
  200.2 14.2 %copy-start = (bf16[256,8192]{1,0:T(8,128)(2,1)}, bf16[256,8192]{1,0:T(8,128)(2,1)S(1)}, u32[]{:S(2)}) copy-start(bf16[256,8192]{1,0:T(8,128)(2,1)S(1)} %constant_dynamic-update-slice_fusion.7) | copy-start | bytes 12582916
  215.4 18.2 %collective-permute-start.8 = (bf16[8,32,1024]{2,1,0:T(8,128)(2,1)}, bf16[8,32,1024]{2,1,0:T(8,128)(2,1)}, u32[]{:S(2)}, u32[]{:S(2)}) collective-permute-start(bf16[8,32,1024]{2,1,0:T(8,128)(2,1)} %collective-permute-done.6), channel_id=1, source_target_pairs={{0,7},{1,0},{2,1},{3,2},{4,3},{5,4},{6,5},{7,6},{8,15},{9,8},{10,9... | collective-permute-start | bytes 1572872 | tf_op jit(solution)/shard_map/ppermute | solution.py:25
  215.5 20.5 %collective-permute-start.7 = (bf16[8,32,1024]{2,1,0:T(8,128)(2,1)}, bf16[8,32,1024]{2,1,0:T(8,128)(2,1)}, u32[]{:S(2)}, u32[]{:S(2)}) collective-permute-start(bf16[8,32,1024]{2,1,0:T(8,128)(2,1)} %collective-permute-done.5), channel_id=1, source_target_pairs={{0,1},{1,2},{2,3},{3,4},{4,5},{5,6},{6,7},{7,0},{8,9},{9,10},{10,1... | collective-permute-start | bytes 1572872 | tf_op jit(solution)/shard_map/ppermute | solution.py:25
  217.4 28.8 %all-to-all-start.7 = ((bf16[8,2,32,1024]{3,2,1,0:T(8,128)(2,1)}), bf16[8,2,32,1024]{3,2,1,0:T(8,128)(2,1)S(1)}, u32[]{:S(2)}, u32[]{:S(2)}) async-start(bf16[8,2,32,1024]{3,2,1,0:T(8,128)(2,1)} %bitcast.98), calls=%async_computation.7 | async-start | bytes 2097152 | tf_op jit(solution)/shard_map/all_to_all | solution.py:16
  234.6 6.5 %collective-permute-start.10 = (bf16[4,32,1024]{2,1,0:T(8,128)(2,1)S(1)}, bf16[4,32,1024]{2,1,0:T(8,128)(2,1)S(1)}, u32[]{:S(2)}, u32[]{:S(2)}) collective-permute-start(bf16[4,32,1024]{2,1,0:T(8,128)(2,1)S(1)} %slice.84), channel_id=1, source_target_pairs={{0,7},{1,0},{2,1},{3,2},{4,3},{5,4},{6,5},{7,6},{8,15},{9,8},{10,9... | collective-permute-start | bytes 786440 | tf_op jit(solution)/shard_map/ppermute | solution.py:25
  237.0 7.7 %copy-start.3 = (bf16[1024,512]{0,1:T(8,128)(2,1)S(1)}, bf16[1024,512]{0,1:T(8,128)(2,1)}, u32[]{:S(2)}) copy-start(bf16[1024,512]{0,1:T(8,128)(2,1)} %maximum_convert_fusion) | copy-start | bytes 3145732
  237.0 7.7 %collective-permute-start.9 = (bf16[4,32,1024]{2,1,0:T(8,128)(2,1)S(1)}, bf16[4,32,1024]{2,1,0:T(8,128)(2,1)S(1)}, u32[]{:S(2)}, u32[]{:S(2)}) collective-permute-start(bf16[4,32,1024]{2,1,0:T(8,128)(2,1)S(1)} %slice.83), channel_id=1, source_target_pairs={{0,1},{1,2},{2,3},{3,4},{4,5},{5,6},{6,7},{7,0},{8,9},{9,10},{10,1... | collective-permute-start | bytes 786440 | tf_op jit(solution)/shard_map/ppermute | solution.py:25
  246.2 17.4 %all-to-all-start.9 = ((bf16[8,1,32,1024]{3,2,1,0:T(8,128)(2,1)}), bf16[8,1,32,1024]{3,2,1,0:T(8,128)(2,1)S(1)}, u32[]{:S(2)}, u32[]{:S(2)}) async-start(bf16[8,1,32,1024]{3,2,1,0:T(8,128)(2,1)} %bitcast.40), calls=%async_computation.9 | async-start | bytes 1048576 | tf_op jit(solution)/shard_map/all_to_all | solution.py:16
  263.7 16.5 %all-to-all-start.8 = ((bf16[8,2,32,1024]{3,2,1,0:T(8,128)(2,1)}), bf16[8,2,32,1024]{3,2,1,0:T(8,128)(2,1)S(1)}, u32[]{:S(2)}, u32[]{:S(2)}) async-start(bf16[8,2,32,1024]{3,2,1,0:T(8,128)(2,1)} %bitcast.97), calls=%async_computation.8 | async-start | bytes 2097152 | tf_op jit(solution)/shard_map/all_to_all | solution.py:16
  (4 other events, 15.9 us)

commit v2 on v0

v2 whole, which is shorter than its diff:
```python
import jax
import jax.numpy as jnp
from jax import lax
from jax.experimental import pallas as pl
from jax.experimental.pallas import tpu as pltpu
from jax.sharding import Mesh, PartitionSpec as P

AXES = ("y", "xh", "c", "xl", "z")
SIZES = (4, 2, 2, 2, 8)
PLANE = ("y", "xh", "xl")
TOK = ("y", "xh", "c")
LATENT = ("xl", "z")
CHIPS, CORES, XLO, DEPTH = 8, 2, 2, 8
SWAP = [(0, 1), (1, 0)]
UP = [(i, (i + 1) % DEPTH) for i in range(DEPTH)]
DOWN = [(i, (i - 1) % DEPTH) for i in range(DEPTH)]


def exchange(block):
    return lax.all_to_all(block, PLANE, split_axis=0, concat_axis=0, tiled=True)


def spread(block):
    return exchange(jnp.broadcast_to(block[None], (CHIPS * XLO,) + block.shape))


def other_half(block):
    cut = block.shape[0] // 2
    return lax.ppermute(block[:cut], "z", UP), lax.ppermute(block[cut:], "z", DOWN)


def place(received, parity, strip, slab, base=None):
    lane = slab // (2 * CHIPS * CORES * XLO)

    def body(par_ref, in_ref, *rest):
        out_ref = rest[-1]
        for xl in range(XLO):
            for c in range(CORES):
                at = (c * XLO + xl) * lane
                out_ref[:, 0, :, at : at + lane] = in_ref[0, xl, :, :, c * lane : (c + 1) * lane]

    width = CORES * XLO * lane
    data = received.reshape(CHIPS, XLO, XLO, strip, 2 * CORES * lane)
    in_specs = [
        pl.BlockSpec((1, XLO, XLO, strip, CORES * lane), lambda h, t, par: (t, 0, 0, 0, h))
    ]
    args = [parity, data]
    if base is not None:
        in_specs.append(pl.BlockSpec(memory_space=pl.ANY))
        args.append(base)
    return pl.pallas_call(
        body,
        out_shape=jax.ShapeDtypeStruct((XLO, 2, strip, slab), jnp.bfloat16),
        grid_spec=pltpu.PrefetchScalarGridSpec(
            num_scalar_prefetch=1,
            grid=(2, CHIPS),
            in_specs=in_specs,
            out_specs=pl.BlockSpec(
                (XLO, 1, strip, width), lambda h, t, par: (0, par[0], 0, h * CHIPS + t)
            ),
        ),
        input_output_aliases={} if base is None else {2: 0},
        cost_estimate=pl.CostEstimate(
            flops=0, bytes_accessed=2 * 2 * XLO * strip * slab, transcendentals=0
        ),
    )(*args)


def per_device(tokens, dec_bias, enc_weight, enc_bias):
    own, width = tokens.shape
    rows, slab = enc_weight.shape
    lane = slab // (2 * CHIPS * CORES * XLO)
    total = own * CHIPS * CORES
    core = lax.axis_index("c")
    xlo = lax.axis_index("xl")
    chip = lax.axis_index("y") * 2 + lax.axis_index("xh")
    z = lax.axis_index("z")
    odd = lax.rem(z, 2)

    centered = (tokens.astype(jnp.float32) - dec_bias).astype(jnp.bfloat16)
    halves = centered.reshape(own, CHIPS, CORES, rows).transpose(2, 0, 1, 3)
    halves = halves.reshape(CORES, own, CHIPS * rows)
    keep = jnp.where(core == 0, halves[0], halves[1])
    give = jnp.where(core == 0, halves[1], halves[0])
    got = lax.ppermute(give, "c", SWAP)
    mine = jnp.where(core == xlo, keep, got)
    part = own // 2
    mine = jnp.where(odd == 0, mine[:part], mine[part:])
    near = spread(mine).reshape(total // 2, CHIPS * rows)
    far = jnp.concatenate(other_half(near))
    batch = jnp.where(odd == 0, jnp.concatenate([near, far]), jnp.concatenate([far, near]))

    biases = enc_bias.reshape(2, CHIPS, CORES, XLO, lane)
    biases = lax.dynamic_index_in_dim(biases, chip, 1, keepdims=False)
    bias_keep = lax.dynamic_index_in_dim(biases, xlo, 2, keepdims=False)
    bias_give = lax.dynamic_index_in_dim(biases, 1 - xlo, 2, keepdims=False)
    bias_got = lax.ppermute(bias_give, "xl", SWAP)
    bias = jnp.where(xlo == 0, jnp.stack([bias_keep, bias_got]), jnp.stack([bias_got, bias_keep]))

    grouped = enc_weight.reshape(rows, 2, CHIPS, CORES, XLO, lane).transpose(1, 2, 4, 0, 3, 5)
    grouped = grouped.reshape(2, CHIPS * XLO, rows, CORES * lane)

    def encode(h):
        weight = exchange(grouped[h]).reshape(CHIPS, XLO, rows, CORES * lane)
        weight = weight.transpose(0, 2, 1, 3).reshape(CHIPS * rows, XLO * CORES * lane)
        pre = jnp.dot(batch, weight, preferred_element_type=jnp.float32)
        other = lax.ppermute(pre, "c", SWAP)
        pre = pre + other + bias[:, h].reshape(XLO * CORES * lane)
        return jnp.maximum(pre, 0.0).astype(jnp.bfloat16)

    first = encode(0)

    panel = jnp.where(core == 0, first[:, :lane], first[:, lane : 2 * lane]).T
    strip = lane // 2
    held = jnp.where(z == 0, panel[:strip], jnp.zeros_like(panel[:strip]))
    for d in range(1, DEPTH):
        piece = panel[(d % 2) * strip : (d % 2 + 1) * strip]
        held = held + lax.ppermute(piece, "z", [(0, d)])

    second = encode(1)
    block = spread(held)
    activity = jnp.concatenate([first, second], axis=1).reshape(total, 2, XLO, CORES * lane)
    activity = activity.transpose(0, 2, 1, 3).reshape(total, XLO * 2 * CORES * lane)

    def gram(rows_of):
        out = lax.dot_general(
            rows_of.reshape(-1, total), activity, (((1,), (0,)), ((), ())),
            preferred_element_type=jnp.float32,
        )
        out = (out / total).astype(jnp.bfloat16)
        out = out.reshape(CHIPS, XLO * strip, XLO, 2 * CORES * lane).transpose(0, 2, 1, 3)
        return exchange(out.reshape(CHIPS * XLO, XLO * strip, 2 * CORES * lane))

    side = jnp.reshape(odd, (1,))
    rest = jnp.concatenate(other_half(block))
    result = place(gram(block), side, strip, slab)
    result = place(gram(rest), 1 - side, strip, slab, result)
    return result.reshape(XLO * 2 * strip, slab)


def solution(mesh):
    fine = Mesh(mesh.devices.reshape(SIZES), AXES)
    return jax.shard_map(
        per_device,
        mesh=fine,
        in_specs=(P(TOK, None), P(), P(TOK, LATENT), P(LATENT)),
        out_specs=P(TOK, LATENT),
        check_vma=False,
    )
```

time: 564 us -> 279 us (0.49)
  waiting for transfers between devices: 362 us -> 95.4 us
  starting transfers between devices: 6.4 us -> 70.9 us
  blocking collectives: 57.8 us -> 0 us
  local copies, waits for them, and re-layouts: 100 us -> 63.9 us
  Pallas kernels: 0 us -> 19.1 us
  between operations: 13.2 us -> 0.34 us
    psum x1 -> x0, waiting for transfers between devices: 198 us -> none  [spread_2(): return lax.psum(jnp.where(mine, shard, jnp.zeros_like(shard)), axis)]
    all_gather x2 -> x0, waiting for transfers between devices: 115 us -> none  [the longest x1 80.1 us: per_device(): columns = lax.all_gather(leading, 'tok', axis=1, tiled=True)]
    all_to_all x1 -> x0, blocking collectives: 57.8 us -> none  [per_device(): lax.all_to_all(blocks, 'tok', split_axis=1, concat_axis=1, tiled=True)]
    ppermute x0 -> x15, waiting for transfers between devices: none -> 39.8 us  [the longest x2 21.6 us: other_half(): lax.ppermute(block[:cut], 'z', UP)]
    all_to_all x1 -> x6, starting transfers between devices: 6.31 us -> 45.3 us  [exchange(): return lax.all_to_all(block, PLANE, split_axis=0, concat_axis=0, tiled=True)]
    transpose x2, local copies, waits for them, and re-layouts: 34.5 us -> 6.71 us  [gram(): out.reshape(CHIPS, XLO * strip, XLO, 2 * CORES * lane).transpose(0, 2, 1, 3)]
    reshape x3 -> x9, local copies, waits for them, and re-layouts: 58.4 us -> 30.6 us  [the longest x2 12.4 us: per_device(): enc_weight.reshape(rows, 2, CHIPS, CORES, XLO, lane)]
    ppermute x0 -> x15, starting transfers between devices: none -> 25.6 us  [the longest x7 16 us: per_device(): held = held + lax.ppermute(piece, 'z', [(0, d)])]
  transfers between devices with their start and end apart: 4 -> 21, of which waited for: 4 -> 12; matrix products, arithmetic and copies ran while one was open for 3% -> 25% of each run, Pallas kernels for 0% -> 4%
where the time goes in v2:
time: 279 us; the launch traced here: 274 us
  waiting for transfers between devices  95.4 us (34%)
  starting transfers between devices  70.9 us (25%)
  local copies, waits for them, and re-layouts  63.9 us (23%)
  Pallas kernels  19.1 us (7%)
  matrix products  15.4 us (6%)
  other arithmetic  8.65 us (3%)
    all_to_all x6, waiting for transfers between devices, exchange(): return lax.all_to_all(block, PLANE, split_axis=0, concat_axis=0, tiled=True)  55.6 us
    all_to_all x6, starting transfers between devices, exchange(): return lax.all_to_all(block, PLANE, split_axis=0, concat_axis=0, tiled=True)  45.3 us
    ppermute x2, waiting for transfers between devices, other_half(): lax.ppermute(block[:cut], 'z', UP)  21.6 us
    pallas_call x2, Pallas kernels, place(): pl.pallas_call(body, out_shape=jax.ShapeDtypeStruct((XLO, 2, strip, slab)...  19.1 us
    ppermute x7, starting transfers between devices, per_device(): held = held + lax.ppermute(piece, 'z', [(0, d)])  16 us
    reshape x2, local copies, waits for them, and re-layouts, per_device(): enc_weight.reshape(rows, 2, CHIPS, CORES, XLO, lane)  12.4 us
    squeeze x2, local copies, waits for them, and re-layouts, encode(): weight = exchange(grouped[h]).reshape(CHIPS, XLO, rows, CORES * lane)  10.5 us
    ppermute x1, waiting for transfers between devices, per_device(): bias_got = lax.ppermute(bias_give, 'xl', SWAP)  10.4 us
  transfers between devices with their start and end apart: 21, of which 12 were waited for; matrix products, arithmetic and copies ran while one was open for 25% of the time, Pallas kernels for 4%

profile of v2, /device:TPU:2, one launch (start us, length us, event | category | flops | bytes accessed | tf_op | source)
XLA Modules:
  0.0 273.6 jit_solution(16146867772871023359)
XLA Ops:
  5.4 7.5 %all-to-all-start = ((bf16[16,32,1792]{2,1,0:T(8,128)(2,1)}), bf16[16,32,1792]{2,1,0:T(8,128)(2,1)S(1)}, u32[]{:S(2)}, u32[]{:S(2)}) async-start(bf16[16,32,1792]{2,1,0:T(8,128)(2,1)} %broadcast_in_dim.6), calls=%async_computation | async-start | bytes 3670016 | tf_op jit(solution)/shard_map/all_to_all | solution.py:20
  12.9 7.1 %reshape.89 = bf16[224,2,8,2,2,128]{5,4,3,2,1,0:T(2,128)(2,1)} reshape(bf16[224,8192]{1,0:T(8,128)(2,1)} %param.6) | data formatting | bytes 7340032 | tf_op jit(solution)/shard_map/reshape | solution.py:100
  19.9 5.4 %copy.19 = bf16[224,2,8,2,2,128]{5,3,0,4,2,1:T(2,128)(2,1)S(1)} copy(bf16[224,2,8,2,2,128]{5,4,3,2,1,0:T(2,128)(2,1)} %reshape.89) | data formatting | bytes 7340032 | tf_op jit(solution)/shard_map/reshape | solution.py:100
  25.3 5.0 %fusion.1 = (bf16[1,8,2,224,2,128]{5,4,3,2,1,0:T(2,128)(2,1)}, bf16[1,8,2,224,2,128]{5,4,3,2,1,0:T(2,128)(2,1)}) fusion(bf16[2,8,2,224,2,128]{5,4,3,2,1,0:T(2,128)(2,1)S(1)} %bitcast.54), kind=kLoop, calls=%fused_computation.20 | loop fusion | bytes 7340032 | tf_op jit(solution)/shard_map/slice | solution.py:104
  30.3 5.3 %squeeze.17 = bf16[16,224,256]{2,1,0:T(8,128)(2,1)} reshape(bf16[1,8,2,224,2,128]{5,4,3,2,1,0:T(2,128)(2,1)} %get-tuple-element.6) | data formatting | bytes 3670016 | tf_op jit(solution)/shard_map/squeeze | solution.py:104
  37.5 8.5 %all-to-all-start.1 = ((bf16[16,224,256]{2,1,0:T(8,128)(2,1)}), bf16[16,224,256]{2,1,0:T(8,128)(2,1)}, u32[]{:S(2)}, u32[]{:S(2)}) async-start(bf16[16,224,256]{2,1,0:T(8,128)(2,1)} %squeeze.17), calls=%async_computation.1 | async-start | bytes 3670016 | tf_op jit(solution)/shard_map/all_to_all | solution.py:20
  48.9 3.9 %collective-permute-start.2 = (bf16[256,1792]{1,0:T(8,128)(2,1)S(1)}, bf16[256,1792]{1,0:T(8,128)(2,1)}, u32[]{:S(2)}, u32[]{:S(2)}) collective-permute-start(bf16[256,1792]{1,0:T(8,128)(2,1)S(1)} %bitcast.70), channel_id=1, source_target_pairs={{0,7},{1,0},{2,1},{3,2},{4,3},{5,4},{6,5},{7,6},{8,15},{9,8},{10,9... | collective-permute-start | bytes 2752520 | tf_op jit(solution)/shard_map/ppermute | solution.py:29
  52.9 5.3 %squeeze.19 = bf16[16,224,256]{2,1,0:T(8,128)(2,1)} reshape(bf16[1,8,2,224,2,128]{5,4,3,2,1,0:T(2,128)(2,1)} %get-tuple-element.5) | data formatting | bytes 3670016 | tf_op jit(solution)/shard_map/squeeze | solution.py:104
  58.1 11.8 %all-to-all-done.1 = bf16[16,224,256]{2,1,0:T(8,128)(2,1)} async-done(((bf16[16,224,256]{2,1,0:T(8,128)(2,1)}), bf16[16,224,256]{2,1,0:T(8,128)(2,1)}, u32[]{:S(2)}, u32[]{:S(2)}) %all-to-all-start.1) | async-done | bytes 1835040 | tf_op jit(solution)/shard_map/all_to_all | solution.py:20
  69.9 7.4 %all-to-all-start.3 = ((bf16[16,224,256]{2,1,0:T(8,128)(2,1)}), bf16[16,224,256]{2,1,0:T(8,128)(2,1)}, u32[]{:S(2)}, u32[]{:S(2)}) async-start(bf16[16,224,256]{2,1,0:T(8,128)(2,1)} %squeeze.19), calls=%async_computation.3 | async-start | bytes 3670016 | tf_op jit(solution)/shard_map/all_to_all | solution.py:20
  87.1 10.4 %collective-permute-done.4 = f32[2,2,128]{2,1,0:T(2,128)S(1)} collective-permute-done((f32[2,2,128]{2,1,0:T(2,128)S(1)}, f32[2,2,128]{2,1,0:T(2,128)S(1)}, u32[]{:S(2)}, u32[]{:S(2)}) %collective-permute-start.4) | collective-permute-done | bytes 2080 | tf_op jit(solution)/shard_map/ppermute | solution.py:97
  111.5 8.2 %collective-permute-start.10 = (bf16[64,1024]{1,0:T(8,128)(2,1)S(1)}, bf16[64,1024]{1,0:T(8,128)(2,1)S(1)}, u32[]{:S(2)}, u32[]{:S(2)}) collective-permute-start(bf16[64,1024]{1,0:T(8,128)(2,1)S(1)} %get-tuple-element.13), channel_id=1, source_target_pairs={{0,6},{8,14},{16,22},{24,30},{32,38},{40,46},{48,54},{56,62},{64,7... | collective-permute-start | bytes 393224 | tf_op jit(solution)/shard_map/ppermute | solution.py:118
  135.8 6.1 %all-to-all-start.2 = ((bf16[16,64,1024]{2,1,0:T(8,128)(2,1)}), bf16[16,64,1024]{2,1,0:T(8,128)(2,1)S(1)}, u32[]{:S(2)}, u32[]{:S(2)}) async-start(bf16[16,64,1024]{2,1,0:T(8,128)(2,1)} %broadcast_in_dim.8), calls=%async_computation.2 | async-start | bytes 4194304 | tf_op jit(solution)/shard_map/all_to_all | solution.py:20
  146.2 23.1 %all-to-all-done.2 = bf16[16,64,1024]{2,1,0:T(8,128)(2,1)S(1)} async-done(((bf16[16,64,1024]{2,1,0:T(8,128)(2,1)}), bf16[16,64,1024]{2,1,0:T(8,128)(2,1)S(1)}, u32[]{:S(2)}, u32[]{:S(2)}) %all-to-all-start.2) | async-done | bytes 2097184 | tf_op jit(solution)/shard_map/all_to_all | solution.py:20
  169.3 6.0 %multiply_convert_fusion = bf16[1024,1024]{1,0:T(8,128)(2,1)} fusion(bf16[1024,1024]{1,0:T(8,128)(2,1)S(1)} %bitcast.57, bf16[1024,1024]{0,1:T(8,128)(2,1)} %bitcast.64), kind=kOutput, calls=%fused_computation | convolution fusion | flops 2149580800 | bytes 6291456 | tf_op jit(solution)/shard_map/dot_general | solution.py:126
  175.3 4.5 %reshape.102 = bf16[8,128,2,512]{3,2,1,0:T(2,128)(2,1)} reshape(bf16[1024,1024]{1,0:T(8,128)(2,1)} %multiply_convert_fusion) | data formatting | bytes 4194304 | tf_op jit(solution)/shard_map/reshape | solution.py:131
  183.2 8.5 %all-to-all-start.5 = ((bf16[16,128,512]{2,1,0:T(8,128)(2,1)}), bf16[16,128,512]{2,1,0:T(8,128)(2,1)S(1)}, u32[]{:S(2)}, u32[]{:S(2)}) async-start(bf16[16,128,512]{2,1,0:T(8,128)(2,1)} %bitcast.56), calls=%async_computation.5 | async-start | bytes 4194304 | tf_op jit(solution)/shard_map/all_to_all | solution.py:20
  196.7 21.6 %collective-permute-done.12 = bf16[8,64,1024]{2,1,0:T(8,128)(2,1)S(1)} collective-permute-done((bf16[8,64,1024]{2,1,0:T(8,128)(2,1)S(1)}, bf16[8,64,1024]{2,1,0:T(8,128)(2,1)S(1)}, u32[]{:S(2)}, u32[]{:S(2)}) %collective-permute-start.12) | collective-permute-done | bytes 1048608 | tf_op jit(solution)/shard_map/ppermute | solution.py:29
  218.5 3.7 %multiply_convert_fusion.1 = bf16[1024,1024]{1,0:T(8,128)(2,1)} fusion(bf16[1024,1024]{1,0:T(8,128)(2,1)S(1)} %bitcast.66, bf16[1024,1024]{0,1:T(8,128)(2,1)S(1)} %bitcast.65), kind=kOutput, calls=%fused_computation.1 | convolution fusion | flops 2149580800 | bytes 6291456 | tf_op jit(solution)/shard_map/dot_general | solution.py:126
  222.2 4.5 %reshape.98 = bf16[8,128,2,512]{3,2,1,0:T(2,128)(2,1)} reshape(bf16[1024,1024]{1,0:T(8,128)(2,1)} %multiply_convert_fusion.1) | data formatting | bytes 4194304 | tf_op jit(solution)/shard_map/reshape | solution.py:131
  231.5 7.3 %all-to-all-start.4 = ((bf16[16,128,512]{2,1,0:T(8,128)(2,1)}), bf16[16,128,512]{2,1,0:T(8,128)(2,1)}, u32[]{:S(2)}, u32[]{:S(2)}) async-start(bf16[16,128,512]{2,1,0:T(8,128)(2,1)} %bitcast.58), calls=%async_computation.4 | async-start | bytes 4194304 | tf_op jit(solution)/shard_map/all_to_all | solution.py:20
  238.8 9.6 %shard_map.46.rest_0_ = bf16[2,2,64,8192]{3,2,1,0:T(8,128)(2,1)} custom-call(s32[1]{0:T(128)} %bitcast.par_ref, bf16[8,2,2,64,512]{4,3,2,1,0:T(8,128)(2,1)} %bitcast.55), custom_call_target="tpu_custom_call" | custom-call | bytes 4194304 | tf_op jit(solution)/shard_map/pallas_call | solution.py:51
  248.4 15.7 %all-to-all-done.4 = bf16[16,128,512]{2,1,0:T(8,128)(2,1)} async-done(((bf16[16,128,512]{2,1,0:T(8,128)(2,1)}), bf16[16,128,512]{2,1,0:T(8,128)(2,1)}, u32[]{:S(2)}, u32[]{:S(2)}) %all-to-all-start.4) | async-done | bytes 2097184 | tf_op jit(solution)/shard_map/all_to_all | solution.py:20
  264.1 9.6 %shard_map.47 = bf16[2,2,64,8192]{3,2,1,0:T(8,128)(2,1)} custom-call(s32[1]{0:T(128)S(6)} %sub.14.par_ref, bf16[8,2,2,64,512]{4,3,2,1,0:T(8,128)(2,1)} %bitcast.23.in_ref, bf16[2,2,64,8192]{3,2,1,0:T(8,128)(2,1)} %shard_map.46.rest_0_), custom_call_target="tpu_custom_call", output_to_operand_aliasing={{}: (2, {})} | custom-call | bytes 4194304 | tf_op jit(solution)/shard_map/pallas_call | solution.py:51
  (71 shorter events, 67.4 us)
Async XLA Ops:
  2.3 1.6 collective-permute-start
  5.4 32.1 %all-to-all-start = ((bf16[16,32,1792]{2,1,0:T(8,128)(2,1)}), bf16[16,32,1792]{2,1,0:T(8,128)(2,1)S(1)}, u32[]{:S(2)}, u32[]{:S(2)}) async-start(bf16[16,32,1792]{2,1,0:T(8,128)(2,1)} %broadcast_in_dim.6), calls=%async_computation | async-start | bytes 3670016 | tf_op jit(solution)/shard_map/all_to_all | solution.py:20
  37.5 32.5 %all-to-all-start.1 = ((bf16[16,224,256]{2,1,0:T(8,128)(2,1)}), bf16[16,224,256]{2,1,0:T(8,128)(2,1)}, u32[]{:S(2)}, u32[]{:S(2)}) async-start(bf16[16,224,256]{2,1,0:T(8,128)(2,1)} %squeeze.17), calls=%async_computation.1 | async-start | bytes 3670016 | tf_op jit(solution)/shard_map/all_to_all | solution.py:20
  47.0 34.2 %collective-permute-start.1 = (bf16[256,1792]{1,0:T(8,128)(2,1)}, bf16[256,1792]{1,0:T(8,128)(2,1)}, u32[]{:S(2)}, u32[]{:S(2)}) collective-permute-start(bf16[256,1792]{1,0:T(8,128)(2,1)} %bitcast.3), channel_id=1, source_target_pairs={{0,1},{1,2},{2,3},{3,4},{4,5},{5,6},{6,7},{7,0},{8,9},{9,10},{10,1... | collective-permute-start | bytes 2752520 | tf_op jit(solution)/shard_map/ppermute | solution.py:29
  48.9 32.3 %collective-permute-start.2 = (bf16[256,1792]{1,0:T(8,128)(2,1)S(1)}, bf16[256,1792]{1,0:T(8,128)(2,1)}, u32[]{:S(2)}, u32[]{:S(2)}) collective-permute-start(bf16[256,1792]{1,0:T(8,128)(2,1)S(1)} %bitcast.70), channel_id=1, source_target_pairs={{0,7},{1,0},{2,1},{3,2},{4,3},{5,4},{6,5},{7,6},{8,15},{9,8},{10,9... | collective-permute-start | bytes 2752520 | tf_op jit(solution)/shard_map/ppermute | solution.py:29
  69.9 30.7 %all-to-all-start.3 = ((bf16[16,224,256]{2,1,0:T(8,128)(2,1)}), bf16[16,224,256]{2,1,0:T(8,128)(2,1)}, u32[]{:S(2)}, u32[]{:S(2)}) async-start(bf16[16,224,256]{2,1,0:T(8,128)(2,1)} %squeeze.19), calls=%async_computation.3 | async-start | bytes 3670016 | tf_op jit(solution)/shard_map/all_to_all | solution.py:20
  83.8 2.1 copy-start.2
  85.9 23.6 %collective-permute-start.3 = (f32[1024,512]{0,1:T(8,128)S(1)}, f32[1024,512]{0,1:T(8,128)}, u32[]{:S(2)}, u32[]{:S(2)}) collective-permute-start(f32[1024,512]{0,1:T(8,128)S(1)} %fusion.6), channel_id=1, source_target_pairs={{0,16},{16,0},{1,17},{17,1},{2,18},{18,2},{3,19},{19,3},{4,20},{20... | collective-permute-start | bytes 6291464 | tf_op jit(solution)/shard_map/ppermute | solution.py:107
  86.8 10.7 %collective-permute-start.4 = (f32[2,2,128]{2,1,0:T(2,128)S(1)}, f32[2,2,128]{2,1,0:T(2,128)S(1)}, u32[]{:S(2)}, u32[]{:S(2)}) collective-permute-start(f32[2,2,128]{2,1,0:T(2,128)S(1)} %bitcast.74), channel_id=1, source_target_pairs={{0,8},{8,0},{1,9},{9,1},{2,10},{10,2},{3,11},{11,3},{4,12},{12,4},... | collective-permute-start | bytes 6152 | tf_op jit(solution)/shard_map/ppermute | solution.py:97
  109.5 32.3 %collective-permute-start.14 = (f32[1024,512]{0,1:T(8,128)}, f32[1024,512]{0,1:T(8,128)}, u32[]{:S(2)}, u32[]{:S(2)}) collective-permute-start(f32[1024,512]{0,1:T(8,128)} %fusion.7), channel_id=1, source_target_pairs={{0,16},{16,0},{1,17},{17,1},{2,18},{18,2},{3,19},{19,3},{4,20},{20... | collective-permute-start | bytes 6291464 | tf_op jit(solution)/shard_map/ppermute | solution.py:107
  111.5 12.1 %collective-permute-start.10 = (bf16[64,1024]{1,0:T(8,128)(2,1)S(1)}, bf16[64,1024]{1,0:T(8,128)(2,1)S(1)}, u32[]{:S(2)}, u32[]{:S(2)}) collective-permute-start(bf16[64,1024]{1,0:T(8,128)(2,1)S(1)} %get-tuple-element.13), channel_id=1, source_target_pairs={{0,6},{8,14},{16,22},{24,30},{32,38},{40,46},{48,54},{56,62},{64,7... | collective-permute-start | bytes 393224 | tf_op jit(solution)/shard_map/ppermute | solution.py:118
  119.7 6.2 %collective-permute-start.11 = (bf16[64,1024]{1,0:T(8,128)(2,1)S(1)}, bf16[64,1024]{1,0:T(8,128)(2,1)S(1)}, u32[]{:S(2)}, u32[]{:S(2)}) collective-permute-start(bf16[64,1024]{1,0:T(8,128)(2,1)S(1)} %get-tuple-element.14), channel_id=1, source_target_pairs={{0,7},{8,15},{16,23},{24,31},{32,39},{40,47},{48,55},{56,63},{64,7... | collective-permute-start | bytes 393224 | tf_op jit(solution)/shard_map/ppermute | solution.py:118
  121.0 6.2 %collective-permute-start.5 = (bf16[64,1024]{1,0:T(8,128)(2,1)S(1)}, bf16[64,1024]{1,0:T(8,128)(2,1)S(1)}, u32[]{:S(2)}, u32[]{:S(2)}) collective-permute-start(bf16[64,1024]{1,0:T(8,128)(2,1)S(1)} %get-tuple-element.14), channel_id=1, source_target_pairs={{0,1},{8,9},{16,17},{24,25},{32,33},{40,41},{48,49},{56,57},{64,65... | collective-permute-start | bytes 393224 | tf_op jit(solution)/shard_map/ppermute | solution.py:118
  122.3 6.6 %collective-permute-start.6 = (bf16[64,1024]{1,0:T(8,128)(2,1)S(1)}, bf16[64,1024]{1,0:T(8,128)(2,1)S(1)}, u32[]{:S(2)}, u32[]{:S(2)}) collective-permute-start(bf16[64,1024]{1,0:T(8,128)(2,1)S(1)} %get-tuple-element.13), channel_id=1, source_target_pairs={{0,2},{8,10},{16,18},{24,26},{32,34},{40,42},{48,50},{56,58},{64,6... | collective-permute-start | bytes 393224 | tf_op jit(solution)/shard_map/ppermute | solution.py:118
  123.6 8.1 %collective-permute-start.7 = (bf16[64,1024]{1,0:T(8,128)(2,1)S(1)}, bf16[64,1024]{1,0:T(8,128)(2,1)S(1)}, u32[]{:S(2)}, u32[]{:S(2)}) collective-permute-start(bf16[64,1024]{1,0:T(8,128)(2,1)S(1)} %get-tuple-element.14), channel_id=1, source_target_pairs={{0,3},{8,11},{16,19},{24,27},{32,35},{40,43},{48,51},{56,59},{64,6... | collective-permute-start | bytes 393224 | tf_op jit(solution)/shard_map/ppermute | solution.py:118
  125.9 8.2 %collective-permute-start.8 = (bf16[64,1024]{1,0:T(8,128)(2,1)S(1)}, bf16[64,1024]{1,0:T(8,128)(2,1)S(1)}, u32[]{:S(2)}, u32[]{:S(2)}) collective-permute-start(bf16[64,1024]{1,0:T(8,128)(2,1)S(1)} %get-tuple-element.13), channel_id=1, source_target_pairs={{0,4},{8,12},{16,20},{24,28},{32,36},{40,44},{48,52},{56,60},{64,6... | collective-permute-start | bytes 393224 | tf_op jit(solution)/shard_map/ppermute | solution.py:118
  127.2 6.9 %collective-permute-start.9 = (bf16[64,1024]{1,0:T(8,128)(2,1)S(1)}, bf16[64,1024]{1,0:T(8,128)(2,1)S(1)}, u32[]{:S(2)}, u32[]{:S(2)}) collective-permute-start(bf16[64,1024]{1,0:T(8,128)(2,1)S(1)} %get-tuple-element.14), channel_id=1, source_target_pairs={{0,5},{8,13},{16,21},{24,29},{32,37},{40,45},{48,53},{56,61},{64,6... | collective-permute-start | bytes 393224 | tf_op jit(solution)/shard_map/ppermute | solution.py:118
  135.8 33.5 %all-to-all-start.2 = ((bf16[16,64,1024]{2,1,0:T(8,128)(2,1)}), bf16[16,64,1024]{2,1,0:T(8,128)(2,1)S(1)}, u32[]{:S(2)}, u32[]{:S(2)}) async-start(bf16[16,64,1024]{2,1,0:T(8,128)(2,1)} %broadcast_in_dim.8), calls=%async_computation.2 | async-start | bytes 4194304 | tf_op jit(solution)/shard_map/all_to_all | solution.py:20
  169.3 6.1 %copy-start.1 = (bf16[16,64,1024]{2,1,0:T(8,128)(2,1)}, bf16[16,64,1024]{2,1,0:T(8,128)(2,1)S(1)}, u32[]{:S(2)}) copy-start(bf16[16,64,1024]{2,1,0:T(8,128)(2,1)S(1)} %all-to-all-done.2) | copy-start | bytes 6291460
  183.2 46.9 %all-to-all-start.5 = ((bf16[16,128,512]{2,1,0:T(8,128)(2,1)}), bf16[16,128,512]{2,1,0:T(8,128)(2,1)S(1)}, u32[]{:S(2)}, u32[]{:S(2)}) async-start(bf16[16,128,512]{2,1,0:T(8,128)(2,1)} %bitcast.56), calls=%async_computation.5 | async-start | bytes 4194304 | tf_op jit(solution)/shard_map/all_to_all | solution.py:20
  193.4 24.9 %collective-permute-start.12 = (bf16[8,64,1024]{2,1,0:T(8,128)(2,1)S(1)}, bf16[8,64,1024]{2,1,0:T(8,128)(2,1)S(1)}, u32[]{:S(2)}, u32[]{:S(2)}) collective-permute-start(bf16[8,64,1024]{2,1,0:T(8,128)(2,1)S(1)} %get-tuple-element.7), channel_id=1, source_target_pairs={{0,1},{1,2},{2,3},{3,4},{4,5},{5,6},{6,7},{7,0},{8,9},{9,10},{10,1... | collective-permute-start | bytes 3145736 | tf_op jit(solution)/shard_map/ppermute | solution.py:29
  193.5 25.0 %copy-start.4 = (bf16[1024,2,2,256]{0,3,1,2:T(8,128)(2,1)S(1)}, bf16[1024,2,2,256]{0,3,1,2:T(8,128)(2,1)}, u32[]{:S(2)}) copy-start(bf16[1024,2,2,256]{0,3,1,2:T(8,128)(2,1)} %copy.12) | copy-start | bytes 6291460
  193.5 24.8 %collective-permute-start.13 = (bf16[8,64,1024]{2,1,0:T(8,128)(2,1)S(1)}, bf16[8,64,1024]{2,1,0:T(8,128)(2,1)S(1)}, u32[]{:S(2)}, u32[]{:S(2)}) collective-permute-start(bf16[8,64,1024]{2,1,0:T(8,128)(2,1)S(1)} %get-tuple-element.8), channel_id=1, source_target_pairs={{0,7},{1,0},{2,1},{3,2},{4,3},{5,4},{6,5},{7,6},{8,15},{9,8},{10,9... | collective-permute-start | bytes 3145736 | tf_op jit(solution)/shard_map/ppermute | solution.py:29
  231.5 32.6 %all-to-all-start.4 = ((bf16[16,128,512]{2,1,0:T(8,128)(2,1)}), bf16[16,128,512]{2,1,0:T(8,128)(2,1)}, u32[]{:S(2)}, u32[]{:S(2)}) async-start(bf16[16,128,512]{2,1,0:T(8,128)(2,1)} %bitcast.58), calls=%async_computation.4 | async-start | bytes 4194304 | tf_op jit(solution)/shard_map/all_to_all | solution.py:20
  (2 other events, 3.4 us)

commit v3 on v0

v3 whole, which is shorter than its diff:
```python
import jax
import jax.numpy as jnp
from jax import lax
from jax.experimental import pallas as pl
from jax.experimental.pallas import tpu as pltpu
from jax.sharding import Mesh, PartitionSpec as P

AXES = ("y", "xh", "c", "xl", "z")
SIZES = (4, 2, 2, 2, 8)
PLANE = ("y", "xh", "xl")
ROW = ("xh", "c", "xl")
TOK = ("y", "xh", "c")
LATENT = ("xl", "z")
YS, CHIPS, CORES, XLO, DEPTH = 4, 8, 2, 2, 8
PEERS = CHIPS * XLO
MATES = 8
SWAP = [(0, 1), (1, 0)]
VMEM = 60 * 1024 * 1024
ORDER = ((0, 0), (-1, 0), (1, 0), (-2, 0), (2, 0), (-3, 0), (3, 0), (4, 0), (4, 1))


def shift(axis, step):
    size = SIZES[AXES.index(axis)]
    return [(i, (i + step) % size) for i in range(size)]


def params(**kw):
    return pltpu.CompilerParams(vmem_limit_bytes=VMEM, **kw)


def cost(flops, moved):
    return pl.CostEstimate(flops=flops, bytes_accessed=moved, transcendentals=0)


def exchange(block, axes):
    return lax.all_to_all(block, axes, split_axis=0, concat_axis=0, tiled=True)


def spread(block, axes, count):
    return exchange(jnp.broadcast_to(block[None], (count,) + block.shape), axes)


def regroup(weight, lane):
    rows = weight.shape[0]

    def body(in_ref, out_ref):
        for xl in range(XLO):
            for c in range(CORES):
                at = (c * XLO + xl) * lane
                out_ref[xl, :, c * lane : (c + 1) * lane] = in_ref[:, at : at + lane]

    return pl.pallas_call(
        body,
        out_shape=jax.ShapeDtypeStruct((PEERS, rows, 2 * CORES * lane), weight.dtype),
        grid=(2, CHIPS),
        in_specs=[pl.BlockSpec((rows, CORES * XLO * lane), lambda h, t: (0, h * CHIPS + t))],
        out_specs=pl.BlockSpec((XLO, rows, CORES * lane), lambda h, t: (t, 0, h)),
        cost_estimate=cost(0, 4 * PEERS * rows * 2 * CORES * lane),
        compiler_params=params(),
    )(weight)


def encode(place_ids, pieces, weight, lane):
    depth = pieces[0].shape[1]
    _, rows, cols = weight.shape
    strip = pieces[0].shape[0]
    total, wide = DEPTH * strip, XLO * cols
    chunk = 2 * strip
    count = len(pieces)

    def body(ids_ref, *refs):
        weight_ref, keep_ref, give_ref, batch, grid, sems = refs[count:]
        z, core = ids_ref[0], ids_ref[1]
        copies = [
            pltpu.make_async_copy(
                weight_ref.at[p],
                grid.at[pl.ds((p // XLO) * rows, rows), pl.ds((p % XLO) * cols, cols)],
                sems.at[p],
            )
            for p in range(PEERS)
        ]
        for i, (ref, (step, cut)) in enumerate(zip(refs[:count], ORDER)):
            start = lax.rem(z + step + DEPTH, DEPTH) * strip + cut * (strip // 2)
            at = pl.ds(pl.multiple_of(start, strip // 2), ref.shape[0])
            copies.append(pltpu.make_async_copy(ref, batch.at[at], sems.at[PEERS + i]))
        for copy in copies:
            copy.start()
        for copy in copies:
            copy.wait()

        @pl.loop(0, total // chunk)
        def _(i):
            at = pl.ds(pl.multiple_of(i * chunk, chunk), chunk)
            for xl in range(XLO):
                out = jnp.dot(
                    batch[at], grid[:, xl * cols : (xl + 1) * cols],
                    preferred_element_type=jnp.float32,
                )
                for h in range(2):
                    a = out[:, 2 * h * lane : (2 * h + 1) * lane]
                    b = out[:, (2 * h + 1) * lane : (2 * h + 2) * lane]
                    to = pl.ds((xl * 2 + h) * lane, lane)
                    keep_ref[at, to] = jnp.where(core == 0, a, b)
                    give_ref[at, to] = jnp.where(core == 0, b, a).astype(jnp.bfloat16)

    mine = wide // CORES
    return pl.pallas_call(
        body,
        out_shape=(
            jax.ShapeDtypeStruct((total, mine), jnp.float32),
            jax.ShapeDtypeStruct((total, mine), jnp.bfloat16),
        ),
        in_specs=[pl.BlockSpec(memory_space=pltpu.SMEM)]
        + [pl.BlockSpec(memory_space=pl.ANY)] * (count + 1),
        out_specs=(pl.BlockSpec(memory_space=pltpu.VMEM), pl.BlockSpec(memory_space=pltpu.VMEM)),
        scratch_shapes=[
            pltpu.VMEM((total, depth), jnp.bfloat16),
            pltpu.VMEM((CHIPS * rows, wide), jnp.bfloat16),
            pltpu.SemaphoreType.DMA((PEERS + count,)),
        ],
        cost_estimate=cost(2 * total * depth * wide, 2 * depth * (total + wide) + 6 * total * mine),
        compiler_params=params(),
    )(place_ids, *pieces, weight)


def gram(panel, own, below, above, far_low, far_high):
    _, strip, total = panel.shape
    wide = own.shape[1]
    cols = wide // XLO
    height = XLO * strip
    cut = total // 2

    def body(panel_ref, own_ref, below_ref, above_ref, low_ref, high_ref, out_ref):
        rows = panel_ref[...].reshape(height, total)
        for r in range(YS):
            if r < 3:
                ref = (own_ref, below_ref, above_ref)[r]
                out = jnp.dot(rows, ref[...], preferred_element_type=jnp.float32)
            else:
                out = jnp.dot(rows[:, :cut], low_ref[...], preferred_element_type=jnp.float32)
                out += jnp.dot(rows[:, cut:], high_ref[...], preferred_element_type=jnp.float32)
            out = (out * (1.0 / total)).astype(jnp.bfloat16)
            for xl in range(XLO):
                out_ref[xl, :, r * cols : (r + 1) * cols] = out[:, xl * cols : (xl + 1) * cols]

    def whole(a):
        return pl.BlockSpec(a.shape, lambda t: (0, 0))

    acts = (own, below, above, far_low, far_high)
    return pl.pallas_call(
        body,
        out_shape=jax.ShapeDtypeStruct((MATES, height, YS * cols), jnp.bfloat16),
        grid=(MATES // XLO,),
        in_specs=[pl.BlockSpec((XLO, strip, total), lambda t: (t, 0, 0))] + [whole(a) for a in acts],
        out_specs=pl.BlockSpec((XLO, height, YS * cols), lambda t: (t, 0, 0)),
        cost_estimate=cost(
            2 * (MATES // XLO) * height * total * YS * wide,
            2 * (MATES * strip * total + YS * total * wide + MATES * height * YS * cols),
        ),
        compiler_params=params(),
    )(panel, *acts)


def place(ys, received, lane):
    _, height, wide = received.shape
    slab = MATES * wide

    def body(ys_ref, in_ref, out_ref):
        for s in range(MATES):
            out_ref[:, s * lane : (s + 1) * lane] = in_ref[s]

    return pl.pallas_call(
        body,
        out_shape=jax.ShapeDtypeStruct((height, slab), jnp.bfloat16),
        grid_spec=pltpu.PrefetchScalarGridSpec(
            num_scalar_prefetch=1,
            grid=(YS, 2),
            in_specs=[pl.BlockSpec((MATES, height, lane), lambda r, h, ys: (0, 0, 2 * r + h))],
            out_specs=pl.BlockSpec((height, MATES * lane), lambda r, h, ys: (0, h * YS + ys[r])),
        ),
        cost_estimate=cost(0, 4 * height * slab),
        compiler_params=params(),
    )(ys, received)


def per_device(tokens, dec_bias, enc_weight, enc_bias):
    own, width = tokens.shape
    rows, slab = enc_weight.shape
    lane = slab // (2 * CHIPS * CORES * XLO)
    total = own * CHIPS * CORES
    core = lax.axis_index("c")
    xlo = lax.axis_index("xl")
    y = lax.axis_index("y")
    chip = y * 2 + lax.axis_index("xh")
    z = lax.axis_index("z")
    ids = jnp.stack([z, core]).astype(jnp.int32)
    ys = lax.rem(jnp.stack([y, y + 3, y + 1, y + 2]), YS).astype(jnp.int32)

    centered = (tokens.astype(jnp.float32) - dec_bias).astype(jnp.bfloat16)
    halves = centered.reshape(own, CHIPS, CORES, rows).transpose(2, 0, 1, 3)
    halves = halves.reshape(CORES, own, CHIPS * rows)
    keep = jnp.where(core == 0, halves[0], halves[1])
    give = jnp.where(core == 0, halves[1], halves[0])
    got = lax.ppermute(give, "c", SWAP)
    mine = jnp.where(core == xlo, keep, got)
    part = own // DEPTH
    mine = lax.dynamic_slice_in_dim(mine, z * part, part, 0)
    near = spread(mine, PLANE, PEERS).reshape(total // DEPTH, CHIPS * rows)
    pieces = [near]
    low = high = near
    for _ in range(DEPTH // 2 - 1):
        low = lax.ppermute(low, "z", shift("z", 1))
        high = lax.ppermute(high, "z", shift("z", -1))
        pieces += [low, high]
    cut = near.shape[0] // 2
    pieces.append(lax.ppermute(low[:cut], "z", shift("z", 1)))
    pieces.append(lax.ppermute(high[cut:], "z", shift("z", -1)))

    biases = enc_bias.reshape(2, CHIPS, CORES, XLO, lane)
    biases = lax.dynamic_index_in_dim(biases, chip, 1, keepdims=False)
    biases = lax.dynamic_index_in_dim(biases, core, 1, keepdims=False)
    bias_keep = lax.dynamic_index_in_dim(biases, xlo, 1, keepdims=False)
    bias_give = lax.dynamic_index_in_dim(biases, 1 - xlo, 1, keepdims=False)
    bias_got = lax.ppermute(bias_give, "xl", SWAP)
    bias = jnp.where(xlo == 0, jnp.stack([bias_keep, bias_got]), jnp.stack([bias_got, bias_keep]))

    weight = exchange(regroup(enc_weight, lane), PLANE)
    sums, sent = encode(ids, pieces, weight, lane)
    other = lax.ppermute(sent, "c", SWAP).astype(jnp.float32)
    activity = jnp.maximum(sums + other + bias.reshape(-1), 0.0).astype(jnp.bfloat16)

    panel = activity[:, :lane].T
    held = panel
    span = DEPTH // 2
    while span:
        moved = lax.ppermute(held, "z", [(i, i + span) for i in range(0, DEPTH, 2 * span)])
        held = jnp.where(lax.rem(z, 2 * span) == span, moved, held)
        span //= 2

    cut = total // 2
    below = lax.ppermute(activity, "y", shift("y", 1))
    above = lax.ppermute(activity, "y", shift("y", -1))
    held, below, above = lax.optimization_barrier((held, below, above))
    panel = spread(held, ROW, MATES)
    far_low = lax.ppermute(above[:cut], "y", shift("y", -1))
    far_high = lax.ppermute(below[cut:], "y", shift("y", 1))

    result = exchange(gram(panel, activity, below, above, far_low, far_high), ROW)
    return place(ys, result, lane)


def solution(mesh):
    fine = Mesh(mesh.devices.reshape(SIZES), AXES)
    return jax.shard_map(
        per_device,
        mesh=fine,
        in_specs=(P(TOK, None), P(), P(TOK, LATENT), P(LATENT)),
        out_specs=P(TOK, LATENT),
        check_vma=False,
    )
```

time: 564 us -> 241 us (0.43)
  waiting for transfers between devices: 362 us -> 125 us
  local copies, waits for them, and re-layouts: 100 us -> 8.12 us
  starting transfers between devices: 6.4 us -> 64.4 us
  blocking collectives: 57.8 us -> 0 us
  Pallas kernels: 0 us -> 36.5 us
  matrix products: 16.5 us -> 0 us
  between operations: 13.2 us -> 0.32 us
    psum x1 -> x0, waiting for transfers between devices: 198 us -> none  [spread_2(): return lax.psum(jnp.where(mine, shard, jnp.zeros_like(shard)), axis)]
    all_gather x2 -> x0, waiting for transfers between devices: 115 us -> none  [the longest x1 80.1 us: per_device(): columns = lax.all_gather(leading, 'tok', axis=1, tiled=True)]
    ppermute x0 -> x18, waiting for transfers between devices: none -> 66.2 us  [the longest x3 26.5 us: per_device(): low = lax.ppermute(low, 'z', shift('z', 1))]
    all_to_all x1 -> x0, blocking collectives: 57.8 us -> none  [per_device(): lax.all_to_all(blocks, 'tok', split_axis=1, concat_axis=1, tiled=True)]
    reshape x3 -> x2, local copies, waits for them, and re-layouts: 58.4 us -> 0.89 us  [per_device(): halves = centered.reshape(own, CHIPS, CORES, rows).transpose(2, 0, 1, 3)]
    ppermute x0 -> x18, starting transfers between devices: none -> 38.6 us  [the longest x3 11.7 us: per_device(): lax.ppermute(held, 'z', [(i, i + span) for i in range(0, DEPTH, 2 * span)])]
    pallas_call x0 -> x4, Pallas kernels: none -> 36.5 us  [the longest x1 10.2 us: encode(): pl.pallas_call(body, out_shape=(jax.ShapeDtypeStruct((total, mine), jnp.f...]
    transpose x2 -> x1, local copies, waits for them, and re-layouts: 34.5 us -> 0.04 us  [per_device(): panel = activity[:, :lane].T]
  transfers between devices with their start and end apart: 4 -> 22, of which waited for: 4 -> 15; matrix products, arithmetic and copies ran while one was open for 3% -> 1% of each run, Pallas kernels for 0% -> 4%
where the time goes in v3:
time: 241 us; the launch traced here: 239 us
  waiting for transfers between devices  125 us (52%)
  starting transfers between devices  64.4 us (27%)
  Pallas kernels  36.5 us (15%)
  local copies, waits for them, and re-layouts  8.12 us (3%)
  other arithmetic  4.49 us (2%)
    all_to_all x4, waiting for transfers between devices, exchange(): return lax.all_to_all(block, axes, split_axis=0, concat_axis=0, tiled=True)  58.5 us
    ppermute x3, waiting for transfers between devices, per_device(): low = lax.ppermute(low, 'z', shift('z', 1))  26.5 us
    all_to_all x4, starting transfers between devices, exchange(): return lax.all_to_all(block, axes, split_axis=0, concat_axis=0, tiled=True)  25.8 us
    ppermute x3, starting transfers between devices, per_device(): lax.ppermute(held, 'z', [(i, i + span) for i in range(0, DEPTH, 2 * span)])  11.7 us
    ppermute x1, waiting for transfers between devices, per_device(): far_low = lax.ppermute(above[:cut], 'y', shift('y', -1))  11.4 us
    ppermute x3, waiting for transfers between devices, per_device(): lax.ppermute(held, 'z', [(i, i + span) for i in range(0, DEPTH, 2 * span)])  10.7 us
    ppermute x3, starting transfers between devices, per_device(): high = lax.ppermute(high, 'z', shift('z', -1))  10.5 us
    pallas_call x1, Pallas kernels, encode(): pl.pallas_call(body, out_shape=(jax.ShapeDtypeStruct((total, mine), jnp.f...  10.2 us
  transfers between devices with their start and end apart: 22, of which 15 were waited for; matrix products, arithmetic and copies ran while one was open for 1% of the time, Pallas kernels for 4%

profile of v3, /device:TPU:2, one launch (start us, length us, event | category | flops | bytes accessed | tf_op | source)
XLA Modules:
  0.0 238.6 jit_solution(3319469395572380768)
XLA Ops:
  4.7 7.5 %all-to-all-start = ((bf16[16,8,1792]{2,1,0:T(8,128)(2,1)}), bf16[16,8,1792]{2,1,0:T(8,128)(2,1)S(1)}, u32[]{:S(2)}, u32[]{:S(2)}) async-start(bf16[16,8,1792]{2,1,0:T(8,128)(2,1)} %broadcast_in_dim.4), calls=%async_computation | async-start | bytes 917504 | tf_op jit(solution)/shard_map/all_to_all | solution.py:36
  12.2 10.1 %shard_map.46 = bf16[16,224,512]{2,1,0:T(8,128)(2,1)} custom-call(bf16[224,8192]{1,0:T(8,128)(2,1)} %in_ref.1), custom_call_target="tpu_custom_call" | custom-call | bytes 7340032 | tf_op jit(solution)/shard_map/pallas_call | solution.py:52
  22.3 7.2 %all-to-all-start.1 = ((bf16[16,224,512]{2,1,0:T(8,128)(2,1)}), bf16[16,224,512]{2,1,0:T(8,128)(2,1)}, u32[]{:S(2)}, u32[]{:S(2)}) async-start(bf16[16,224,512]{2,1,0:T(8,128)(2,1)} %shard_map.46), calls=%async_computation.1 | async-start | bytes 7340032 | tf_op jit(solution)/shard_map/all_to_all | solution.py:36
  31.5 4.0 %collective-permute-start.2 = (bf16[128,1792]{1,0:T(8,128)(2,1)S(1)}, bf16[128,1792]{1,0:T(8,128)(2,1)S(1)}, u32[]{:S(2)}, u32[]{:S(2)}) collective-permute-start(bf16[128,1792]{1,0:T(8,128)(2,1)S(1)} %bitcast.25), channel_id=1, source_target_pairs={{0,7},{1,0},{2,1},{3,2},{4,3},{5,4},{6,5},{7,6},{8,15},{9,8},{10,9... | collective-permute-start | bytes 1376264 | tf_op jit(solution)/shard_map/ppermute | solution.py:213
  35.5 9.6 %collective-permute-done.1.refs_1_ = bf16[128,1792]{1,0:T(8,128)(2,1)S(1)} collective-permute-done((bf16[128,1792]{1,0:T(8,128)(2,1)S(1)}, bf16[128,1792]{1,0:T(8,128)(2,1)S(1)}, u32[]{:S(2)}, u32[]{:S(2)}) %collective-permute-start.1) | collective-permute-done | bytes 458784 | tf_op jit(solution)/shard_map/ppermute | solution.py:212
  48.4 8.9 %collective-permute-done.3.refs_3_ = bf16[128,1792]{1,0:T(8,128)(2,1)S(1)} collective-permute-done((bf16[128,1792]{1,0:T(8,128)(2,1)S(1)}, bf16[128,1792]{1,0:T(8,128)(2,1)S(1)}, u32[]{:S(2)}, u32[]{:S(2)}) %collective-permute-start.3) | collective-permute-done | bytes 458784 | tf_op jit(solution)/shard_map/ppermute | solution.py:212
  57.3 3.2 %collective-permute-start.6 = (bf16[128,1792]{1,0:T(8,128)(2,1)S(1)}, bf16[128,1792]{1,0:T(8,128)(2,1)S(1)}, u32[]{:S(2)}, u32[]{:S(2)}) collective-permute-start(bf16[128,1792]{1,0:T(8,128)(2,1)S(1)} %collective-permute-done.4.refs_4_), channel_id=1, source_target_pairs={{0,7},{1,0},{2,1},{3,2},{4,3},{5,4},{6,5},{7,6},{8,15},{9,8},{10,9... | collective-permute-start | bytes 1376264 | tf_op jit(solution)/shard_map/ppermute | solution.py:213
  60.5 8.1 %collective-permute-done.5.refs_5_ = bf16[128,1792]{1,0:T(8,128)(2,1)S(1)} collective-permute-done((bf16[128,1792]{1,0:T(8,128)(2,1)S(1)}, bf16[128,1792]{1,0:T(8,128)(2,1)S(1)}, u32[]{:S(2)}, u32[]{:S(2)}) %collective-permute-start.5) | collective-permute-done | bytes 458784 | tf_op jit(solution)/shard_map/ppermute | solution.py:212
  68.7 3.3 %collective-permute-start.8 = (bf16[64,1792]{1,0:T(8,128)(2,1)S(1)}, bf16[64,1792]{1,0:T(8,128)(2,1)S(1)}, u32[]{:S(2)}, u32[]{:S(2)}) collective-permute-start(bf16[64,1792]{1,0:T(8,128)(2,1)S(1)} %slice.35), channel_id=1, source_target_pairs={{0,7},{1,0},{2,1},{3,2},{4,3},{5,4},{6,5},{7,6},{8,15},{9,8},{10,9... | collective-permute-start | bytes 688136 | tf_op jit(solution)/shard_map/ppermute | solution.py:217
  72.6 3.3 %collective-permute-done.7.refs_7_ = bf16[64,1792]{1,0:T(8,128)(2,1)S(1)} collective-permute-done((bf16[64,1792]{1,0:T(8,128)(2,1)S(1)}, bf16[64,1792]{1,0:T(8,128)(2,1)S(1)}, u32[]{:S(2)}, u32[]{:S(2)}) %collective-permute-start.7) | collective-permute-done | bytes 229408 | tf_op jit(solution)/shard_map/ppermute | solution.py:216
  75.9 4.2 %all-to-all-done.1.refs_9_ = bf16[16,224,512]{2,1,0:T(8,128)(2,1)} async-done(((bf16[16,224,512]{2,1,0:T(8,128)(2,1)}), bf16[16,224,512]{2,1,0:T(8,128)(2,1)}, u32[]{:S(2)}, u32[]{:S(2)}) %all-to-all-start.1) | async-done | bytes 3670048 | tf_op jit(solution)/shard_map/all_to_all | solution.py:36
  80.1 10.2 %shard_map.47 = (f32[1024,512]{1,0:T(8,128)}, bf16[1024,512]{1,0:T(8,128)(2,1)}) custom-call(s32[2]{0:T(128)} %pad_add_fusion.ids_ref, bf16[128,1792]{1,0:T(8,128)(2,1)} %bitcast.26, bf16[128,1792]{1,0:T(8,128)(2,1)} %copy-done.8, bf16[128,1792]{1,0:T(8,128)(2,1)} %copy-done.9, bf16[128,1792]{1,0:T(8,128)(2,1)} %copy-done.10, bf16[128,1792]{1,0:T(8,128)(2,1)} %copy-done.11, ...), custom_call_target="tpu_custom_call" | custom-call | flops 3758096384 | bytes 10485760 | tf_op jit(solution)/shard_map/pallas_call | solution.py:107
  91.2 4.2 %collective-permute-start.10 = (f32[2,128]{1,0:T(2,128)S(1)}, f32[2,128]{1,0:T(2,128)S(1)}, u32[]{:S(2)}, u32[]{:S(2)}) collective-permute-start(f32[2,128]{1,0:T(2,128)S(1)} %bitcast.29), channel_id=1, source_target_pairs={{0,8},{8,0},{1,9},{9,1},{2,10},{10,2},{3,11},{11,3},{4,12},{12,4},... | collective-permute-start | bytes 3080 | tf_op jit(solution)/shard_map/ppermute | solution.py:224
  99.0 9.1 %collective-permute-start.11 = (bf16[128,1024]{0,1:T(8,128)(2,1)S(1)}, bf16[128,1024]{0,1:T(8,128)(2,1)S(1)}, u32[]{:S(2)}, u32[]{:S(2)}) collective-permute-start(bf16[128,1024]{0,1:T(8,128)(2,1)S(1)} %slice_bitcast_fusion), channel_id=1, source_target_pairs={{0,4},{8,12},{16,20},{24,28},{32,36},{40,44},{48,52},{56,60},{64,6... | collective-permute-start | bytes 786440 | tf_op jit(solution)/shard_map/ppermute | solution.py:236
  114.8 4.8 %collective-permute-done.12 = bf16[128,1024]{0,1:T(8,128)(2,1)S(1)} collective-permute-done((bf16[128,1024]{0,1:T(8,128)(2,1)S(1)}, bf16[128,1024]{0,1:T(8,128)(2,1)S(1)}, u32[]{:S(2)}, u32[]{:S(2)}) %collective-permute-start.12) | collective-permute-done | bytes 262176 | tf_op jit(solution)/shard_map/ppermute | solution.py:236
  121.0 4.1 %collective-permute-done.13 = bf16[128,1024]{0,1:T(8,128)(2,1)S(1)} collective-permute-done((bf16[128,1024]{0,1:T(8,128)(2,1)S(1)}, bf16[128,1024]{0,1:T(8,128)(2,1)S(1)}, u32[]{:S(2)}, u32[]{:S(2)}) %collective-permute-start.13) | collective-permute-done | bytes 262176 | tf_op jit(solution)/shard_map/ppermute | solution.py:236
  125.1 8.9 %collective-permute-done.14.below_ref = bf16[1024,512]{1,0:T(8,128)(2,1)S(1)} collective-permute-done((bf16[1024,512]{1,0:T(8,128)(2,1)S(1)}, bf16[1024,512]{1,0:T(8,128)(2,1)S(1)}, u32[]{:S(2)}, u32[]{:S(2)}) %collective-permute-start.14) | collective-permute-done | bytes 1048608 | tf_op jit(solution)/shard_map/ppermute | solution.py:241
  135.7 5.2 %all-to-all-start.2 = ((bf16[8,128,1024]{2,1,0:T(8,128)(2,1)}), bf16[8,128,1024]{2,1,0:T(8,128)(2,1)S(1)}, u32[]{:S(2)}, u32[]{:S(2)}) async-start(bf16[8,128,1024]{2,1,0:T(8,128)(2,1)} %broadcast_in_dim.5), calls=%async_computation.2 | async-start | bytes 4194304 | tf_op jit(solution)/shard_map/all_to_all | solution.py:36
  145.3 11.4 %collective-permute-done.16.low_ref = bf16[512,512]{1,0:T(8,128)(2,1)S(1)} collective-permute-done((bf16[512,512]{1,0:T(8,128)(2,1)S(1)}, bf16[512,512]{1,0:T(8,128)(2,1)S(1)}, u32[]{:S(2)}, u32[]{:S(2)}) %collective-permute-start.16) | collective-permute-done | bytes 524320 | tf_op jit(solution)/shard_map/ppermute | solution.py:245
  160.2 6.6 %all-to-all-done.2.panel_ref = bf16[8,128,1024]{2,1,0:T(8,128)(2,1)S(1)} async-done(((bf16[8,128,1024]{2,1,0:T(8,128)(2,1)}), bf16[8,128,1024]{2,1,0:T(8,128)(2,1)S(1)}, u32[]{:S(2)}, u32[]{:S(2)}) %all-to-all-start.2) | async-done | bytes 2097184 | tf_op jit(solution)/shard_map/all_to_all | solution.py:36
  168.2 8.5 %shard_map.48 = bf16[8,256,1024]{2,1,0:T(8,128)(2,1)} custom-call(bf16[8,128,1024]{2,1,0:T(8,128)(2,1)} %copy-done.1, bf16[1024,512]{1,0:T(8,128)(2,1)} %copy-done, bf16[1024,512]{1,0:T(8,128)(2,1)} %copy-done.3, bf16[1024,512]{1,0:T(8,128)(2,1)} %collective-permute-done.15.above_ref, bf16[512,512]{1,0:T(8,128)(2,1)} %copy-done.6, bf16[512,512]{1,0:T(8,128)(2,1)} %copy-done.7), custom_call_target="tpu_custom_call" | custom-call | flops 4294967296 | bytes 10485760 | tf_op jit(solution)/shard_map/pallas_call | solution.py:150
  176.7 5.9 %all-to-all-start.3 = ((bf16[8,256,1024]{2,1,0:T(8,128)(2,1)}), bf16[8,256,1024]{2,1,0:T(8,128)(2,1)}, u32[]{:S(2)}, u32[]{:S(2)}) async-start(bf16[8,256,1024]{2,1,0:T(8,128)(2,1)} %shard_map.48), calls=%async_computation.3 | async-start | bytes 8388608 | tf_op jit(solution)/shard_map/all_to_all | solution.py:36
  183.2 47.7 %all-to-all-done.3.in_ref = bf16[8,256,1024]{2,1,0:T(8,128)(2,1)} async-done(((bf16[8,256,1024]{2,1,0:T(8,128)(2,1)}), bf16[8,256,1024]{2,1,0:T(8,128)(2,1)}, u32[]{:S(2)}, u32[]{:S(2)}) %all-to-all-start.3) | async-done | bytes 4194336 | tf_op jit(solution)/shard_map/all_to_all | solution.py:36
  230.9 7.7 %shard_map.49 = bf16[256,8192]{1,0:T(8,128)(2,1)} custom-call(s32[4]{0:T(128)} %compare_select_fusion.ys_ref, bf16[8,256,1024]{2,1,0:T(8,128)(2,1)} %all-to-all-done.3.in_ref), custom_call_target="tpu_custom_call" | custom-call | bytes 8388608 | tf_op jit(solution)/shard_map/pallas_call | solution.py:172
  (75 shorter events, 34.6 us)
Async XLA Ops:
  2.3 1.6 collective-permute-start
  4.7 17.6 %all-to-all-start = ((bf16[16,8,1792]{2,1,0:T(8,128)(2,1)}), bf16[16,8,1792]{2,1,0:T(8,128)(2,1)S(1)}, u32[]{:S(2)}, u32[]{:S(2)}) async-start(bf16[16,8,1792]{2,1,0:T(8,128)(2,1)} %broadcast_in_dim.4), calls=%async_computation | async-start | bytes 917504 | tf_op jit(solution)/shard_map/all_to_all | solution.py:36
  22.3 57.7 %all-to-all-start.1 = ((bf16[16,224,512]{2,1,0:T(8,128)(2,1)}), bf16[16,224,512]{2,1,0:T(8,128)(2,1)}, u32[]{:S(2)}, u32[]{:S(2)}) async-start(bf16[16,224,512]{2,1,0:T(8,128)(2,1)} %shard_map.46), calls=%async_computation.1 | async-start | bytes 7340032 | tf_op jit(solution)/shard_map/all_to_all | solution.py:36
  29.6 15.6 %collective-permute-start.1 = (bf16[128,1792]{1,0:T(8,128)(2,1)S(1)}, bf16[128,1792]{1,0:T(8,128)(2,1)S(1)}, u32[]{:S(2)}, u32[]{:S(2)}) collective-permute-start(bf16[128,1792]{1,0:T(8,128)(2,1)S(1)} %bitcast.24), channel_id=1, source_target_pairs={{0,1},{1,2},{2,3},{3,4},{4,5},{5,6},{6,7},{7,0},{8,9},{9,10},{10,1... | collective-permute-start | bytes 1376264 | tf_op jit(solution)/shard_map/ppermute | solution.py:212
  31.5 13.6 %collective-permute-start.2 = (bf16[128,1792]{1,0:T(8,128)(2,1)S(1)}, bf16[128,1792]{1,0:T(8,128)(2,1)S(1)}, u32[]{:S(2)}, u32[]{:S(2)}) collective-permute-start(bf16[128,1792]{1,0:T(8,128)(2,1)S(1)} %bitcast.25), channel_id=1, source_target_pairs={{0,7},{1,0},{2,1},{3,2},{4,3},{5,4},{6,5},{7,6},{8,15},{9,8},{10,9... | collective-permute-start | bytes 1376264 | tf_op jit(solution)/shard_map/ppermute | solution.py:213
  45.1 34.9 %copy-start.8 = (bf16[128,1792]{1,0:T(8,128)(2,1)}, bf16[128,1792]{1,0:T(8,128)(2,1)S(1)}, u32[]{:S(2)}) copy-start(bf16[128,1792]{1,0:T(8,128)(2,1)S(1)} %collective-permute-done.1.refs_1_) | copy-start | bytes 1376260
  45.1 12.1 %collective-permute-start.3 = (bf16[128,1792]{1,0:T(8,128)(2,1)S(1)}, bf16[128,1792]{1,0:T(8,128)(2,1)S(1)}, u32[]{:S(2)}, u32[]{:S(2)}) collective-permute-start(bf16[128,1792]{1,0:T(8,128)(2,1)S(1)} %collective-permute-done.1.refs_1_), channel_id=1, source_target_pairs={{0,1},{1,2},{2,3},{3,4},{4,5},{5,6},{6,7},{7,0},{8,9},{9,10},{10,1... | collective-permute-start | bytes 1376264 | tf_op jit(solution)/shard_map/ppermute | solution.py:212
  45.1 12.1 %collective-permute-start.4 = (bf16[128,1792]{1,0:T(8,128)(2,1)S(1)}, bf16[128,1792]{1,0:T(8,128)(2,1)S(1)}, u32[]{:S(2)}, u32[]{:S(2)}) collective-permute-start(bf16[128,1792]{1,0:T(8,128)(2,1)S(1)} %collective-permute-done.2.refs_2_), channel_id=1, source_target_pairs={{0,7},{1,0},{2,1},{3,2},{4,3},{5,4},{6,5},{7,6},{8,15},{9,8},{10,9... | collective-permute-start | bytes 1376264 | tf_op jit(solution)/shard_map/ppermute | solution.py:213
  57.2 11.3 %collective-permute-start.5 = (bf16[128,1792]{1,0:T(8,128)(2,1)S(1)}, bf16[128,1792]{1,0:T(8,128)(2,1)S(1)}, u32[]{:S(2)}, u32[]{:S(2)}) collective-permute-start(bf16[128,1792]{1,0:T(8,128)(2,1)S(1)} %collective-permute-done.3.refs_3_), channel_id=1, source_target_pairs={{0,1},{1,2},{2,3},{3,4},{4,5},{5,6},{6,7},{7,0},{8,9},{9,10},{10,1... | collective-permute-start | bytes 1376264 | tf_op jit(solution)/shard_map/ppermute | solution.py:212
  57.3 11.4 %collective-permute-start.6 = (bf16[128,1792]{1,0:T(8,128)(2,1)S(1)}, bf16[128,1792]{1,0:T(8,128)(2,1)S(1)}, u32[]{:S(2)}, u32[]{:S(2)}) collective-permute-start(bf16[128,1792]{1,0:T(8,128)(2,1)S(1)} %collective-permute-done.4.refs_4_), channel_id=1, source_target_pairs={{0,7},{1,0},{2,1},{3,2},{4,3},{5,4},{6,5},{7,6},{8,15},{9,8},{10,9... | collective-permute-start | bytes 1376264 | tf_op jit(solution)/shard_map/ppermute | solution.py:213
  68.6 7.3 %collective-permute-start.7 = (bf16[64,1792]{1,0:T(8,128)(2,1)S(1)}, bf16[64,1792]{1,0:T(8,128)(2,1)S(1)}, u32[]{:S(2)}, u32[]{:S(2)}) collective-permute-start(bf16[64,1792]{1,0:T(8,128)(2,1)S(1)} %slice.34), channel_id=1, source_target_pairs={{0,1},{1,2},{2,3},{3,4},{4,5},{5,6},{6,7},{7,0},{8,9},{9,10},{10,1... | collective-permute-start | bytes 688136 | tf_op jit(solution)/shard_map/ppermute | solution.py:216
  68.7 7.2 %collective-permute-start.8 = (bf16[64,1792]{1,0:T(8,128)(2,1)S(1)}, bf16[64,1792]{1,0:T(8,128)(2,1)S(1)}, u32[]{:S(2)}, u32[]{:S(2)}) collective-permute-start(bf16[64,1792]{1,0:T(8,128)(2,1)S(1)} %slice.35), channel_id=1, source_target_pairs={{0,7},{1,0},{2,1},{3,2},{4,3},{5,4},{6,5},{7,6},{8,15},{9,8},{10,9... | collective-permute-start | bytes 688136 | tf_op jit(solution)/shard_map/ppermute | solution.py:217
  90.3 6.7 %collective-permute-start.9 = (bf16[1024,512]{1,0:T(8,128)(2,1)}, bf16[1024,512]{1,0:T(8,128)(2,1)S(1)}, u32[]{:S(2)}, u32[]{:S(2)}) collective-permute-start(bf16[1024,512]{1,0:T(8,128)(2,1)} %get-tuple-element.11), channel_id=1, source_target_pairs={{0,16},{16,0},{1,17},{17,1},{2,18},{18,2},{3,19},{19,3},{4,20},{20... | collective-permute-start | bytes 3145736 | tf_op jit(solution)/shard_map/ppermute | solution.py:229
  91.2 5.8 %collective-permute-start.10 = (f32[2,128]{1,0:T(2,128)S(1)}, f32[2,128]{1,0:T(2,128)S(1)}, u32[]{:S(2)}, u32[]{:S(2)}) collective-permute-start(f32[2,128]{1,0:T(2,128)S(1)} %bitcast.29), channel_id=1, source_target_pairs={{0,8},{8,0},{1,9},{9,1},{2,10},{10,2},{3,11},{11,3},{4,12},{12,4},... | collective-permute-start | bytes 3080 | tf_op jit(solution)/shard_map/ppermute | solution.py:224
  99.0 36.8 %copy-start = (bf16[1024,512]{1,0:T(8,128)(2,1)}, bf16[1024,512]{1,0:T(8,128)(2,1)S(1)}, u32[]{:S(2)}) copy-start(bf16[1024,512]{1,0:T(8,128)(2,1)S(1)} %maximum_convert_fusion.own_ref) | copy-start | bytes 3145732
  99.0 14.4 %collective-permute-start.11 = (bf16[128,1024]{0,1:T(8,128)(2,1)S(1)}, bf16[128,1024]{0,1:T(8,128)(2,1)S(1)}, u32[]{:S(2)}, u32[]{:S(2)}) collective-permute-start(bf16[128,1024]{0,1:T(8,128)(2,1)S(1)} %slice_bitcast_fusion), channel_id=1, source_target_pairs={{0,4},{8,12},{16,20},{24,28},{32,36},{40,44},{48,52},{56,60},{64,6... | collective-permute-start | bytes 786440 | tf_op jit(solution)/shard_map/ppermute | solution.py:236
  108.1 25.8 %collective-permute-start.14 = (bf16[1024,512]{1,0:T(8,128)(2,1)S(1)}, bf16[1024,512]{1,0:T(8,128)(2,1)S(1)}, u32[]{:S(2)}, u32[]{:S(2)}) collective-permute-start(bf16[1024,512]{1,0:T(8,128)(2,1)S(1)} %maximum_convert_fusion.own_ref), channel_id=1, source_target_pairs={{0,64},{64,128},{128,192},{192,0},{1,65},{65,129},{129,193},{193,1... | collective-permute-start | bytes 3145736 | tf_op jit(solution)/shard_map/ppermute | solution.py:241
  108.5 25.5 %collective-permute-start.15 = (bf16[1024,512]{1,0:T(8,128)(2,1)S(1)}, bf16[1024,512]{1,0:T(8,128)(2,1)}, u32[]{:S(2)}, u32[]{:S(2)}) collective-permute-start(bf16[1024,512]{1,0:T(8,128)(2,1)S(1)} %maximum_convert_fusion.own_ref), channel_id=1, source_target_pairs={{0,192},{64,0},{128,64},{192,128},{1,193},{65,1},{129,65},{193,129... | collective-permute-start | bytes 3145736 | tf_op jit(solution)/shard_map/ppermute | solution.py:242
  113.5 6.2 %collective-permute-start.12 = (bf16[128,1024]{0,1:T(8,128)(2,1)S(1)}, bf16[128,1024]{0,1:T(8,128)(2,1)S(1)}, u32[]{:S(2)}, u32[]{:S(2)}) collective-permute-start(bf16[128,1024]{0,1:T(8,128)(2,1)S(1)} %broadcast_select_fusion.2), channel_id=1, source_target_pairs={{0,2},{4,6},{8,10},{12,14},{16,18},{20,22},{24,26},{28,30},{32,34}... | collective-permute-start | bytes 786440 | tf_op jit(solution)/shard_map/ppermute | solution.py:236
  119.7 5.4 %collective-permute-start.13 = (bf16[128,1024]{0,1:T(8,128)(2,1)S(1)}, bf16[128,1024]{0,1:T(8,128)(2,1)S(1)}, u32[]{:S(2)}, u32[]{:S(2)}) collective-permute-start(bf16[128,1024]{0,1:T(8,128)(2,1)S(1)} %broadcast_select_fusion.3), channel_id=1, source_target_pairs={{0,1},{2,3},{4,5},{6,7},{8,9},{10,11},{12,13},{14,15},{16,17},{18,... | collective-permute-start | bytes 786440 | tf_op jit(solution)/shard_map/ppermute | solution.py:236
  135.7 31.1 %all-to-all-start.2 = ((bf16[8,128,1024]{2,1,0:T(8,128)(2,1)}), bf16[8,128,1024]{2,1,0:T(8,128)(2,1)S(1)}, u32[]{:S(2)}, u32[]{:S(2)}) async-start(bf16[8,128,1024]{2,1,0:T(8,128)(2,1)} %broadcast_in_dim.5), calls=%async_computation.2 | async-start | bytes 4194304 | tf_op jit(solution)/shard_map/all_to_all | solution.py:36
  142.1 14.6 %collective-permute-start.16 = (bf16[512,512]{1,0:T(8,128)(2,1)S(1)}, bf16[512,512]{1,0:T(8,128)(2,1)S(1)}, u32[]{:S(2)}, u32[]{:S(2)}) collective-permute-start(bf16[512,512]{1,0:T(8,128)(2,1)S(1)} %slice.30), channel_id=1, source_target_pairs={{0,192},{64,0},{128,64},{192,128},{1,193},{65,1},{129,65},{193,129... | collective-permute-start | bytes 1572872 | tf_op jit(solution)/shard_map/ppermute | solution.py:245
  145.2 15.0 %collective-permute-start.17 = (bf16[512,512]{1,0:T(8,128)(2,1)S(1)}, bf16[512,512]{1,0:T(8,128)(2,1)S(1)}, u32[]{:S(2)}, u32[]{:S(2)}) collective-permute-start(bf16[512,512]{1,0:T(8,128)(2,1)S(1)} %slice.31), channel_id=1, source_target_pairs={{0,64},{64,128},{128,192},{192,0},{1,65},{65,129},{129,193},{193,1... | collective-permute-start | bytes 1572872 | tf_op jit(solution)/shard_map/ppermute | solution.py:246
  176.7 54.3 %all-to-all-start.3 = ((bf16[8,256,1024]{2,1,0:T(8,128)(2,1)}), bf16[8,256,1024]{2,1,0:T(8,128)(2,1)}, u32[]{:S(2)}, u32[]{:S(2)}) async-start(bf16[8,256,1024]{2,1,0:T(8,128)(2,1)} %shard_map.48), calls=%async_computation.3 | async-start | bytes 8388608 | tf_op jit(solution)/shard_map/all_to_all | solution.py:36
  (12 other events, 141.1 us)

commit v4 on v3

v4 whole, which is shorter than its diff:
```python
import jax
import jax.numpy as jnp
from jax import lax
from jax.experimental import pallas as pl
from jax.experimental.pallas import tpu as pltpu
from jax.sharding import Mesh, PartitionSpec as P

AXES = ("y", "xh", "c", "xl", "z")
SIZES = (4, 2, 2, 2, 8)
PLANE = ("y", "xh", "xl")
ROW = ("xh", "c", "xl")
LINE = ("xh", "xl")
TOK = ("y", "xh", "c")
LATENT = ("xl", "z")
YS, CHIPS, CORES, XLO, DEPTH = 4, 8, 2, 2, 8
PEERS = CHIPS * XLO
MATES = 8
SWAP = [(0, 1), (1, 0)]
VMEM = 60 * 1024 * 1024
ORDER = ((0, 0), (-1, 0), (1, 0), (-2, 0), (2, 0), (-3, 0), (3, 0), (4, 0), (4, 1))


def shift(axis, step):
    size = SIZES[AXES.index(axis)]
    return [(i, (i + step) % size) for i in range(size)]


def params(limit=VMEM):
    return pltpu.CompilerParams(vmem_limit_bytes=limit)


def cost(flops, moved):
    return pl.CostEstimate(flops=flops, bytes_accessed=moved, transcendentals=0)


def exchange(block, axes):
    return lax.all_to_all(block, axes, split_axis=0, concat_axis=0, tiled=True)


def spread(block, axes, count):
    return exchange(jnp.broadcast_to(block[None], (count,) + block.shape), axes)


def regroup(weight, lane):
    rows = weight.shape[0]
    group = 4

    def body(in_ref, out_ref):
        for t in range(group):
            for xl in range(XLO):
                for c in range(CORES):
                    at = ((t * CORES + c) * XLO + xl) * lane
                    to = slice(c * lane, (c + 1) * lane)
                    out_ref[t * XLO + xl, :, to] = in_ref[:, at : at + lane]

    wide = group * CORES * XLO * lane
    steps = CHIPS // group
    return pl.pallas_call(
        body,
        out_shape=jax.ShapeDtypeStruct((PEERS, rows, 2 * CORES * lane), weight.dtype),
        grid=(2, steps),
        in_specs=[pl.BlockSpec((rows, wide), lambda h, t: (0, h * steps + t))],
        out_specs=pl.BlockSpec((group * XLO, rows, CORES * lane), lambda h, t: (t, 0, h)),
        cost_estimate=cost(0, 4 * PEERS * rows * 2 * CORES * lane),
        compiler_params=params(),
    )(weight)


def collect(z, pieces):
    strip, depth = pieces[0].shape
    count = len(pieces)

    def body(z_ref, *refs):
        out_ref, sems = refs[-2:]
        copies = []
        for i, (step, cut) in enumerate(ORDER):
            start = lax.rem(z_ref[0] + step + DEPTH, DEPTH) * strip + cut * (strip // 2)
            at = pl.ds(pl.multiple_of(start, strip // 2), refs[i].shape[0])
            copies.append(pltpu.make_async_copy(refs[i], out_ref.at[at], sems.at[i]))
        for copy in copies:
            copy.start()
        for copy in copies:
            copy.wait()

    return pl.pallas_call(
        body,
        out_shape=jax.ShapeDtypeStruct((DEPTH * strip, depth), pieces[0].dtype),
        in_specs=[pl.BlockSpec(memory_space=pltpu.SMEM)]
        + [pl.BlockSpec(memory_space=pl.ANY)] * count,
        out_specs=pl.BlockSpec(memory_space=pl.ANY),
        scratch_shapes=[pltpu.SemaphoreType.DMA((count,))],
        cost_estimate=cost(0, 4 * DEPTH * strip * depth),
        compiler_params=params(16 * 1024 * 1024),
    )(z, *pieces)


def encode(core, batch, weight, lane):
    total, depth = batch.shape
    _, rows, cols = weight.shape
    wide = XLO * cols
    chunk = total // 4

    def body(core_ref, batch_ref, weight_ref, keep_ref, give_ref, grid, sems):
        slabs = [
            [
                pltpu.make_async_copy(
                    weight_ref.at[t * XLO + xl],
                    grid.at[xl, pl.ds(t * rows, rows)],
                    sems.at[t * XLO + xl],
                )
                for t in range(CHIPS)
            ]
            for xl in range(XLO)
        ]
        xl, i = pl.program_id(0), pl.program_id(1)

        @pl.when((xl == 0) & (i == 0))
        def _():
            for copy in slabs[0] + slabs[1]:
                copy.start()
            for copy in slabs[0]:
                copy.wait()

        @pl.when((xl == 1) & (i == 0))
        def _():
            for copy in slabs[1]:
                copy.wait()

        at = pl.ds(pl.multiple_of(i * chunk, chunk), chunk)
        out = jnp.dot(batch_ref[at], grid[xl], preferred_element_type=jnp.float32)
        for h in range(2):
            a = out[:, 2 * h * lane : (2 * h + 1) * lane]
            b = out[:, (2 * h + 1) * lane : (2 * h + 2) * lane]
            keep_ref[:, h * lane : (h + 1) * lane] = jnp.where(core_ref[0] == 0, a, b)
            give_ref[:, h * lane : (h + 1) * lane] = jnp.where(core_ref[0] == 0, b, a)

    mine = wide // CORES
    block = pl.BlockSpec((chunk, 2 * lane), lambda xl, i: (i, xl))
    return pl.pallas_call(
        body,
        out_shape=(
            jax.ShapeDtypeStruct((total, mine), jnp.float32),
            jax.ShapeDtypeStruct((total, mine), jnp.float32),
        ),
        grid=(XLO, total // chunk),
        in_specs=[
            pl.BlockSpec(memory_space=pltpu.SMEM),
            pl.BlockSpec(memory_space=pltpu.VMEM),
            pl.BlockSpec(memory_space=pl.ANY),
        ],
        out_specs=(block, block),
        scratch_shapes=[
            pltpu.VMEM((XLO, CHIPS * rows, cols), jnp.bfloat16),
            pltpu.SemaphoreType.DMA((PEERS,)),
        ],
        cost_estimate=cost(2 * total * depth * wide, 2 * depth * (total + wide) + 8 * total * mine),
        compiler_params=params(58 * 1024 * 1024),
    )(core, batch, weight)


def finish(sums, other, bias):
    total, wide = sums.shape
    lane = wide // (2 * XLO)
    half = total // 2
    chunk = half // 2

    def body(low_sums, high_sums, low_other, high_other, bias_ref, low_ref, high_ref, *turned):
        refs = ((low_sums, low_other, low_ref), (high_sums, high_other, high_ref))
        for (sums_ref, other_ref, act_ref), turned_ref in zip(refs, turned):
            act = jnp.maximum(sums_ref[...] + other_ref[...] + bias_ref[...], 0.0)
            act_ref[...] = act.astype(jnp.bfloat16)
            turned_ref[...] = act[:, :lane].T.astype(jnp.bfloat16)

    steps = half // chunk
    low = pl.BlockSpec((chunk, wide), lambda i: (i, 0))
    high = pl.BlockSpec((chunk, wide), lambda i: (i + steps, 0))
    turned = pl.BlockSpec((lane, chunk), lambda i: (0, i))
    return pl.pallas_call(
        body,
        out_shape=(jax.ShapeDtypeStruct((half, wide), jnp.bfloat16),) * 2
        + (jax.ShapeDtypeStruct((lane, half), jnp.bfloat16),) * 2,
        grid=(steps,),
        in_specs=[low, high, low, high, pl.BlockSpec((1, wide), lambda i: (0, 0))],
        out_specs=(low, low, turned, turned),
        cost_estimate=cost(0, 10 * total * wide),
        compiler_params=params(8 * 1024 * 1024),
    )(sums, sums, other, other, bias.reshape(1, wide))


def assemble(here, parts, size):
    strip, total = parts[0].shape
    order = (0, -1, 1, 2)

    def body(here_ref, *refs):
        out_ref, sems = refs[-2:]
        copies = []
        for i, step in enumerate(order):
            slot = lax.rem(here_ref[0] + step + size, size)
            copies.append(pltpu.make_async_copy(refs[i], out_ref.at[slot], sems.at[i]))
        for copy in copies:
            copy.start()
        for copy in copies:
            copy.wait()

    return pl.pallas_call(
        body,
        out_shape=jax.ShapeDtypeStruct((size, strip, total), parts[0].dtype),
        in_specs=[pl.BlockSpec(memory_space=pltpu.SMEM)]
        + [pl.BlockSpec(memory_space=pl.ANY)] * len(order),
        out_specs=pl.BlockSpec(memory_space=pl.ANY),
        scratch_shapes=[pltpu.SemaphoreType.DMA((len(order),))],
        cost_estimate=cost(0, 4 * size * strip * total),
        compiler_params=params(16 * 1024 * 1024),
    )(here, *parts)


def gram(core, mine, theirs, acts):
    _, strip, total = mine.shape
    wide = acts[0].shape[1]
    lane = wide // (2 * XLO)
    height = XLO * strip
    cut = total // 2

    def body(core_ref, mine_ref, theirs_ref, *refs):
        out_ref = refs[-1]

        def emit(panel_ref):
            rows = panel_ref[...].reshape(height, total)
            for r in range(YS):
                low, high = refs[2 * r][...], refs[2 * r + 1][...]
                out = jnp.dot(rows[:, :cut], low, preferred_element_type=jnp.float32)
                out += jnp.dot(rows[:, cut:], high, preferred_element_type=jnp.float32)
                out = (out * (1.0 / total)).astype(jnp.bfloat16)
                for xl in range(XLO):
                    for h in range(2):
                        at = (xl * 2 + h) * lane
                        out_ref[0, xl, 2 * r + h] = out[:, at : at + lane]

        pl.when(pl.program_id(0) == 0)(lambda: emit(mine_ref))
        pl.when(pl.program_id(0) == 1)(lambda: emit(theirs_ref))

    def whole(a):
        return pl.BlockSpec(a.shape, lambda k, t, core: (0, 0))

    strips = (XLO, strip, total)
    out = pl.pallas_call(
        body,
        out_shape=jax.ShapeDtypeStruct((2 * CORES, XLO, 2 * YS, height, lane), jnp.bfloat16),
        grid_spec=pltpu.PrefetchScalarGridSpec(
            num_scalar_prefetch=1,
            grid=(CORES, 2),
            in_specs=[
                pl.BlockSpec(strips, lambda k, t, core: (jnp.where(k == 0, t, 1), 0, 0)),
                pl.BlockSpec(strips, lambda k, t, core: (jnp.where(k == 0, 0, t), 0, 0)),
            ]
            + [whole(a) for a in acts],
            out_specs=pl.BlockSpec(
                (1, XLO, 2 * YS, height, lane),
                lambda k, t, core: (t * CORES + jnp.where(k == 0, core[0], 1 - core[0]), 0, 0, 0, 0),
            ),
        ),
        cost_estimate=cost(
            2 * 2 * CORES * height * total * YS * wide,
            2 * (MATES * strip * total + YS * total * wide + MATES * height * 2 * YS * lane),
        ),
        compiler_params=params(),
    )(core, mine, theirs, *acts)
    return out.reshape(MATES, 2 * YS, height, lane)


def place(ys, received):
    _, _, height, lane = received.shape
    slab = MATES * 2 * YS * lane

    def body(ys_ref, in_ref, out_ref):
        for s in range(MATES):
            out_ref[:, s * lane : (s + 1) * lane] = in_ref[s, 0]

    return pl.pallas_call(
        body,
        out_shape=jax.ShapeDtypeStruct((height, slab), jnp.bfloat16),
        grid_spec=pltpu.PrefetchScalarGridSpec(
            num_scalar_prefetch=1,
            grid=(YS, 2),
            in_specs=[
                pl.BlockSpec((MATES, 1, height, lane), lambda r, h, ys: (0, 2 * r + h, 0, 0))
            ],
            out_specs=pl.BlockSpec((height, MATES * lane), lambda r, h, ys: (0, h * YS + ys[r])),
        ),
        cost_estimate=cost(0, 4 * height * slab),
        compiler_params=params(8 * 1024 * 1024),
    )(ys, received)


def per_device(tokens, dec_bias, enc_weight, enc_bias):
    own, width = tokens.shape
    rows, slab = enc_weight.shape
    lane = slab // (2 * CHIPS * CORES * XLO)
    total = own * CHIPS * CORES
    core = lax.axis_index("c")
    xlo = lax.axis_index("xl")
    y = lax.axis_index("y")
    chip = y * 2 + lax.axis_index("xh")
    z = lax.axis_index("z")
    which = jnp.reshape(core, (1,)).astype(jnp.int32)
    ys = lax.rem(jnp.stack([y, y + 3, y + 1, y + 2]), YS).astype(jnp.int32)

    centered = (tokens.astype(jnp.float32) - dec_bias).astype(jnp.bfloat16)
    halves = centered.reshape(own, CHIPS, CORES, rows).transpose(2, 0, 1, 3)
    halves = halves.reshape(CORES, own, CHIPS * rows)
    keep = jnp.where(core == 0, halves[0], halves[1])
    give = jnp.where(core == 0, halves[1], halves[0])
    got = lax.ppermute(give, "c", SWAP)
    mine = jnp.where(core == xlo, keep, got)
    part = own // DEPTH
    mine = lax.dynamic_slice_in_dim(mine, z * part, part, 0)
    near = spread(mine, PLANE, PEERS).reshape(total // DEPTH, CHIPS * rows)
    pieces = [near]
    low = high = near
    for _ in range(DEPTH // 2 - 1):
        low = lax.ppermute(low, "z", shift("z", 1))
        high = lax.ppermute(high, "z", shift("z", -1))
        pieces += [low, high]
    cut = near.shape[0] // 2
    pieces.append(lax.ppermute(low[:cut], "z", shift("z", 1)))
    pieces.append(lax.ppermute(high[cut:], "z", shift("z", -1)))
    batch = collect(jnp.reshape(z, (1,)).astype(jnp.int32), pieces)

    biases = enc_bias.reshape(2, CHIPS, CORES, XLO, lane)
    biases = lax.dynamic_index_in_dim(biases, chip, 1, keepdims=False)
    biases = lax.dynamic_index_in_dim(biases, core, 1, keepdims=False)
    bias_keep = lax.dynamic_index_in_dim(biases, xlo, 1, keepdims=False)
    bias_give = lax.dynamic_index_in_dim(biases, 1 - xlo, 1, keepdims=False)
    bias_got = lax.ppermute(bias_give, "xl", SWAP)
    bias = jnp.where(xlo == 0, jnp.stack([bias_keep, bias_got]), jnp.stack([bias_got, bias_keep]))

    weight = exchange(regroup(enc_weight, lane), PLANE)
    sums, sent = encode(which, batch, weight, lane)
    other = lax.ppermute(sent, "c", SWAP)
    low, high, *turned = finish(sums, other, bias)
    held = jnp.concatenate(turned, axis=1)

    def reach(held, span):
        moved = lax.ppermute(held, "z", [(i, i + span) for i in range(0, DEPTH, 2 * span)])
        return jnp.where(lax.rem(z, 2 * span) == span, moved, held)

    size = MATES // CORES
    forth = [(i, (i + 1) % size) for i in range(size)]
    back = [(i, (i - 1) % size) for i in range(size)]
    held = reach(held, 4)
    below_high = lax.ppermute(high, "y", shift("y", 1))
    above_low = lax.ppermute(low, "y", shift("y", -1))
    held, below_high, above_low = lax.optimization_barrier((held, below_high, above_low))
    held = reach(reach(held, 2), 1)
    below_low = lax.ppermute(low, "y", shift("y", 1))
    above_high = lax.ppermute(high, "y", shift("y", -1))
    held, below_low, above_high = lax.optimization_barrier((held, below_low, above_high))
    left = lax.ppermute(held, LINE, forth)
    right = lax.ppermute(held, LINE, back)
    far_low = lax.ppermute(above_low, "y", shift("y", -1))
    far_high = lax.ppermute(below_high, "y", shift("y", 1))
    right, far_low, far_high = lax.optimization_barrier((right, far_low, far_high))
    over = lax.ppermute(right, LINE, back)
    here = jnp.reshape(lax.axis_index("xh") * XLO + xlo, (1,)).astype(jnp.int32)
    panel = assemble(here, (held, left, right, over), size)
    theirs = lax.ppermute(panel, "c", SWAP)

    acts = (low, high, below_low, below_high, above_low, above_high, far_low, far_high)
    sent = gram(which, panel, theirs, acts)
    return place(ys, exchange(sent, ROW))


def solution(mesh):
    fine = Mesh(mesh.devices.reshape(SIZES), AXES)
    return jax.shard_map(
        per_device,
        mesh=fine,
        in_specs=(P(TOK, None), P(), P(TOK, LATENT), P(LATENT)),
        out_specs=P(TOK, LATENT),
        check_vma=False,
    )
```

time: 241 us -> 226 us (0.938)
  waiting for transfers between devices: 125 us -> 110 us
  starting transfers between devices: 64.4 us -> 68.9 us
  other arithmetic: 4.49 us -> 1.32 us
    ppermute x8 -> x14, starting transfers between devices: 18.5 us -> 28.8 us  [the longest x3 13.1 us: reach(): lax.ppermute(held, 'z', [(i, i + span) for i in range(0, DEPTH, 2 * span)])]
    ppermute x8 -> x14, waiting for transfers between devices: 33.7 us -> 25.7 us  [the longest x3 6.92 us: reach(): lax.ppermute(held, 'z', [(i, i + span) for i in range(0, DEPTH, 2 * span)])]
    all_to_all x4 -> x3, starting transfers between devices: 25.8 us -> 20.1 us  [exchange(): return lax.all_to_all(block, axes, split_axis=0, concat_axis=0, tiled=True)]
    pallas_call x1, Pallas kernels: 10.1 us -> 4.72 us  [regroup(): pl.pallas_call(body, out_shape=jax.ShapeDtypeStruct((PEERS, rows, 2 * COR...]
    all_to_all x4 -> x3, waiting for transfers between devices: 58.5 us -> 53.3 us  [exchange(): return lax.all_to_all(block, axes, split_axis=0, concat_axis=0, tiled=True)]
    pallas_call x1 -> x4, Pallas kernels: 8.53 us -> 12.1 us  [the longest x1 8.73 us: gram(): pl.pallas_call(body, out_shape=jax.ShapeDtypeStruct((2 * CORES, XLO, 2 *...]
  transfers between devices with their start and end apart: 22 -> 27, of which waited for: 15 -> 16; matrix products, arithmetic and copies ran while one was open for 1% -> 1% of each run, Pallas kernels for 4% -> 3%
where the time goes in v4:
time: 226 us; the launch traced here: 223 us
  waiting for transfers between devices  110 us (49%)
  starting transfers between devices  68.9 us (30%)
  Pallas kernels  34.9 us (15%)
  local copies, waits for them, and re-layouts  7.47 us (3%)
    all_to_all x3, waiting for transfers between devices, exchange(): return lax.all_to_all(block, axes, split_axis=0, concat_axis=0, tiled=True)  53.3 us
    ppermute x3, waiting for transfers between devices, per_device(): low = lax.ppermute(low, 'z', shift('z', 1))  24.7 us
    all_to_all x3, starting transfers between devices, exchange(): return lax.all_to_all(block, axes, split_axis=0, concat_axis=0, tiled=True)  20.1 us
    ppermute x3, starting transfers between devices, reach(): lax.ppermute(held, 'z', [(i, i + span) for i in range(0, DEPTH, 2 * span)])  13.1 us
    ppermute x3, starting transfers between devices, per_device(): high = lax.ppermute(high, 'z', shift('z', -1))  10.5 us
    pallas_call x1, Pallas kernels, encode(): pl.pallas_call(body, out_shape=(jax.ShapeDtypeStruct((total, mine), jnp.f...  10.4 us
    pallas_call x1, Pallas kernels, gram(): pl.pallas_call(body, out_shape=jax.ShapeDtypeStruct((2 * CORES, XLO, 2 *...  8.73 us
    pallas_call x1, Pallas kernels, place(): pl.pallas_call(body, out_shape=jax.ShapeDtypeStruct((height, slab), jnp.b...  7.58 us
  transfers between devices with their start and end apart: 27, of which 16 were waited for; matrix products, arithmetic and copies ran while one was open for 1% of the time, Pallas kernels for 3%

profile of v4, /device:TPU:2, one launch (start us, length us, event | category | flops | bytes accessed | tf_op | source)
XLA Modules:
  0.0 223.3 jit_solution(13769122544562339946)
XLA Ops:
  4.7 7.5 %all-to-all-start = ((bf16[16,8,1792]{2,1,0:T(8,128)(2,1)}), bf16[16,8,1792]{2,1,0:T(8,128)(2,1)S(1)}, u32[]{:S(2)}, u32[]{:S(2)}) async-start(bf16[16,8,1792]{2,1,0:T(8,128)(2,1)} %broadcast_in_dim.2), calls=%async_computation | async-start | bytes 917504 | tf_op jit(solution)/shard_map/all_to_all | solution.py:37
  12.2 4.7 %shard_map.47 = bf16[16,224,512]{2,1,0:T(8,128)(2,1)} custom-call(bf16[224,8192]{1,0:T(8,128)(2,1)} %in_ref.1), custom_call_target="tpu_custom_call" | custom-call | bytes 7340032 | tf_op jit(solution)/shard_map/pallas_call | solution.py:58
  16.9 5.0 %all-to-all-done = bf16[16,8,1792]{2,1,0:T(8,128)(2,1)S(1)} async-done(((bf16[16,8,1792]{2,1,0:T(8,128)(2,1)}), bf16[16,8,1792]{2,1,0:T(8,128)(2,1)S(1)}, u32[]{:S(2)}, u32[]{:S(2)}) %all-to-all-start) | async-done | bytes 458784 | tf_op jit(solution)/shard_map/all_to_all | solution.py:37
  21.9 5.7 %all-to-all-start.1 = ((bf16[16,224,512]{2,1,0:T(8,128)(2,1)}), bf16[16,224,512]{2,1,0:T(8,128)(2,1)}, u32[]{:S(2)}, u32[]{:S(2)}) async-start(bf16[16,224,512]{2,1,0:T(8,128)(2,1)} %shard_map.47), calls=%async_computation.1 | async-start | bytes 7340032 | tf_op jit(solution)/shard_map/all_to_all | solution.py:37
  29.6 4.0 %collective-permute-start.2 = (bf16[128,1792]{1,0:T(8,128)(2,1)S(1)}, bf16[128,1792]{1,0:T(8,128)(2,1)S(1)}, u32[]{:S(2)}, u32[]{:S(2)}) collective-permute-start(bf16[128,1792]{1,0:T(8,128)(2,1)S(1)} %bitcast.22), channel_id=1, source_target_pairs={{0,7},{1,0},{2,1},{3,2},{4,3},{5,4},{6,5},{7,6},{8,15},{9,8},{10,9... | collective-permute-start | bytes 1376264 | tf_op jit(solution)/shard_map/ppermute | solution.py:322
  33.6 9.0 %collective-permute-done.1.refs_1_ = bf16[128,1792]{1,0:T(8,128)(2,1)S(1)} collective-permute-done((bf16[128,1792]{1,0:T(8,128)(2,1)S(1)}, bf16[128,1792]{1,0:T(8,128)(2,1)S(1)}, u32[]{:S(2)}, u32[]{:S(2)}) %collective-permute-start.1) | collective-permute-done | bytes 458784 | tf_op jit(solution)/shard_map/ppermute | solution.py:321
  42.6 3.2 %collective-permute-start.4 = (bf16[128,1792]{1,0:T(8,128)(2,1)S(1)}, bf16[128,1792]{1,0:T(8,128)(2,1)S(1)}, u32[]{:S(2)}, u32[]{:S(2)}) collective-permute-start(bf16[128,1792]{1,0:T(8,128)(2,1)S(1)} %collective-permute-done.2.refs_2_), channel_id=1, source_target_pairs={{0,7},{1,0},{2,1},{3,2},{4,3},{5,4},{6,5},{7,6},{8,15},{9,8},{10,9... | collective-permute-start | bytes 1376264 | tf_op jit(solution)/shard_map/ppermute | solution.py:322
  45.8 8.3 %collective-permute-done.3.refs_3_ = bf16[128,1792]{1,0:T(8,128)(2,1)S(1)} collective-permute-done((bf16[128,1792]{1,0:T(8,128)(2,1)S(1)}, bf16[128,1792]{1,0:T(8,128)(2,1)S(1)}, u32[]{:S(2)}, u32[]{:S(2)}) %collective-permute-start.3) | collective-permute-done | bytes 458784 | tf_op jit(solution)/shard_map/ppermute | solution.py:321
  54.1 3.2 %collective-permute-start.6 = (bf16[128,1792]{1,0:T(8,128)(2,1)S(1)}, bf16[128,1792]{1,0:T(8,128)(2,1)S(1)}, u32[]{:S(2)}, u32[]{:S(2)}) collective-permute-start(bf16[128,1792]{1,0:T(8,128)(2,1)S(1)} %collective-permute-done.4.refs_4_), channel_id=1, source_target_pairs={{0,7},{1,0},{2,1},{3,2},{4,3},{5,4},{6,5},{7,6},{8,15},{9,8},{10,9... | collective-permute-start | bytes 1376264 | tf_op jit(solution)/shard_map/ppermute | solution.py:322
  57.3 7.4 %collective-permute-done.5.refs_5_ = bf16[128,1792]{1,0:T(8,128)(2,1)S(1)} collective-permute-done((bf16[128,1792]{1,0:T(8,128)(2,1)S(1)}, bf16[128,1792]{1,0:T(8,128)(2,1)S(1)}, u32[]{:S(2)}, u32[]{:S(2)}) %collective-permute-start.5) | collective-permute-done | bytes 458784 | tf_op jit(solution)/shard_map/ppermute | solution.py:321
  64.9 3.3 %collective-permute-start.8 = (bf16[64,1792]{1,0:T(8,128)(2,1)S(1)}, bf16[64,1792]{1,0:T(8,128)(2,1)S(1)}, u32[]{:S(2)}, u32[]{:S(2)}) collective-permute-start(bf16[64,1792]{1,0:T(8,128)(2,1)S(1)} %slice.23), channel_id=1, source_target_pairs={{0,7},{1,0},{2,1},{3,2},{4,3},{5,4},{6,5},{7,6},{8,15},{9,8},{10,9... | collective-permute-start | bytes 688136 | tf_op jit(solution)/shard_map/ppermute | solution.py:326
  68.2 3.9 %collective-permute-done.7.refs_7_ = bf16[64,1792]{1,0:T(8,128)(2,1)S(1)} collective-permute-done((bf16[64,1792]{1,0:T(8,128)(2,1)S(1)}, bf16[64,1792]{1,0:T(8,128)(2,1)S(1)}, u32[]{:S(2)}, u32[]{:S(2)}) %collective-permute-start.7) | collective-permute-done | bytes 229408 | tf_op jit(solution)/shard_map/ppermute | solution.py:325
  76.7 10.4 %shard_map.48 = (f32[1024,512]{1,0:T(8,128)}, f32[1024,512]{1,0:T(8,128)}) custom-call(s32[1]{0:T(128)} %bitcast.4.core_ref, bf16[1024,1792]{1,0:T(8,128)(2,1)} %copy-done.1, bf16[16,224,512]{2,1,0:T(8,128)(2,1)} %all-to-all-done.1.weight_ref), custom_call_target="tpu_custom_call" | custom-call | flops 3758096384 | bytes 11534336 | tf_op jit(solution)/shard_map/pallas_call | solution.py:139
  88.0 4.2 %collective-permute-start.10 = (f32[2,128]{1,0:T(2,128)S(1)}, f32[2,128]{1,0:T(2,128)S(1)}, u32[]{:S(2)}, u32[]{:S(2)}) collective-permute-start(f32[2,128]{1,0:T(2,128)S(1)} %bitcast.28), channel_id=1, source_target_pairs={{0,8},{8,0},{1,9},{9,1},{2,10},{10,2},{3,11},{11,3},{4,12},{12,4},... | collective-permute-start | bytes 3080 | tf_op jit(solution)/shard_map/ppermute | solution.py:334
  99.3 9.1 %collective-permute-start.11 = (bf16[128,1024]{1,0:T(8,128)(2,1)S(1)}, bf16[128,1024]{1,0:T(8,128)(2,1)S(1)}, u32[]{:S(2)}, u32[]{:S(2)}) collective-permute-start(bf16[128,1024]{1,0:T(8,128)(2,1)S(1)} %constant_dynamic-update-slice_fusion), channel_id=1, source_target_pairs={{0,4},{8,12},{16,20},{24,28},{32,36},{40,44},{48,52},{56,60},{64,6... | collective-permute-start | bytes 786440 | tf_op jit(solution)/shard_map/ppermute | solution.py:344
  108.4 4.7 %collective-permute-done.11 = bf16[128,1024]{1,0:T(8,128)(2,1)S(1)} collective-permute-done((bf16[128,1024]{1,0:T(8,128)(2,1)S(1)}, bf16[128,1024]{1,0:T(8,128)(2,1)S(1)}, u32[]{:S(2)}, u32[]{:S(2)}) %collective-permute-start.11) | collective-permute-done | bytes 262176 | tf_op jit(solution)/shard_map/ppermute | solution.py:344
  122.1 3.2 %collective-permute-start.20 = (bf16[512,512]{1,0:T(8,128)(2,1)S(1)}, bf16[512,512]{1,0:T(8,128)(2,1)}, u32[]{:S(2)}, u32[]{:S(2)}) collective-permute-start(bf16[512,512]{1,0:T(8,128)(2,1)S(1)} %collective-permute-done.13.refs_4_), channel_id=1, source_target_pairs={{0,192},{64,0},{128,64},{192,128},{1,193},{65,1},{129,65},{193,129... | collective-permute-start | bytes 1572872 | tf_op jit(solution)/shard_map/ppermute | solution.py:360
  126.0 6.1 %collective-permute-done.16.refs_2_ = bf16[512,512]{1,0:T(8,128)(2,1)S(1)} collective-permute-done((bf16[512,512]{1,0:T(8,128)(2,1)S(1)}, bf16[512,512]{1,0:T(8,128)(2,1)S(1)}, u32[]{:S(2)}, u32[]{:S(2)}) %collective-permute-start.16) | collective-permute-done | bytes 524320 | tf_op jit(solution)/shard_map/ppermute | solution.py:355
  134.6 5.3 %collective-permute-done.20.refs_6_ = bf16[512,512]{1,0:T(8,128)(2,1)} collective-permute-done((bf16[512,512]{1,0:T(8,128)(2,1)S(1)}, bf16[512,512]{1,0:T(8,128)(2,1)}, u32[]{:S(2)}, u32[]{:S(2)}) %collective-permute-start.20) | collective-permute-done | bytes 524320 | tf_op jit(solution)/shard_map/ppermute | solution.py:360
  143.9 3.9 %collective-permute-done.22.refs_3_ = bf16[128,1024]{1,0:T(8,128)(2,1)S(1)} collective-permute-done((bf16[128,1024]{1,0:T(8,128)(2,1)S(1)}, bf16[128,1024]{1,0:T(8,128)(2,1)S(1)}, u32[]{:S(2)}, u32[]{:S(2)}) %collective-permute-start.22) | collective-permute-done | bytes 262176 | tf_op jit(solution)/shard_map/ppermute | solution.py:363
  151.7 8.7 %shard_map.51 = bf16[4,2,8,256,128]{4,3,2,1,0:T(8,128)(2,1)} custom-call(s32[1]{0:T(128)} %bitcast.4.core_ref, bf16[4,128,1024]{2,1,0:T(8,128)(2,1)} %copy-done.2, bf16[4,128,1024]{2,1,0:T(8,128)(2,1)} %copy-done.5, bf16[512,512]{1,0:T(8,128)(2,1)} %copy-done.3, bf16[512,512]{1,0:T(8,128)(2,1)} %copy-done.4, bf16[512,512]{1,0:T(8,128)(2,1)} %copy-done.8, ...), custom_call_target="tpu_custom_call" | custom-call | flops 4294967296 | bytes 10485760 | tf_op jit(solution)/shard_map/pallas_call | solution.py:246
  160.4 6.9 %all-to-all-start.2 = ((bf16[8,8,256,128]{3,2,1,0:T(8,128)(2,1)}), bf16[8,8,256,128]{3,2,1,0:T(8,128)(2,1)}, u32[]{:S(2)}, u32[]{:S(2)}) async-start(bf16[8,8,256,128]{3,2,1,0:T(8,128)(2,1)} %bitcast.25), calls=%async_computation.2 | async-start | bytes 8388608 | tf_op jit(solution)/shard_map/all_to_all | solution.py:37
  167.4 48.3 %all-to-all-done.2.in_ref = bf16[8,8,256,128]{3,2,1,0:T(8,128)(2,1)} async-done(((bf16[8,8,256,128]{3,2,1,0:T(8,128)(2,1)}), bf16[8,8,256,128]{3,2,1,0:T(8,128)(2,1)}, u32[]{:S(2)}, u32[]{:S(2)}) %all-to-all-start.2) | async-done | bytes 4194336 | tf_op jit(solution)/shard_map/all_to_all | solution.py:37
  215.7 7.6 %shard_map.52 = bf16[256,8192]{1,0:T(8,128)(2,1)} custom-call(s32[4]{0:T(128)S(1)} %compare_select_fusion.ys_ref, bf16[8,8,256,128]{3,2,1,0:T(8,128)(2,1)} %all-to-all-done.2.in_ref), custom_call_target="tpu_custom_call" | custom-call | bytes 8388608 | tf_op jit(solution)/shard_map/pallas_call | solution.py:279
  (73 shorter events, 39.2 us)
Async XLA Ops:
  4.7 17.2 %all-to-all-start = ((bf16[16,8,1792]{2,1,0:T(8,128)(2,1)}), bf16[16,8,1792]{2,1,0:T(8,128)(2,1)S(1)}, u32[]{:S(2)}, u32[]{:S(2)}) async-start(bf16[16,8,1792]{2,1,0:T(8,128)(2,1)} %broadcast_in_dim.2), calls=%async_computation | async-start | bytes 917504 | tf_op jit(solution)/shard_map/all_to_all | solution.py:37
  21.9 54.8 %all-to-all-start.1 = ((bf16[16,224,512]{2,1,0:T(8,128)(2,1)}), bf16[16,224,512]{2,1,0:T(8,128)(2,1)}, u32[]{:S(2)}, u32[]{:S(2)}) async-start(bf16[16,224,512]{2,1,0:T(8,128)(2,1)} %shard_map.47), calls=%async_computation.1 | async-start | bytes 7340032 | tf_op jit(solution)/shard_map/all_to_all | solution.py:37
  27.6 14.9 %collective-permute-start.1 = (bf16[128,1792]{1,0:T(8,128)(2,1)S(1)}, bf16[128,1792]{1,0:T(8,128)(2,1)S(1)}, u32[]{:S(2)}, u32[]{:S(2)}) collective-permute-start(bf16[128,1792]{1,0:T(8,128)(2,1)S(1)} %bitcast.21), channel_id=1, source_target_pairs={{0,1},{1,2},{2,3},{3,4},{4,5},{5,6},{6,7},{7,0},{8,9},{9,10},{10,1... | collective-permute-start | bytes 1376264 | tf_op jit(solution)/shard_map/ppermute | solution.py:321
  29.6 13.0 %collective-permute-start.2 = (bf16[128,1792]{1,0:T(8,128)(2,1)S(1)}, bf16[128,1792]{1,0:T(8,128)(2,1)S(1)}, u32[]{:S(2)}, u32[]{:S(2)}) collective-permute-start(bf16[128,1792]{1,0:T(8,128)(2,1)S(1)} %bitcast.22), channel_id=1, source_target_pairs={{0,7},{1,0},{2,1},{3,2},{4,3},{5,4},{6,5},{7,6},{8,15},{9,8},{10,9... | collective-permute-start | bytes 1376264 | tf_op jit(solution)/shard_map/ppermute | solution.py:322
  42.6 11.5 %collective-permute-start.3 = (bf16[128,1792]{1,0:T(8,128)(2,1)S(1)}, bf16[128,1792]{1,0:T(8,128)(2,1)S(1)}, u32[]{:S(2)}, u32[]{:S(2)}) collective-permute-start(bf16[128,1792]{1,0:T(8,128)(2,1)S(1)} %collective-permute-done.1.refs_1_), channel_id=1, source_target_pairs={{0,1},{1,2},{2,3},{3,4},{4,5},{5,6},{6,7},{7,0},{8,9},{9,10},{10,1... | collective-permute-start | bytes 1376264 | tf_op jit(solution)/shard_map/ppermute | solution.py:321
  42.6 11.5 %collective-permute-start.4 = (bf16[128,1792]{1,0:T(8,128)(2,1)S(1)}, bf16[128,1792]{1,0:T(8,128)(2,1)S(1)}, u32[]{:S(2)}, u32[]{:S(2)}) collective-permute-start(bf16[128,1792]{1,0:T(8,128)(2,1)S(1)} %collective-permute-done.2.refs_2_), channel_id=1, source_target_pairs={{0,7},{1,0},{2,1},{3,2},{4,3},{5,4},{6,5},{7,6},{8,15},{9,8},{10,9... | collective-permute-start | bytes 1376264 | tf_op jit(solution)/shard_map/ppermute | solution.py:322
  54.1 10.7 %collective-permute-start.5 = (bf16[128,1792]{1,0:T(8,128)(2,1)S(1)}, bf16[128,1792]{1,0:T(8,128)(2,1)S(1)}, u32[]{:S(2)}, u32[]{:S(2)}) collective-permute-start(bf16[128,1792]{1,0:T(8,128)(2,1)S(1)} %collective-permute-done.3.refs_3_), channel_id=1, source_target_pairs={{0,1},{1,2},{2,3},{3,4},{4,5},{5,6},{6,7},{7,0},{8,9},{9,10},{10,1... | collective-permute-start | bytes 1376264 | tf_op jit(solution)/shard_map/ppermute | solution.py:321
  54.1 10.8 %collective-permute-start.6 = (bf16[128,1792]{1,0:T(8,128)(2,1)S(1)}, bf16[128,1792]{1,0:T(8,128)(2,1)S(1)}, u32[]{:S(2)}, u32[]{:S(2)}) collective-permute-start(bf16[128,1792]{1,0:T(8,128)(2,1)S(1)} %collective-permute-done.4.refs_4_), channel_id=1, source_target_pairs={{0,7},{1,0},{2,1},{3,2},{4,3},{5,4},{6,5},{7,6},{8,15},{9,8},{10,9... | collective-permute-start | bytes 1376264 | tf_op jit(solution)/shard_map/ppermute | solution.py:322
  64.8 7.3 %collective-permute-start.7 = (bf16[64,1792]{1,0:T(8,128)(2,1)S(1)}, bf16[64,1792]{1,0:T(8,128)(2,1)S(1)}, u32[]{:S(2)}, u32[]{:S(2)}) collective-permute-start(bf16[64,1792]{1,0:T(8,128)(2,1)S(1)} %slice.22), channel_id=1, source_target_pairs={{0,1},{1,2},{2,3},{3,4},{4,5},{5,6},{6,7},{7,0},{8,9},{9,10},{10,1... | collective-permute-start | bytes 688136 | tf_op jit(solution)/shard_map/ppermute | solution.py:325
  64.9 7.2 %collective-permute-start.8 = (bf16[64,1792]{1,0:T(8,128)(2,1)S(1)}, bf16[64,1792]{1,0:T(8,128)(2,1)S(1)}, u32[]{:S(2)}, u32[]{:S(2)}) collective-permute-start(bf16[64,1792]{1,0:T(8,128)(2,1)S(1)} %slice.23), channel_id=1, source_target_pairs={{0,7},{1,0},{2,1},{3,2},{4,3},{5,4},{6,5},{7,6},{8,15},{9,8},{10,9... | collective-permute-start | bytes 688136 | tf_op jit(solution)/shard_map/ppermute | solution.py:326
  87.1 6.7 %collective-permute-start.9 = (f32[1024,512]{1,0:T(8,128)}, f32[1024,512]{1,0:T(8,128)S(1)}, u32[]{:S(2)}, u32[]{:S(2)}) collective-permute-start(f32[1024,512]{1,0:T(8,128)} %get-tuple-element.21), channel_id=1, source_target_pairs={{0,16},{16,0},{1,17},{17,1},{2,18},{18,2},{3,19},{19,3},{4,20},{20... | collective-permute-start | bytes 6291464 | tf_op jit(solution)/shard_map/ppermute | solution.py:339
  88.0 5.8 %collective-permute-start.10 = (f32[2,128]{1,0:T(2,128)S(1)}, f32[2,128]{1,0:T(2,128)S(1)}, u32[]{:S(2)}, u32[]{:S(2)}) collective-permute-start(f32[2,128]{1,0:T(2,128)S(1)} %bitcast.28), channel_id=1, source_target_pairs={{0,8},{8,0},{1,9},{9,1},{2,10},{10,2},{3,11},{11,3},{4,12},{12,4},... | collective-permute-start | bytes 3080 | tf_op jit(solution)/shard_map/ppermute | solution.py:334
  96.0 17.2 %collective-permute-start.12 = (bf16[512,512]{1,0:T(8,128)(2,1)S(1)}, bf16[512,512]{1,0:T(8,128)(2,1)S(1)}, u32[]{:S(2)}, u32[]{:S(2)}) collective-permute-start(bf16[512,512]{1,0:T(8,128)(2,1)S(1)} %get-tuple-element.24.refs_1_), channel_id=1, source_target_pairs={{0,64},{64,128},{128,192},{192,0},{1,65},{65,129},{129,193},{193,1... | collective-permute-start | bytes 1572872 | tf_op jit(solution)/shard_map/ppermute | solution.py:351
  96.5 16.8 %collective-permute-start.13 = (bf16[512,512]{1,0:T(8,128)(2,1)S(1)}, bf16[512,512]{1,0:T(8,128)(2,1)S(1)}, u32[]{:S(2)}, u32[]{:S(2)}) collective-permute-start(bf16[512,512]{1,0:T(8,128)(2,1)S(1)} %get-tuple-element.25.refs_0_), channel_id=1, source_target_pairs={{0,192},{64,0},{128,64},{192,128},{1,193},{65,1},{129,65},{193,129... | collective-permute-start | bytes 1572872 | tf_op jit(solution)/shard_map/ppermute | solution.py:352
  99.3 13.8 %collective-permute-start.11 = (bf16[128,1024]{1,0:T(8,128)(2,1)S(1)}, bf16[128,1024]{1,0:T(8,128)(2,1)S(1)}, u32[]{:S(2)}, u32[]{:S(2)}) collective-permute-start(bf16[128,1024]{1,0:T(8,128)(2,1)S(1)} %constant_dynamic-update-slice_fusion), channel_id=1, source_target_pairs={{0,4},{8,12},{16,20},{24,28},{32,36},{40,44},{48,52},{56,60},{64,6... | collective-permute-start | bytes 786440 | tf_op jit(solution)/shard_map/ppermute | solution.py:344
  113.2 7.5 %collective-permute-start.14 = (bf16[128,1024]{1,0:T(8,128)(2,1)S(1)}, bf16[128,1024]{1,0:T(8,128)(2,1)S(1)}, u32[]{:S(2)}, u32[]{:S(2)}) collective-permute-start(bf16[128,1024]{1,0:T(8,128)(2,1)S(1)} %broadcast_select_fusion.2), channel_id=1, source_target_pairs={{0,2},{4,6},{8,10},{12,14},{16,18},{20,22},{24,26},{28,30},{32,34}... | collective-permute-start | bytes 786440 | tf_op jit(solution)/shard_map/ppermute | solution.py:344
  115.9 16.1 %collective-permute-start.16 = (bf16[512,512]{1,0:T(8,128)(2,1)S(1)}, bf16[512,512]{1,0:T(8,128)(2,1)S(1)}, u32[]{:S(2)}, u32[]{:S(2)}) collective-permute-start(bf16[512,512]{1,0:T(8,128)(2,1)S(1)} %get-tuple-element.25.refs_0_), channel_id=1, source_target_pairs={{0,64},{64,128},{128,192},{192,0},{1,65},{65,129},{129,193},{193,1... | collective-permute-start | bytes 1572872 | tf_op jit(solution)/shard_map/ppermute | solution.py:355
  116.4 15.7 %collective-permute-start.17 = (bf16[512,512]{1,0:T(8,128)(2,1)S(1)}, bf16[512,512]{1,0:T(8,128)(2,1)}, u32[]{:S(2)}, u32[]{:S(2)}) collective-permute-start(bf16[512,512]{1,0:T(8,128)(2,1)S(1)} %get-tuple-element.24.refs_1_), channel_id=1, source_target_pairs={{0,192},{64,0},{128,64},{192,128},{1,193},{65,1},{129,65},{193,129... | collective-permute-start | bytes 1572872 | tf_op jit(solution)/shard_map/ppermute | solution.py:356
  122.1 17.8 %collective-permute-start.20 = (bf16[512,512]{1,0:T(8,128)(2,1)S(1)}, bf16[512,512]{1,0:T(8,128)(2,1)}, u32[]{:S(2)}, u32[]{:S(2)}) collective-permute-start(bf16[512,512]{1,0:T(8,128)(2,1)S(1)} %collective-permute-done.13.refs_4_), channel_id=1, source_target_pairs={{0,192},{64,0},{128,64},{192,128},{1,193},{65,1},{129,65},{193,129... | collective-permute-start | bytes 1572872 | tf_op jit(solution)/shard_map/ppermute | solution.py:360
  125.3 15.5 %collective-permute-start.21 = (bf16[512,512]{1,0:T(8,128)(2,1)S(1)}, bf16[512,512]{1,0:T(8,128)(2,1)}, u32[]{:S(2)}, u32[]{:S(2)}) collective-permute-start(bf16[512,512]{1,0:T(8,128)(2,1)S(1)} %collective-permute-done.12.refs_3_), channel_id=1, source_target_pairs={{0,64},{64,128},{128,192},{192,0},{1,65},{65,129},{129,193},{193,1... | collective-permute-start | bytes 1572872 | tf_op jit(solution)/shard_map/ppermute | solution.py:361
  132.1 8.7 %collective-permute-start.19 = (bf16[128,1024]{1,0:T(8,128)(2,1)S(1)}, bf16[128,1024]{1,0:T(8,128)(2,1)S(1)}, u32[]{:S(2)}, u32[]{:S(2)}) collective-permute-start(bf16[128,1024]{1,0:T(8,128)(2,1)S(1)} %broadcast_select_fusion.4.refs_0_), channel_id=1, source_target_pairs={{0,40},{8,0},{32,8},{40,32},{1,41},{9,1},{33,9},{41,33},{2,42},{10... | collective-permute-start | bytes 786440 | tf_op jit(solution)/shard_map/ppermute | solution.py:359
  134.6 9.3 %collective-permute-start.18 = (bf16[128,1024]{1,0:T(8,128)(2,1)S(1)}, bf16[128,1024]{1,0:T(8,128)(2,1)S(1)}, u32[]{:S(2)}, u32[]{:S(2)}) collective-permute-start(bf16[128,1024]{1,0:T(8,128)(2,1)S(1)} %broadcast_select_fusion.4.refs_0_), channel_id=1, source_target_pairs={{0,8},{8,32},{32,40},{40,0},{1,9},{9,33},{33,41},{41,1},{2,10},{10... | collective-permute-start | bytes 786440 | tf_op jit(solution)/shard_map/ppermute | solution.py:358
  140.8 7.0 %collective-permute-start.22 = (bf16[128,1024]{1,0:T(8,128)(2,1)S(1)}, bf16[128,1024]{1,0:T(8,128)(2,1)S(1)}, u32[]{:S(2)}, u32[]{:S(2)}) collective-permute-start(bf16[128,1024]{1,0:T(8,128)(2,1)S(1)} %collective-permute-done.19.refs_2_), channel_id=1, source_target_pairs={{0,40},{8,0},{32,8},{40,32},{1,41},{9,1},{33,9},{41,33},{2,42},{10... | collective-permute-start | bytes 786440 | tf_op jit(solution)/shard_map/ppermute | solution.py:363
  160.4 55.3 %all-to-all-start.2 = ((bf16[8,8,256,128]{3,2,1,0:T(8,128)(2,1)}), bf16[8,8,256,128]{3,2,1,0:T(8,128)(2,1)}, u32[]{:S(2)}, u32[]{:S(2)}) async-start(bf16[8,8,256,128]{3,2,1,0:T(8,128)(2,1)} %bitcast.25), calls=%async_computation.2 | async-start | bytes 8388608 | tf_op jit(solution)/shard_map/all_to_all | solution.py:37
  (12 other events, 204.1 us)

commit v5 on v4

--- a/solution.py
+++ b/solution.py
@@ -98,7 +98,7 @@
     total, depth = batch.shape
     _, rows, cols = weight.shape
     wide = XLO * cols
-    chunk = total // 4
+    chunk = total // 2
 
     def body(core_ref, batch_ref, weight_ref, keep_ref, give_ref, grid, sems):
         slabs = [
@@ -263,7 +263,7 @@
             2 * 2 * CORES * height * total * YS * wide,
             2 * (MATES * strip * total + YS * total * wide + MATES * height * 2 * YS * lane),
         ),
-        compiler_params=params(),
+        compiler_params=params(20 * 1024 * 1024),
     )(core, mine, theirs, *acts)
     return out.reshape(MATES, 2 * YS, height, lane)
 
@@ -340,18 +340,22 @@
     low, high, *turned = finish(sums, other, bias)
     held = jnp.concatenate(turned, axis=1)
 
-    def reach(held, span):
-        moved = lax.ppermute(held, "z", [(i, i + span) for i in range(0, DEPTH, 2 * span)])
-        return jnp.where(lax.rem(z, 2 * span) == span, moved, held)
+    def reach(held, step, sources):
+        up = lax.ppermute(held, "z", [(i, (i + step) % DEPTH) for i in sources[0]])
+        down = lax.ppermute(held, "z", [(i, (i - step) % DEPTH) for i in sources[1]])
+        for moved, origins, sign in ((up, sources[0], 1), (down, sources[1], -1)):
+            for i in origins:
+                held = jnp.where(z == (i + sign * step) % DEPTH, moved, held)
+        return held
 
     size = MATES // CORES
     forth = [(i, (i + 1) % size) for i in range(size)]
     back = [(i, (i - 1) % size) for i in range(size)]
-    held = reach(held, 4)
+    held = reach(held, 3, ((0,), (0,)))
     below_high = lax.ppermute(high, "y", shift("y", 1))
     above_low = lax.ppermute(low, "y", shift("y", -1))
     held, below_high, above_low = lax.optimization_barrier((held, below_high, above_low))
-    held = reach(reach(held, 2), 1)
+    held = reach(held, 1, ((0, 3, 5), (0, 3)))
     below_low = lax.ppermute(low, "y", shift("y", 1))
     above_high = lax.ppermute(high, "y", shift("y", -1))
     held, below_low, above_high = lax.optimization_barrier((held, below_low, above_high))
@@ -359,14 +363,14 @@
     right = lax.ppermute(held, LINE, back)
     far_low = lax.ppermute(above_low, "y", shift("y", -1))
     far_high = lax.ppermute(below_high, "y", shift("y", 1))
-    right, far_low, far_high = lax.optimization_barrier((right, far_low, far_high))
     over = lax.ppermute(right, LINE, back)
+    over, far_low, far_high = lax.optimization_barrier((over, far_low, far_high))
     here = jnp.reshape(lax.axis_index("xh") * XLO + xlo, (1,)).astype(jnp.int32)
     panel = assemble(here, (held, left, right, over), size)
     theirs = lax.ppermute(panel, "c", SWAP)
 
     acts = (low, high, below_low, below_high, above_low, above_high, far_low, far_high)
-    sent = gram(which, panel, theirs, acts)
+    sent, ys = lax.optimization_barrier((gram(which, panel, theirs, acts), ys))
     return place(ys, exchange(sent, ROW))
 
 

time: 226 us -> 215 us (0.951)
  waiting for transfers between devices: 110 us -> 54.7 us
  blocking collectives: 0 us -> 52 us
  Pallas kernels: 34.9 us -> 28.7 us
  starting transfers between devices: 68.9 us -> 64.7 us
  local copies, waits for them, and re-layouts: 7.47 us -> 10.4 us
    all_to_all x0 -> x1, blocking collectives: none -> 52 us  [exchange(): return lax.all_to_all(block, axes, split_axis=0, concat_axis=0, tiled=True)]
    all_to_all x3 -> x2, waiting for transfers between devices: 53.3 us -> 5.03 us  [exchange(): return lax.all_to_all(block, axes, split_axis=0, concat_axis=0, tiled=True)]
    all_to_all x3 -> x2, starting transfers between devices: 20.1 us -> 13.2 us  [exchange(): return lax.all_to_all(block, axes, split_axis=0, concat_axis=0, tiled=True)]
    ppermute x1, waiting for transfers between devices: 6.07 us -> 0.01 us  [per_device(): below_low = lax.ppermute(low, 'y', shift('y', 1))]
    ppermute x1, waiting for transfers between devices: 0.01 us -> 5.59 us  [per_device(): right = lax.ppermute(held, LINE, back)]
    ppermute x3 -> x4, starting transfers between devices: 13.1 us -> 18.5 us  [the longest x2 14.4 us: reach(): lax.ppermute(held, 'z', [(i, (i - step) % DEPTH) for i in sources[1]])]
    ppermute x1, waiting for transfers between devices: 5.32 us -> 0.01 us  [per_device(): far_low = lax.ppermute(above_low, 'y', shift('y', -1))]
    ppermute x3 -> x4, waiting for transfers between devices: 6.92 us -> 3.05 us  [the longest x2 2.71 us: reach(): lax.ppermute(held, 'z', [(i, (i - step) % DEPTH) for i in sources[1]])]
  transfers between devices with their start and end apart: 27 -> 27, of which waited for: 16 -> 15; matrix products, arithmetic and copies ran while one was open for 1% -> 1% of each run, Pallas kernels for 3% -> 4%
where the time goes in v5:
time: 215 us; the launch traced here: 213 us
  starting transfers between devices  64.7 us (30%)
  waiting for transfers between devices  54.7 us (25%)
  blocking collectives  52 us (24%)
  Pallas kernels  28.7 us (13%)
  local copies, waits for them, and re-layouts  10.4 us (5%)
  other arithmetic  2.28 us (1%)
    all_to_all x1, blocking collectives, exchange(): return lax.all_to_all(block, axes, split_axis=0, concat_axis=0, tiled=True)  52 us
    ppermute x3, waiting for transfers between devices, per_device(): low = lax.ppermute(low, 'z', shift('z', 1))  24.7 us
    ppermute x2, starting transfers between devices, reach(): lax.ppermute(held, 'z', [(i, (i - step) % DEPTH) for i in sources[1]])  14.4 us
    all_to_all x2, starting transfers between devices, exchange(): return lax.all_to_all(block, axes, split_axis=0, concat_axis=0, tiled=True)  13.2 us
    ppermute x3, starting transfers between devices, per_device(): high = lax.ppermute(high, 'z', shift('z', -1))  10.5 us
    pallas_call x1, Pallas kernels, encode(): pl.pallas_call(body, out_shape=(jax.ShapeDtypeStruct((total, mine), jnp.f...  9.4 us
    unnamed x17, local copies, waits for them, and re-layouts  7.35 us
    pallas_call x1, Pallas kernels, gram(): pl.pallas_call(body, out_shape=jax.ShapeDtypeStruct((2 * CORES, XLO, 2 *...  6.52 us
  transfers between devices with their start and end apart: 27, of which 15 were waited for; matrix products, arithmetic and copies ran while one was open for 1% of the time, Pallas kernels for 4%

profile of v5, /device:TPU:2, one launch (start us, length us, event | category | flops | bytes accessed | tf_op | source)
XLA Modules:
  0.0 213.0 jit_solution(9574943711419200384)
XLA Ops:
  4.7 7.5 %all-to-all-start = ((bf16[16,8,1792]{2,1,0:T(8,128)(2,1)}), bf16[16,8,1792]{2,1,0:T(8,128)(2,1)S(1)}, u32[]{:S(2)}, u32[]{:S(2)}) async-start(bf16[16,8,1792]{2,1,0:T(8,128)(2,1)} %broadcast_in_dim.2), calls=%async_computation | async-start | bytes 917504 | tf_op jit(solution)/shard_map/all_to_all | solution.py:37
  12.2 4.7 %shard_map.47 = bf16[16,224,512]{2,1,0:T(8,128)(2,1)} custom-call(bf16[224,8192]{1,0:T(8,128)(2,1)} %in_ref.1), custom_call_target="tpu_custom_call" | custom-call | bytes 7340032 | tf_op jit(solution)/shard_map/pallas_call | solution.py:58
  16.9 5.0 %all-to-all-done = bf16[16,8,1792]{2,1,0:T(8,128)(2,1)S(1)} async-done(((bf16[16,8,1792]{2,1,0:T(8,128)(2,1)}), bf16[16,8,1792]{2,1,0:T(8,128)(2,1)S(1)}, u32[]{:S(2)}, u32[]{:S(2)}) %all-to-all-start) | async-done | bytes 458784 | tf_op jit(solution)/shard_map/all_to_all | solution.py:37
  21.9 5.7 %all-to-all-start.1 = ((bf16[16,224,512]{2,1,0:T(8,128)(2,1)}), bf16[16,224,512]{2,1,0:T(8,128)(2,1)}, u32[]{:S(2)}, u32[]{:S(2)}) async-start(bf16[16,224,512]{2,1,0:T(8,128)(2,1)} %shard_map.47), calls=%async_computation.1 | async-start | bytes 7340032 | tf_op jit(solution)/shard_map/all_to_all | solution.py:37
  29.6 4.0 %collective-permute-start.2 = (bf16[128,1792]{1,0:T(8,128)(2,1)S(1)}, bf16[128,1792]{1,0:T(8,128)(2,1)S(1)}, u32[]{:S(2)}, u32[]{:S(2)}) collective-permute-start(bf16[128,1792]{1,0:T(8,128)(2,1)S(1)} %bitcast.23), channel_id=1, source_target_pairs={{0,7},{1,0},{2,1},{3,2},{4,3},{5,4},{6,5},{7,6},{8,15},{9,8},{10,9... | collective-permute-start | bytes 1376264 | tf_op jit(solution)/shard_map/ppermute | solution.py:322
  33.6 9.0 %collective-permute-done.1.refs_1_ = bf16[128,1792]{1,0:T(8,128)(2,1)S(1)} collective-permute-done((bf16[128,1792]{1,0:T(8,128)(2,1)S(1)}, bf16[128,1792]{1,0:T(8,128)(2,1)S(1)}, u32[]{:S(2)}, u32[]{:S(2)}) %collective-permute-start.1) | collective-permute-done | bytes 458784 | tf_op jit(solution)/shard_map/ppermute | solution.py:321
  42.6 3.2 %collective-permute-start.4 = (bf16[128,1792]{1,0:T(8,128)(2,1)S(1)}, bf16[128,1792]{1,0:T(8,128)(2,1)S(1)}, u32[]{:S(2)}, u32[]{:S(2)}) collective-permute-start(bf16[128,1792]{1,0:T(8,128)(2,1)S(1)} %collective-permute-done.2.refs_2_), channel_id=1, source_target_pairs={{0,7},{1,0},{2,1},{3,2},{4,3},{5,4},{6,5},{7,6},{8,15},{9,8},{10,9... | collective-permute-start | bytes 1376264 | tf_op jit(solution)/shard_map/ppermute | solution.py:322
  45.8 8.3 %collective-permute-done.3.refs_3_ = bf16[128,1792]{1,0:T(8,128)(2,1)S(1)} collective-permute-done((bf16[128,1792]{1,0:T(8,128)(2,1)S(1)}, bf16[128,1792]{1,0:T(8,128)(2,1)S(1)}, u32[]{:S(2)}, u32[]{:S(2)}) %collective-permute-start.3) | collective-permute-done | bytes 458784 | tf_op jit(solution)/shard_map/ppermute | solution.py:321
  54.1 3.2 %collective-permute-start.6 = (bf16[128,1792]{1,0:T(8,128)(2,1)S(1)}, bf16[128,1792]{1,0:T(8,128)(2,1)S(1)}, u32[]{:S(2)}, u32[]{:S(2)}) collective-permute-start(bf16[128,1792]{1,0:T(8,128)(2,1)S(1)} %collective-permute-done.4.refs_4_), channel_id=1, source_target_pairs={{0,7},{1,0},{2,1},{3,2},{4,3},{5,4},{6,5},{7,6},{8,15},{9,8},{10,9... | collective-permute-start | bytes 1376264 | tf_op jit(solution)/shard_map/ppermute | solution.py:322
  57.3 7.4 %collective-permute-done.5.refs_5_ = bf16[128,1792]{1,0:T(8,128)(2,1)S(1)} collective-permute-done((bf16[128,1792]{1,0:T(8,128)(2,1)S(1)}, bf16[128,1792]{1,0:T(8,128)(2,1)S(1)}, u32[]{:S(2)}, u32[]{:S(2)}) %collective-permute-start.5) | collective-permute-done | bytes 458784 | tf_op jit(solution)/shard_map/ppermute | solution.py:321
  64.9 3.3 %collective-permute-start.8 = (bf16[64,1792]{1,0:T(8,128)(2,1)S(1)}, bf16[64,1792]{1,0:T(8,128)(2,1)S(1)}, u32[]{:S(2)}, u32[]{:S(2)}) collective-permute-start(bf16[64,1792]{1,0:T(8,128)(2,1)S(1)} %slice.23), channel_id=1, source_target_pairs={{0,7},{1,0},{2,1},{3,2},{4,3},{5,4},{6,5},{7,6},{8,15},{9,8},{10,9... | collective-permute-start | bytes 688136 | tf_op jit(solution)/shard_map/ppermute | solution.py:326
  68.2 3.9 %collective-permute-done.7.refs_7_ = bf16[64,1792]{1,0:T(8,128)(2,1)S(1)} collective-permute-done((bf16[64,1792]{1,0:T(8,128)(2,1)S(1)}, bf16[64,1792]{1,0:T(8,128)(2,1)S(1)}, u32[]{:S(2)}, u32[]{:S(2)}) %collective-permute-start.7) | collective-permute-done | bytes 229408 | tf_op jit(solution)/shard_map/ppermute | solution.py:325
  72.1 2.8 %shard_map.46.batch_ref = bf16[1024,1792]{1,0:T(8,128)(2,1)S(1)} custom-call(s32[1]{0:T(128)} %bitcast.2.z_ref, bf16[128,1792]{1,0:T(8,128)(2,1)S(1)} %bitcast.24, bf16[128,1792]{1,0:T(8,128)(2,1)S(1)} %collective-permute-done.1.refs_1_, bf16[128,1792]{1,0:T(8,128)(2,1)S(1)} %collective-permute-done.2.refs_2_, ...), custom_call_target="tpu_custom_call" | custom-call | bytes 7340032 | tf_op jit(solution)/shard_map/pallas_call | solution.py:85
  76.7 9.4 %shard_map.48 = (f32[1024,512]{1,0:T(8,128)}, f32[1024,512]{1,0:T(8,128)}) custom-call(s32[1]{0:T(128)} %bitcast.core_ref, bf16[1024,1792]{1,0:T(8,128)(2,1)} %copy-done.1, bf16[16,224,512]{2,1,0:T(8,128)(2,1)} %all-to-all-done.1.weight_ref), custom_call_target="tpu_custom_call" | custom-call | flops 3758096384 | bytes 11534336 | tf_op jit(solution)/shard_map/pallas_call | solution.py:139
  87.0 4.2 %collective-permute-start.10 = (f32[2,128]{1,0:T(2,128)S(1)}, f32[2,128]{1,0:T(2,128)S(1)}, u32[]{:S(2)}, u32[]{:S(2)}) collective-permute-start(f32[2,128]{1,0:T(2,128)S(1)} %bitcast.28), channel_id=1, source_target_pairs={{0,8},{8,0},{1,9},{9,1},{2,10},{10,2},{3,11},{11,3},{4,12},{12,4},... | collective-permute-start | bytes 3080 | tf_op jit(solution)/shard_map/ppermute | solution.py:334
  95.6 2.8 %collective-permute-start.14 = (bf16[512,512]{1,0:T(8,128)(2,1)S(1)}, bf16[512,512]{1,0:T(8,128)(2,1)S(1)}, u32[]{:S(2)}, u32[]{:S(2)}) collective-permute-start(bf16[512,512]{1,0:T(8,128)(2,1)S(1)} %get-tuple-element.27.refs_0_), channel_id=1, source_target_pairs={{0,192},{64,0},{128,64},{192,128},{1,193},{65,1},{129,65},{193,129... | collective-permute-start | bytes 1572872 | tf_op jit(solution)/shard_map/ppermute | solution.py:356
  98.5 8.7 %collective-permute-start.11 = (bf16[128,1024]{1,0:T(8,128)(2,1)S(1)}, bf16[128,1024]{1,0:T(8,128)(2,1)S(1)}, u32[]{:S(2)}, u32[]{:S(2)}) collective-permute-start(bf16[128,1024]{1,0:T(8,128)(2,1)S(1)} %constant_dynamic-update-slice_fusion), channel_id=1, source_target_pairs={{0,5},{8,13},{16,21},{24,29},{32,37},{40,45},{48,53},{56,61},{64,6... | collective-permute-start | bytes 786440 | tf_op jit(solution)/shard_map/ppermute | solution.py:345
  113.3 5.8 %collective-permute-start.15 = (bf16[128,1024]{1,0:T(8,128)(2,1)S(1)}, bf16[128,1024]{1,0:T(8,128)(2,1)S(1)}, u32[]{:S(2)}, u32[]{:S(2)}) collective-permute-start(bf16[128,1024]{1,0:T(8,128)(2,1)S(1)} %select_select_fusion.2), channel_id=1, source_target_pairs={{0,7},{3,2},{8,15},{11,10},{16,23},{19,18},{24,31},{27,26},{32,39}... | collective-permute-start | bytes 786440 | tf_op jit(solution)/shard_map/ppermute | solution.py:345
  121.1 3.2 %collective-permute-start.22 = (bf16[512,512]{1,0:T(8,128)(2,1)S(1)}, bf16[512,512]{1,0:T(8,128)(2,1)}, u32[]{:S(2)}, u32[]{:S(2)}) collective-permute-start(bf16[512,512]{1,0:T(8,128)(2,1)S(1)} %collective-permute-done.14.refs_4_), channel_id=1, source_target_pairs={{0,192},{64,0},{128,64},{192,128},{1,193},{65,1},{129,65},{193,129... | collective-permute-start | bytes 1572872 | tf_op jit(solution)/shard_map/ppermute | solution.py:364
  129.4 5.6 %collective-permute-done.20.refs_2_ = bf16[128,1024]{1,0:T(8,128)(2,1)S(1)} collective-permute-done((bf16[128,1024]{1,0:T(8,128)(2,1)S(1)}, bf16[128,1024]{1,0:T(8,128)(2,1)S(1)}, u32[]{:S(2)}, u32[]{:S(2)}) %collective-permute-start.20) | collective-permute-done | bytes 262176 | tf_op jit(solution)/shard_map/ppermute | solution.py:363
  137.5 3.2 %collective-permute-done.23.refs_7_ = bf16[512,512]{1,0:T(8,128)(2,1)} collective-permute-done((bf16[512,512]{1,0:T(8,128)(2,1)S(1)}, bf16[512,512]{1,0:T(8,128)(2,1)}, u32[]{:S(2)}, u32[]{:S(2)}) %collective-permute-start.23) | collective-permute-done | bytes 524320 | tf_op jit(solution)/shard_map/ppermute | solution.py:365
  149.8 6.5 %shard_map.51 = bf16[4,2,8,256,128]{4,3,2,1,0:T(8,128)(2,1)S(1)} custom-call(s32[1]{0:T(128)} %bitcast.core_ref, bf16[4,128,1024]{2,1,0:T(8,128)(2,1)S(1)} %shard_map.50.mine_ref, bf16[4,128,1024]{2,1,0:T(8,128)(2,1)S(1)} %collective-permute-done.24.theirs_ref, bf16[512,512]{1,0:T(8,128)(2,1)S(1)} %get-tuple-element.27.refs_0_, ...), custom_call_target="tpu_custom_call" | custom-call | flops 4294967296 | bytes 10485760 | tf_op jit(solution)/shard_map/pallas_call | solution.py:246
  156.4 52.0 %all_to_all.15.in_ref = bf16[8,8,256,128]{3,2,1,0:T(8,128)(2,1)S(1)} all-to-all(bf16[8,8,256,128]{3,2,1,0:T(8,128)(2,1)S(1)} %bitcast.21), channel_id=1, replica_groups=mesh['y'=4,'xh'=2,'c'=2,'xl'=2,'z'=8] {'xh','c','xl'}, dimensions={0} | all-to-all | bytes 8388608 | tf_op jit(solution)/shard_map/all_to_all | solution.py:37
  208.3 4.7 %shard_map.52 = bf16[256,8192]{1,0:T(8,128)(2,1)} custom-call(s32[4]{0:T(128)S(1)} %compare_select_fusion.ys_ref, bf16[8,8,256,128]{3,2,1,0:T(8,128)(2,1)S(1)} %all_to_all.15.in_ref), custom_call_target="tpu_custom_call" | custom-call | bytes 8388608 | tf_op jit(solution)/shard_map/pallas_call | solution.py:279
  (71 shorter events, 38.5 us)
Async XLA Ops:
  4.7 17.2 %all-to-all-start = ((bf16[16,8,1792]{2,1,0:T(8,128)(2,1)}), bf16[16,8,1792]{2,1,0:T(8,128)(2,1)S(1)}, u32[]{:S(2)}, u32[]{:S(2)}) async-start(bf16[16,8,1792]{2,1,0:T(8,128)(2,1)} %broadcast_in_dim.2), calls=%async_computation | async-start | bytes 917504 | tf_op jit(solution)/shard_map/all_to_all | solution.py:37
  21.9 54.8 %all-to-all-start.1 = ((bf16[16,224,512]{2,1,0:T(8,128)(2,1)}), bf16[16,224,512]{2,1,0:T(8,128)(2,1)}, u32[]{:S(2)}, u32[]{:S(2)}) async-start(bf16[16,224,512]{2,1,0:T(8,128)(2,1)} %shard_map.47), calls=%async_computation.1 | async-start | bytes 7340032 | tf_op jit(solution)/shard_map/all_to_all | solution.py:37
  27.6 14.9 %collective-permute-start.1 = (bf16[128,1792]{1,0:T(8,128)(2,1)S(1)}, bf16[128,1792]{1,0:T(8,128)(2,1)S(1)}, u32[]{:S(2)}, u32[]{:S(2)}) collective-permute-start(bf16[128,1792]{1,0:T(8,128)(2,1)S(1)} %bitcast.22), channel_id=1, source_target_pairs={{0,1},{1,2},{2,3},{3,4},{4,5},{5,6},{6,7},{7,0},{8,9},{9,10},{10,1... | collective-permute-start | bytes 1376264 | tf_op jit(solution)/shard_map/ppermute | solution.py:321
  29.6 13.0 %collective-permute-start.2 = (bf16[128,1792]{1,0:T(8,128)(2,1)S(1)}, bf16[128,1792]{1,0:T(8,128)(2,1)S(1)}, u32[]{:S(2)}, u32[]{:S(2)}) collective-permute-start(bf16[128,1792]{1,0:T(8,128)(2,1)S(1)} %bitcast.23), channel_id=1, source_target_pairs={{0,7},{1,0},{2,1},{3,2},{4,3},{5,4},{6,5},{7,6},{8,15},{9,8},{10,9... | collective-permute-start | bytes 1376264 | tf_op jit(solution)/shard_map/ppermute | solution.py:322
  42.6 11.5 %collective-permute-start.3 = (bf16[128,1792]{1,0:T(8,128)(2,1)S(1)}, bf16[128,1792]{1,0:T(8,128)(2,1)S(1)}, u32[]{:S(2)}, u32[]{:S(2)}) collective-permute-start(bf16[128,1792]{1,0:T(8,128)(2,1)S(1)} %collective-permute-done.1.refs_1_), channel_id=1, source_target_pairs={{0,1},{1,2},{2,3},{3,4},{4,5},{5,6},{6,7},{7,0},{8,9},{9,10},{10,1... | collective-permute-start | bytes 1376264 | tf_op jit(solution)/shard_map/ppermute | solution.py:321
  42.6 11.5 %collective-permute-start.4 = (bf16[128,1792]{1,0:T(8,128)(2,1)S(1)}, bf16[128,1792]{1,0:T(8,128)(2,1)S(1)}, u32[]{:S(2)}, u32[]{:S(2)}) collective-permute-start(bf16[128,1792]{1,0:T(8,128)(2,1)S(1)} %collective-permute-done.2.refs_2_), channel_id=1, source_target_pairs={{0,7},{1,0},{2,1},{3,2},{4,3},{5,4},{6,5},{7,6},{8,15},{9,8},{10,9... | collective-permute-start | bytes 1376264 | tf_op jit(solution)/shard_map/ppermute | solution.py:322
  54.1 10.7 %collective-permute-start.5 = (bf16[128,1792]{1,0:T(8,128)(2,1)S(1)}, bf16[128,1792]{1,0:T(8,128)(2,1)S(1)}, u32[]{:S(2)}, u32[]{:S(2)}) collective-permute-start(bf16[128,1792]{1,0:T(8,128)(2,1)S(1)} %collective-permute-done.3.refs_3_), channel_id=1, source_target_pairs={{0,1},{1,2},{2,3},{3,4},{4,5},{5,6},{6,7},{7,0},{8,9},{9,10},{10,1... | collective-permute-start | bytes 1376264 | tf_op jit(solution)/shard_map/ppermute | solution.py:321
  54.1 10.8 %collective-permute-start.6 = (bf16[128,1792]{1,0:T(8,128)(2,1)S(1)}, bf16[128,1792]{1,0:T(8,128)(2,1)S(1)}, u32[]{:S(2)}, u32[]{:S(2)}) collective-permute-start(bf16[128,1792]{1,0:T(8,128)(2,1)S(1)} %collective-permute-done.4.refs_4_), channel_id=1, source_target_pairs={{0,7},{1,0},{2,1},{3,2},{4,3},{5,4},{6,5},{7,6},{8,15},{9,8},{10,9... | collective-permute-start | bytes 1376264 | tf_op jit(solution)/shard_map/ppermute | solution.py:322
  64.8 7.3 %collective-permute-start.7 = (bf16[64,1792]{1,0:T(8,128)(2,1)S(1)}, bf16[64,1792]{1,0:T(8,128)(2,1)S(1)}, u32[]{:S(2)}, u32[]{:S(2)}) collective-permute-start(bf16[64,1792]{1,0:T(8,128)(2,1)S(1)} %slice.22), channel_id=1, source_target_pairs={{0,1},{1,2},{2,3},{3,4},{4,5},{5,6},{6,7},{7,0},{8,9},{9,10},{10,1... | collective-permute-start | bytes 688136 | tf_op jit(solution)/shard_map/ppermute | solution.py:325
  64.9 7.2 %collective-permute-start.8 = (bf16[64,1792]{1,0:T(8,128)(2,1)S(1)}, bf16[64,1792]{1,0:T(8,128)(2,1)S(1)}, u32[]{:S(2)}, u32[]{:S(2)}) collective-permute-start(bf16[64,1792]{1,0:T(8,128)(2,1)S(1)} %slice.23), channel_id=1, source_target_pairs={{0,7},{1,0},{2,1},{3,2},{4,3},{5,4},{6,5},{7,6},{8,15},{9,8},{10,9... | collective-permute-start | bytes 688136 | tf_op jit(solution)/shard_map/ppermute | solution.py:326
  86.1 6.7 %collective-permute-start.9 = (f32[1024,512]{1,0:T(8,128)}, f32[1024,512]{1,0:T(8,128)S(1)}, u32[]{:S(2)}, u32[]{:S(2)}) collective-permute-start(f32[1024,512]{1,0:T(8,128)} %get-tuple-element.23), channel_id=1, source_target_pairs={{0,16},{16,0},{1,17},{17,1},{2,18},{18,2},{3,19},{19,3},{4,20},{20... | collective-permute-start | bytes 6291464 | tf_op jit(solution)/shard_map/ppermute | solution.py:339
  87.0 5.8 %collective-permute-start.10 = (f32[2,128]{1,0:T(2,128)S(1)}, f32[2,128]{1,0:T(2,128)S(1)}, u32[]{:S(2)}, u32[]{:S(2)}) collective-permute-start(f32[2,128]{1,0:T(2,128)S(1)} %bitcast.28), channel_id=1, source_target_pairs={{0,8},{8,0},{1,9},{9,1},{2,10},{10,2},{3,11},{11,3},{4,12},{12,4},... | collective-permute-start | bytes 3080 | tf_op jit(solution)/shard_map/ppermute | solution.py:334
  95.0 18.3 %collective-permute-start.13 = (bf16[512,512]{1,0:T(8,128)(2,1)S(1)}, bf16[512,512]{1,0:T(8,128)(2,1)S(1)}, u32[]{:S(2)}, u32[]{:S(2)}) collective-permute-start(bf16[512,512]{1,0:T(8,128)(2,1)S(1)} %get-tuple-element.26.refs_1_), channel_id=1, source_target_pairs={{0,64},{64,128},{128,192},{192,0},{1,65},{65,129},{129,193},{193,1... | collective-permute-start | bytes 1572872 | tf_op jit(solution)/shard_map/ppermute | solution.py:355
  95.6 17.6 %collective-permute-start.14 = (bf16[512,512]{1,0:T(8,128)(2,1)S(1)}, bf16[512,512]{1,0:T(8,128)(2,1)S(1)}, u32[]{:S(2)}, u32[]{:S(2)}) collective-permute-start(bf16[512,512]{1,0:T(8,128)(2,1)S(1)} %get-tuple-element.27.refs_0_), channel_id=1, source_target_pairs={{0,192},{64,0},{128,64},{192,128},{1,193},{65,1},{129,65},{193,129... | collective-permute-start | bytes 1572872 | tf_op jit(solution)/shard_map/ppermute | solution.py:356
  98.5 13.4 %collective-permute-start.11 = (bf16[128,1024]{1,0:T(8,128)(2,1)S(1)}, bf16[128,1024]{1,0:T(8,128)(2,1)S(1)}, u32[]{:S(2)}, u32[]{:S(2)}) collective-permute-start(bf16[128,1024]{1,0:T(8,128)(2,1)S(1)} %constant_dynamic-update-slice_fusion), channel_id=1, source_target_pairs={{0,5},{8,13},{16,21},{24,29},{32,37},{40,45},{48,53},{56,61},{64,6... | collective-permute-start | bytes 786440 | tf_op jit(solution)/shard_map/ppermute | solution.py:345
  107.1 6.0 %collective-permute-start.12 = (bf16[128,1024]{1,0:T(8,128)(2,1)S(1)}, bf16[128,1024]{1,0:T(8,128)(2,1)}, u32[]{:S(2)}, u32[]{:S(2)}) collective-permute-start(bf16[128,1024]{1,0:T(8,128)(2,1)S(1)} %constant_dynamic-update-slice_fusion), channel_id=1, source_target_pairs={{0,3},{8,11},{16,19},{24,27},{32,35},{40,43},{48,51},{56,59},{64,6... | collective-permute-start | bytes 786440 | tf_op jit(solution)/shard_map/ppermute | solution.py:344
  109.2 16.2 %collective-permute-start.17 = (bf16[512,512]{1,0:T(8,128)(2,1)S(1)}, bf16[512,512]{1,0:T(8,128)(2,1)S(1)}, u32[]{:S(2)}, u32[]{:S(2)}) collective-permute-start(bf16[512,512]{1,0:T(8,128)(2,1)S(1)} %get-tuple-element.27.refs_0_), channel_id=1, source_target_pairs={{0,64},{64,128},{128,192},{192,0},{1,65},{65,129},{129,193},{193,1... | collective-permute-start | bytes 1572872 | tf_op jit(solution)/shard_map/ppermute | solution.py:359
  111.9 15.0 %collective-permute-start.18 = (bf16[512,512]{1,0:T(8,128)(2,1)S(1)}, bf16[512,512]{1,0:T(8,128)(2,1)}, u32[]{:S(2)}, u32[]{:S(2)}) collective-permute-start(bf16[512,512]{1,0:T(8,128)(2,1)S(1)} %get-tuple-element.26.refs_1_), channel_id=1, source_target_pairs={{0,192},{64,0},{128,64},{192,128},{1,193},{65,1},{129,65},{193,129... | collective-permute-start | bytes 1572872 | tf_op jit(solution)/shard_map/ppermute | solution.py:360
  113.3 11.0 %collective-permute-start.15 = (bf16[128,1024]{1,0:T(8,128)(2,1)S(1)}, bf16[128,1024]{1,0:T(8,128)(2,1)S(1)}, u32[]{:S(2)}, u32[]{:S(2)}) collective-permute-start(bf16[128,1024]{1,0:T(8,128)(2,1)S(1)} %select_select_fusion.2), channel_id=1, source_target_pairs={{0,7},{3,2},{8,15},{11,10},{16,23},{19,18},{24,31},{27,26},{32,39}... | collective-permute-start | bytes 786440 | tf_op jit(solution)/shard_map/ppermute | solution.py:345
  121.1 16.4 %collective-permute-start.22 = (bf16[512,512]{1,0:T(8,128)(2,1)S(1)}, bf16[512,512]{1,0:T(8,128)(2,1)}, u32[]{:S(2)}, u32[]{:S(2)}) collective-permute-start(bf16[512,512]{1,0:T(8,128)(2,1)S(1)} %collective-permute-done.14.refs_4_), channel_id=1, source_target_pairs={{0,192},{64,0},{128,64},{192,128},{1,193},{65,1},{129,65},{193,129... | collective-permute-start | bytes 1572872 | tf_op jit(solution)/shard_map/ppermute | solution.py:364
  126.8 8.1 %collective-permute-start.20 = (bf16[128,1024]{1,0:T(8,128)(2,1)S(1)}, bf16[128,1024]{1,0:T(8,128)(2,1)S(1)}, u32[]{:S(2)}, u32[]{:S(2)}) collective-permute-start(bf16[128,1024]{1,0:T(8,128)(2,1)S(1)} %select_select_fusion.refs_0_), channel_id=1, source_target_pairs={{0,40},{8,0},{32,8},{40,32},{1,41},{9,1},{33,9},{41,33},{2,42},{10... | collective-permute-start | bytes 786440 | tf_op jit(solution)/shard_map/ppermute | solution.py:363
  129.4 11.3 %collective-permute-start.23 = (bf16[512,512]{1,0:T(8,128)(2,1)S(1)}, bf16[512,512]{1,0:T(8,128)(2,1)}, u32[]{:S(2)}, u32[]{:S(2)}) collective-permute-start(bf16[512,512]{1,0:T(8,128)(2,1)S(1)} %collective-permute-done.13.refs_3_), channel_id=1, source_target_pairs={{0,64},{64,128},{128,192},{192,0},{1,65},{65,129},{129,193},{193,1... | collective-permute-start | bytes 1572872 | tf_op jit(solution)/shard_map/ppermute | solution.py:365
  135.0 6.4 %collective-permute-start.21 = (bf16[128,1024]{1,0:T(8,128)(2,1)S(1)}, bf16[128,1024]{1,0:T(8,128)(2,1)S(1)}, u32[]{:S(2)}, u32[]{:S(2)}) collective-permute-start(bf16[128,1024]{1,0:T(8,128)(2,1)S(1)} %collective-permute-done.20.refs_2_), channel_id=1, source_target_pairs={{0,40},{8,0},{32,8},{40,32},{1,41},{9,1},{33,9},{41,33},{2,42},{10... | collective-permute-start | bytes 786440 | tf_op jit(solution)/shard_map/ppermute | solution.py:366
  137.5 6.4 %collective-permute-start.19 = (bf16[128,1024]{1,0:T(8,128)(2,1)S(1)}, bf16[128,1024]{1,0:T(8,128)(2,1)S(1)}, u32[]{:S(2)}, u32[]{:S(2)}) collective-permute-start(bf16[128,1024]{1,0:T(8,128)(2,1)S(1)} %select_select_fusion.refs_0_), channel_id=1, source_target_pairs={{0,8},{8,32},{32,40},{40,0},{1,9},{9,33},{33,41},{41,1},{2,10},{10... | collective-permute-start | bytes 786440 | tf_op jit(solution)/shard_map/ppermute | solution.py:362
  (11 other events, 78.1 us)

commit v6 on v5

--- a/solution.py
+++ b/solution.py
@@ -263,32 +263,41 @@
             2 * 2 * CORES * height * total * YS * wide,
             2 * (MATES * strip * total + YS * total * wide + MATES * height * 2 * YS * lane),
         ),
-        compiler_params=params(20 * 1024 * 1024),
+        compiler_params=params(57 * 1024 * 1024),
     )(core, mine, theirs, *acts)
     return out.reshape(MATES, 2 * YS, height, lane)
 
 
 def place(ys, received):
-    _, _, height, lane = received.shape
-    slab = MATES * 2 * YS * lane
-
-    def body(ys_ref, in_ref, out_ref):
-        for s in range(MATES):
-            out_ref[:, s * lane : (s + 1) * lane] = in_ref[s, 0]
-
-    return pl.pallas_call(
-        body,
-        out_shape=jax.ShapeDtypeStruct((height, slab), jnp.bfloat16),
-        grid_spec=pltpu.PrefetchScalarGridSpec(
-            num_scalar_prefetch=1,
-            grid=(YS, 2),
-            in_specs=[
-                pl.BlockSpec((MATES, 1, height, lane), lambda r, h, ys: (0, 2 * r + h, 0, 0))
-            ],
-            out_specs=pl.BlockSpec((height, MATES * lane), lambda r, h, ys: (0, h * YS + ys[r])),
-        ),
-        cost_estimate=cost(0, 4 * height * slab),
-        compiler_params=params(8 * 1024 * 1024),
+    _, strips, height, lane = received.shape
+    wide = MATES * lane
+
+    def body(ys_ref, in_ref, out_ref, staged, sems):
+        copies = []
+        for i in range(strips):
+            for s in range(MATES):
+                staged[i, :, s * lane : (s + 1) * lane] = in_ref[s, i]
+            start = ((i % 2) * YS + ys_ref[i // 2]) * wide
+            to = out_ref.at[:, pl.ds(pl.multiple_of(start, lane), wide)]
+            copies.append(pltpu.make_async_copy(staged.at[i], to, sems.at[i]))
+            copies[-1].start()
+        for copy in copies:
+            copy.wait()
+
+    return pl.pallas_call(
+        body,
+        out_shape=jax.ShapeDtypeStruct((height, strips * wide), jnp.bfloat16),
+        in_specs=[
+            pl.BlockSpec(memory_space=pltpu.SMEM),
+            pl.BlockSpec(memory_space=pltpu.VMEM),
+        ],
+        out_specs=pl.BlockSpec(memory_space=pl.ANY),
+        scratch_shapes=[
+            pltpu.VMEM((strips, height, wide), jnp.bfloat16),
+            pltpu.SemaphoreType.DMA((strips,)),
+        ],
+        cost_estimate=cost(0, 4 * height * strips * wide),
+        compiler_params=params(16 * 1024 * 1024),
     )(ys, received)
 
 
@@ -363,7 +372,7 @@
     right = lax.ppermute(held, LINE, back)
     far_low = lax.ppermute(above_low, "y", shift("y", -1))
     far_high = lax.ppermute(below_high, "y", shift("y", 1))
-    over = lax.ppermute(right, LINE, back)
+    over = lax.ppermute(held, LINE, [(i, (i + 2) % size) for i in range(size)])
     over, far_low, far_high = lax.optimization_barrier((over, far_low, far_high))
     here = jnp.reshape(lax.axis_index("xh") * XLO + xlo, (1,)).astype(jnp.int32)
     panel = assemble(here, (held, left, right, over), size)

time: 215 us -> 210 us (0.977)
  waiting for transfers between devices: 54.7 us -> 51.4 us
  blocking collectives: 52 us -> 54.4 us
  starting transfers between devices: 64.7 us -> 62.5 us
    ppermute x1, waiting for transfers between devices: 5.59 us -> 0.38 us  [per_device(): right = lax.ppermute(held, LINE, back)]
    ppermute x1, waiting for transfers between devices: 0.67 us -> 3.89 us  [per_device(): over = lax.ppermute(held, LINE, [(i, (i + 2) % size) for i in range(size)])]
    ppermute x1, waiting for transfers between devices: 3.22 us -> 0.01 us  [per_device(): far_high = lax.ppermute(below_high, 'y', shift('y', 1))]
    ppermute x1, starting transfers between devices: 0.01 us -> 2.86 us  [per_device(): left = lax.ppermute(held, LINE, forth)]
    ppermute x1, starting transfers between devices: 2.55 us -> 0.01 us  [per_device(): right = lax.ppermute(held, LINE, back)]
    all_to_all x1, blocking collectives: 52 us -> 54.4 us  [exchange(): return lax.all_to_all(block, axes, split_axis=0, concat_axis=0, tiled=True)]
    pallas_call x1, Pallas kernels: 6.52 us -> 8.73 us  [gram(): pl.pallas_call(body, out_shape=jax.ShapeDtypeStruct((2 * CORES, XLO, 2 *...]
where the time goes in v6:
time: 210 us; the launch traced here: 208 us
  starting transfers between devices  62.5 us (30%)
  blocking collectives  54.4 us (26%)
  waiting for transfers between devices  51.4 us (24%)
  Pallas kernels  29 us (14%)
  local copies, waits for them, and re-layouts  9.03 us (4%)
    all_to_all x1, blocking collectives, exchange(): return lax.all_to_all(block, axes, split_axis=0, concat_axis=0, tiled=True)  54.4 us
    ppermute x3, waiting for transfers between devices, per_device(): low = lax.ppermute(low, 'z', shift('z', 1))  24.7 us
    ppermute x2, starting transfers between devices, reach(): lax.ppermute(held, 'z', [(i, (i - step) % DEPTH) for i in sources[1]])  14.6 us
    all_to_all x2, starting transfers between devices, exchange(): return lax.all_to_all(block, axes, split_axis=0, concat_axis=0, tiled=True)  13.2 us
    ppermute x3, starting transfers between devices, per_device(): high = lax.ppermute(high, 'z', shift('z', -1))  10.5 us
    pallas_call x1, Pallas kernels, encode(): pl.pallas_call(body, out_shape=(jax.ShapeDtypeStruct((total, mine), jnp.f...  9.4 us
    pallas_call x1, Pallas kernels, gram(): pl.pallas_call(body, out_shape=jax.ShapeDtypeStruct((2 * CORES, XLO, 2 *...  8.73 us
    unnamed x17, local copies, waits for them, and re-layouts  5.99 us
  transfers between devices with their start and end apart: 27, of which 15 were waited for; matrix products, arithmetic and copies ran while one was open for 1% of the time, Pallas kernels for 4%

profile of v6, /device:TPU:2, one launch (start us, length us, event | category | flops | bytes accessed | tf_op | source)
XLA Modules:
  0.0 208.2 jit_solution(16682568266985615302)
XLA Ops:
  4.7 7.5 %all-to-all-start = ((bf16[16,8,1792]{2,1,0:T(8,128)(2,1)}), bf16[16,8,1792]{2,1,0:T(8,128)(2,1)S(1)}, u32[]{:S(2)}, u32[]{:S(2)}) async-start(bf16[16,8,1792]{2,1,0:T(8,128)(2,1)} %broadcast_in_dim.2), calls=%async_computation | async-start | bytes 917504 | tf_op jit(solution)/shard_map/all_to_all | solution.py:37
  12.2 4.7 %shard_map.47 = bf16[16,224,512]{2,1,0:T(8,128)(2,1)} custom-call(bf16[224,8192]{1,0:T(8,128)(2,1)} %in_ref.1), custom_call_target="tpu_custom_call" | custom-call | bytes 7340032 | tf_op jit(solution)/shard_map/pallas_call | solution.py:58
  16.9 5.0 %all-to-all-done = bf16[16,8,1792]{2,1,0:T(8,128)(2,1)S(1)} async-done(((bf16[16,8,1792]{2,1,0:T(8,128)(2,1)}), bf16[16,8,1792]{2,1,0:T(8,128)(2,1)S(1)}, u32[]{:S(2)}, u32[]{:S(2)}) %all-to-all-start) | async-done | bytes 458784 | tf_op jit(solution)/shard_map/all_to_all | solution.py:37
  21.9 5.7 %all-to-all-start.1 = ((bf16[16,224,512]{2,1,0:T(8,128)(2,1)}), bf16[16,224,512]{2,1,0:T(8,128)(2,1)}, u32[]{:S(2)}, u32[]{:S(2)}) async-start(bf16[16,224,512]{2,1,0:T(8,128)(2,1)} %shard_map.47), calls=%async_computation.1 | async-start | bytes 7340032 | tf_op jit(solution)/shard_map/all_to_all | solution.py:37
  29.6 4.0 %collective-permute-start.2 = (bf16[128,1792]{1,0:T(8,128)(2,1)S(1)}, bf16[128,1792]{1,0:T(8,128)(2,1)S(1)}, u32[]{:S(2)}, u32[]{:S(2)}) collective-permute-start(bf16[128,1792]{1,0:T(8,128)(2,1)S(1)} %bitcast.22), channel_id=1, source_target_pairs={{0,7},{1,0},{2,1},{3,2},{4,3},{5,4},{6,5},{7,6},{8,15},{9,8},{10,9... | collective-permute-start | bytes 1376264 | tf_op jit(solution)/shard_map/ppermute | solution.py:331
  33.6 9.0 %collective-permute-done.1.refs_1_ = bf16[128,1792]{1,0:T(8,128)(2,1)S(1)} collective-permute-done((bf16[128,1792]{1,0:T(8,128)(2,1)S(1)}, bf16[128,1792]{1,0:T(8,128)(2,1)S(1)}, u32[]{:S(2)}, u32[]{:S(2)}) %collective-permute-start.1) | collective-permute-done | bytes 458784 | tf_op jit(solution)/shard_map/ppermute | solution.py:330
  42.6 3.2 %collective-permute-start.4 = (bf16[128,1792]{1,0:T(8,128)(2,1)S(1)}, bf16[128,1792]{1,0:T(8,128)(2,1)S(1)}, u32[]{:S(2)}, u32[]{:S(2)}) collective-permute-start(bf16[128,1792]{1,0:T(8,128)(2,1)S(1)} %collective-permute-done.2.refs_2_), channel_id=1, source_target_pairs={{0,7},{1,0},{2,1},{3,2},{4,3},{5,4},{6,5},{7,6},{8,15},{9,8},{10,9... | collective-permute-start | bytes 1376264 | tf_op jit(solution)/shard_map/ppermute | solution.py:331
  45.8 8.3 %collective-permute-done.3.refs_3_ = bf16[128,1792]{1,0:T(8,128)(2,1)S(1)} collective-permute-done((bf16[128,1792]{1,0:T(8,128)(2,1)S(1)}, bf16[128,1792]{1,0:T(8,128)(2,1)S(1)}, u32[]{:S(2)}, u32[]{:S(2)}) %collective-permute-start.3) | collective-permute-done | bytes 458784 | tf_op jit(solution)/shard_map/ppermute | solution.py:330
  54.1 3.2 %collective-permute-start.6 = (bf16[128,1792]{1,0:T(8,128)(2,1)S(1)}, bf16[128,1792]{1,0:T(8,128)(2,1)S(1)}, u32[]{:S(2)}, u32[]{:S(2)}) collective-permute-start(bf16[128,1792]{1,0:T(8,128)(2,1)S(1)} %collective-permute-done.4.refs_4_), channel_id=1, source_target_pairs={{0,7},{1,0},{2,1},{3,2},{4,3},{5,4},{6,5},{7,6},{8,15},{9,8},{10,9... | collective-permute-start | bytes 1376264 | tf_op jit(solution)/shard_map/ppermute | solution.py:331
  57.3 7.4 %collective-permute-done.5.refs_5_ = bf16[128,1792]{1,0:T(8,128)(2,1)S(1)} collective-permute-done((bf16[128,1792]{1,0:T(8,128)(2,1)S(1)}, bf16[128,1792]{1,0:T(8,128)(2,1)S(1)}, u32[]{:S(2)}, u32[]{:S(2)}) %collective-permute-start.5) | collective-permute-done | bytes 458784 | tf_op jit(solution)/shard_map/ppermute | solution.py:330
  64.9 3.3 %collective-permute-start.8 = (bf16[64,1792]{1,0:T(8,128)(2,1)S(1)}, bf16[64,1792]{1,0:T(8,128)(2,1)S(1)}, u32[]{:S(2)}, u32[]{:S(2)}) collective-permute-start(bf16[64,1792]{1,0:T(8,128)(2,1)S(1)} %slice.23), channel_id=1, source_target_pairs={{0,7},{1,0},{2,1},{3,2},{4,3},{5,4},{6,5},{7,6},{8,15},{9,8},{10,9... | collective-permute-start | bytes 688136 | tf_op jit(solution)/shard_map/ppermute | solution.py:335
  68.2 3.9 %collective-permute-done.7.refs_7_ = bf16[64,1792]{1,0:T(8,128)(2,1)S(1)} collective-permute-done((bf16[64,1792]{1,0:T(8,128)(2,1)S(1)}, bf16[64,1792]{1,0:T(8,128)(2,1)S(1)}, u32[]{:S(2)}, u32[]{:S(2)}) %collective-permute-start.7) | collective-permute-done | bytes 229408 | tf_op jit(solution)/shard_map/ppermute | solution.py:334
  72.1 2.8 %shard_map.46.batch_ref = bf16[1024,1792]{1,0:T(8,128)(2,1)S(1)} custom-call(s32[1]{0:T(128)} %bitcast.2.z_ref, bf16[128,1792]{1,0:T(8,128)(2,1)S(1)} %bitcast.23, bf16[128,1792]{1,0:T(8,128)(2,1)S(1)} %collective-permute-done.1.refs_1_, bf16[128,1792]{1,0:T(8,128)(2,1)S(1)} %collective-permute-done.2.refs_2_, ...), custom_call_target="tpu_custom_call" | custom-call | bytes 7340032 | tf_op jit(solution)/shard_map/pallas_call | solution.py:85
  76.7 9.4 %shard_map.48 = (f32[1024,512]{1,0:T(8,128)}, f32[1024,512]{1,0:T(8,128)}) custom-call(s32[1]{0:T(128)} %bitcast.core_ref, bf16[1024,1792]{1,0:T(8,128)(2,1)} %copy-done.1, bf16[16,224,512]{2,1,0:T(8,128)(2,1)} %all-to-all-done.1.weight_ref), custom_call_target="tpu_custom_call" | custom-call | flops 3758096384 | bytes 11534336 | tf_op jit(solution)/shard_map/pallas_call | solution.py:139
  87.0 4.2 %collective-permute-start.10 = (f32[2,128]{1,0:T(2,128)S(1)}, f32[2,128]{1,0:T(2,128)S(1)}, u32[]{:S(2)}, u32[]{:S(2)}) collective-permute-start(f32[2,128]{1,0:T(2,128)S(1)} %bitcast.28), channel_id=1, source_target_pairs={{0,8},{8,0},{1,9},{9,1},{2,10},{10,2},{3,11},{11,3},{4,12},{12,4},... | collective-permute-start | bytes 3080 | tf_op jit(solution)/shard_map/ppermute | solution.py:343
  95.6 2.8 %collective-permute-start.14 = (bf16[512,512]{1,0:T(8,128)(2,1)S(1)}, bf16[512,512]{1,0:T(8,128)(2,1)}, u32[]{:S(2)}, u32[]{:S(2)}) collective-permute-start(bf16[512,512]{1,0:T(8,128)(2,1)S(1)} %get-tuple-element.27.refs_0_), channel_id=1, source_target_pairs={{0,192},{64,0},{128,64},{192,128},{1,193},{65,1},{129,65},{193,129... | collective-permute-start | bytes 1572872 | tf_op jit(solution)/shard_map/ppermute | solution.py:365
  98.5 8.7 %collective-permute-start.11 = (bf16[128,1024]{1,0:T(8,128)(2,1)S(1)}, bf16[128,1024]{1,0:T(8,128)(2,1)S(1)}, u32[]{:S(2)}, u32[]{:S(2)}) collective-permute-start(bf16[128,1024]{1,0:T(8,128)(2,1)S(1)} %constant_dynamic-update-slice_fusion), channel_id=1, source_target_pairs={{0,5},{8,13},{16,21},{24,29},{32,37},{40,45},{48,53},{56,61},{64,6... | collective-permute-start | bytes 786440 | tf_op jit(solution)/shard_map/ppermute | solution.py:354
  108.6 3.3 %collective-permute-done.11 = bf16[128,1024]{1,0:T(8,128)(2,1)S(1)} collective-permute-done((bf16[128,1024]{1,0:T(8,128)(2,1)S(1)}, bf16[128,1024]{1,0:T(8,128)(2,1)S(1)}, u32[]{:S(2)}, u32[]{:S(2)}) %collective-permute-start.11) | collective-permute-done | bytes 262176 | tf_op jit(solution)/shard_map/ppermute | solution.py:354
  113.3 5.9 %collective-permute-start.15 = (bf16[128,1024]{1,0:T(8,128)(2,1)S(1)}, bf16[128,1024]{1,0:T(8,128)(2,1)S(1)}, u32[]{:S(2)}, u32[]{:S(2)}) collective-permute-start(bf16[128,1024]{1,0:T(8,128)(2,1)S(1)} %select_select_fusion.2), channel_id=1, source_target_pairs={{0,7},{3,2},{8,15},{11,10},{16,23},{19,18},{24,31},{27,26},{32,39}... | collective-permute-start | bytes 786440 | tf_op jit(solution)/shard_map/ppermute | solution.py:354
  120.5 3.3 %collective-permute-start.22 = (bf16[512,512]{1,0:T(8,128)(2,1)}, bf16[512,512]{1,0:T(8,128)(2,1)}, u32[]{:S(2)}, u32[]{:S(2)}) collective-permute-start(bf16[512,512]{1,0:T(8,128)(2,1)} %collective-permute-done.14.refs_4_), channel_id=1, source_target_pairs={{0,192},{64,0},{128,64},{192,128},{1,193},{65,1},{129,65},{193,129... | collective-permute-start | bytes 1572872 | tf_op jit(solution)/shard_map/ppermute | solution.py:373
  128.7 2.9 %collective-permute-start.19 = (bf16[128,1024]{1,0:T(8,128)(2,1)S(1)}, bf16[128,1024]{1,0:T(8,128)(2,1)S(1)}, u32[]{:S(2)}, u32[]{:S(2)}) collective-permute-start(bf16[128,1024]{1,0:T(8,128)(2,1)S(1)} %select_select_fusion.refs_0_), channel_id=1, source_target_pairs={{0,8},{8,32},{32,40},{40,0},{1,9},{9,33},{33,41},{41,1},{2,10},{10... | collective-permute-start | bytes 786440 | tf_op jit(solution)/shard_map/ppermute | solution.py:371
  131.6 3.9 %collective-permute-done.21.refs_3_ = bf16[128,1024]{1,0:T(8,128)(2,1)S(1)} collective-permute-done((bf16[128,1024]{1,0:T(8,128)(2,1)S(1)}, bf16[128,1024]{1,0:T(8,128)(2,1)S(1)}, u32[]{:S(2)}, u32[]{:S(2)}) %collective-permute-start.21) | collective-permute-done | bytes 262176 | tf_op jit(solution)/shard_map/ppermute | solution.py:375
  142.1 8.7 %shard_map.51 = bf16[4,2,8,256,128]{4,3,2,1,0:T(8,128)(2,1)} custom-call(s32[1]{0:T(128)} %bitcast.core_ref, bf16[4,128,1024]{2,1,0:T(8,128)(2,1)} %copy-done.2, bf16[4,128,1024]{2,1,0:T(8,128)(2,1)} %copy-done.5, bf16[512,512]{1,0:T(8,128)(2,1)} %copy-done.3, bf16[512,512]{1,0:T(8,128)(2,1)} %copy-done.4, bf16[512,512]{1,0:T(8,128)(2,1)} %copy-done.6, ...), custom_call_target="tpu_custom_call" | custom-call | flops 4294967296 | bytes 10485760 | tf_op jit(solution)/shard_map/pallas_call | solution.py:246
  150.8 54.4 %all_to_all.15.in_ref = bf16[8,8,256,128]{3,2,1,0:T(8,128)(2,1)S(1)} all-to-all(bf16[8,8,256,128]{3,2,1,0:T(8,128)(2,1)} %bitcast.25), channel_id=1, replica_groups=mesh['y'=4,'xh'=2,'c'=2,'xl'=2,'z'=8] {'xh','c','xl'}, dimensions={0} | all-to-all | bytes 8388608 | tf_op jit(solution)/shard_map/all_to_all | solution.py:37
  (71 shorter events, 32.0 us)
Async XLA Ops:
  4.7 17.2 %all-to-all-start = ((bf16[16,8,1792]{2,1,0:T(8,128)(2,1)}), bf16[16,8,1792]{2,1,0:T(8,128)(2,1)S(1)}, u32[]{:S(2)}, u32[]{:S(2)}) async-start(bf16[16,8,1792]{2,1,0:T(8,128)(2,1)} %broadcast_in_dim.2), calls=%async_computation | async-start | bytes 917504 | tf_op jit(solution)/shard_map/all_to_all | solution.py:37
  21.9 54.8 %all-to-all-start.1 = ((bf16[16,224,512]{2,1,0:T(8,128)(2,1)}), bf16[16,224,512]{2,1,0:T(8,128)(2,1)}, u32[]{:S(2)}, u32[]{:S(2)}) async-start(bf16[16,224,512]{2,1,0:T(8,128)(2,1)} %shard_map.47), calls=%async_computation.1 | async-start | bytes 7340032 | tf_op jit(solution)/shard_map/all_to_all | solution.py:37
  27.6 14.9 %collective-permute-start.1 = (bf16[128,1792]{1,0:T(8,128)(2,1)S(1)}, bf16[128,1792]{1,0:T(8,128)(2,1)S(1)}, u32[]{:S(2)}, u32[]{:S(2)}) collective-permute-start(bf16[128,1792]{1,0:T(8,128)(2,1)S(1)} %bitcast.21), channel_id=1, source_target_pairs={{0,1},{1,2},{2,3},{3,4},{4,5},{5,6},{6,7},{7,0},{8,9},{9,10},{10,1... | collective-permute-start | bytes 1376264 | tf_op jit(solution)/shard_map/ppermute | solution.py:330
  29.6 13.0 %collective-permute-start.2 = (bf16[128,1792]{1,0:T(8,128)(2,1)S(1)}, bf16[128,1792]{1,0:T(8,128)(2,1)S(1)}, u32[]{:S(2)}, u32[]{:S(2)}) collective-permute-start(bf16[128,1792]{1,0:T(8,128)(2,1)S(1)} %bitcast.22), channel_id=1, source_target_pairs={{0,7},{1,0},{2,1},{3,2},{4,3},{5,4},{6,5},{7,6},{8,15},{9,8},{10,9... | collective-permute-start | bytes 1376264 | tf_op jit(solution)/shard_map/ppermute | solution.py:331
  42.6 11.5 %collective-permute-start.3 = (bf16[128,1792]{1,0:T(8,128)(2,1)S(1)}, bf16[128,1792]{1,0:T(8,128)(2,1)S(1)}, u32[]{:S(2)}, u32[]{:S(2)}) collective-permute-start(bf16[128,1792]{1,0:T(8,128)(2,1)S(1)} %collective-permute-done.1.refs_1_), channel_id=1, source_target_pairs={{0,1},{1,2},{2,3},{3,4},{4,5},{5,6},{6,7},{7,0},{8,9},{9,10},{10,1... | collective-permute-start | bytes 1376264 | tf_op jit(solution)/shard_map/ppermute | solution.py:330
  42.6 11.5 %collective-permute-start.4 = (bf16[128,1792]{1,0:T(8,128)(2,1)S(1)}, bf16[128,1792]{1,0:T(8,128)(2,1)S(1)}, u32[]{:S(2)}, u32[]{:S(2)}) collective-permute-start(bf16[128,1792]{1,0:T(8,128)(2,1)S(1)} %collective-permute-done.2.refs_2_), channel_id=1, source_target_pairs={{0,7},{1,0},{2,1},{3,2},{4,3},{5,4},{6,5},{7,6},{8,15},{9,8},{10,9... | collective-permute-start | bytes 1376264 | tf_op jit(solution)/shard_map/ppermute | solution.py:331
  54.1 10.7 %collective-permute-start.5 = (bf16[128,1792]{1,0:T(8,128)(2,1)S(1)}, bf16[128,1792]{1,0:T(8,128)(2,1)S(1)}, u32[]{:S(2)}, u32[]{:S(2)}) collective-permute-start(bf16[128,1792]{1,0:T(8,128)(2,1)S(1)} %collective-permute-done.3.refs_3_), channel_id=1, source_target_pairs={{0,1},{1,2},{2,3},{3,4},{4,5},{5,6},{6,7},{7,0},{8,9},{9,10},{10,1... | collective-permute-start | bytes 1376264 | tf_op jit(solution)/shard_map/ppermute | solution.py:330
  54.1 10.8 %collective-permute-start.6 = (bf16[128,1792]{1,0:T(8,128)(2,1)S(1)}, bf16[128,1792]{1,0:T(8,128)(2,1)S(1)}, u32[]{:S(2)}, u32[]{:S(2)}) collective-permute-start(bf16[128,1792]{1,0:T(8,128)(2,1)S(1)} %collective-permute-done.4.refs_4_), channel_id=1, source_target_pairs={{0,7},{1,0},{2,1},{3,2},{4,3},{5,4},{6,5},{7,6},{8,15},{9,8},{10,9... | collective-permute-start | bytes 1376264 | tf_op jit(solution)/shard_map/ppermute | solution.py:331
  64.8 7.3 %collective-permute-start.7 = (bf16[64,1792]{1,0:T(8,128)(2,1)S(1)}, bf16[64,1792]{1,0:T(8,128)(2,1)S(1)}, u32[]{:S(2)}, u32[]{:S(2)}) collective-permute-start(bf16[64,1792]{1,0:T(8,128)(2,1)S(1)} %slice.22), channel_id=1, source_target_pairs={{0,1},{1,2},{2,3},{3,4},{4,5},{5,6},{6,7},{7,0},{8,9},{9,10},{10,1... | collective-permute-start | bytes 688136 | tf_op jit(solution)/shard_map/ppermute | solution.py:334
  64.9 7.2 %collective-permute-start.8 = (bf16[64,1792]{1,0:T(8,128)(2,1)S(1)}, bf16[64,1792]{1,0:T(8,128)(2,1)S(1)}, u32[]{:S(2)}, u32[]{:S(2)}) collective-permute-start(bf16[64,1792]{1,0:T(8,128)(2,1)S(1)} %slice.23), channel_id=1, source_target_pairs={{0,7},{1,0},{2,1},{3,2},{4,3},{5,4},{6,5},{7,6},{8,15},{9,8},{10,9... | collective-permute-start | bytes 688136 | tf_op jit(solution)/shard_map/ppermute | solution.py:335
  86.1 6.7 %collective-permute-start.9 = (f32[1024,512]{1,0:T(8,128)}, f32[1024,512]{1,0:T(8,128)S(1)}, u32[]{:S(2)}, u32[]{:S(2)}) collective-permute-start(f32[1024,512]{1,0:T(8,128)} %get-tuple-element.23), channel_id=1, source_target_pairs={{0,16},{16,0},{1,17},{17,1},{2,18},{18,2},{3,19},{19,3},{4,20},{20... | collective-permute-start | bytes 6291464 | tf_op jit(solution)/shard_map/ppermute | solution.py:348
  87.0 5.8 %collective-permute-start.10 = (f32[2,128]{1,0:T(2,128)S(1)}, f32[2,128]{1,0:T(2,128)S(1)}, u32[]{:S(2)}, u32[]{:S(2)}) collective-permute-start(f32[2,128]{1,0:T(2,128)S(1)} %bitcast.28), channel_id=1, source_target_pairs={{0,8},{8,0},{1,9},{9,1},{2,10},{10,2},{3,11},{11,3},{4,12},{12,4},... | collective-permute-start | bytes 3080 | tf_op jit(solution)/shard_map/ppermute | solution.py:343
  95.0 18.3 %collective-permute-start.13 = (bf16[512,512]{1,0:T(8,128)(2,1)S(1)}, bf16[512,512]{1,0:T(8,128)(2,1)}, u32[]{:S(2)}, u32[]{:S(2)}) collective-permute-start(bf16[512,512]{1,0:T(8,128)(2,1)S(1)} %get-tuple-element.26.refs_1_), channel_id=1, source_target_pairs={{0,64},{64,128},{128,192},{192,0},{1,65},{65,129},{129,193},{193,1... | collective-permute-start | bytes 1572872 | tf_op jit(solution)/shard_map/ppermute | solution.py:364
  95.6 17.6 %collective-permute-start.14 = (bf16[512,512]{1,0:T(8,128)(2,1)S(1)}, bf16[512,512]{1,0:T(8,128)(2,1)}, u32[]{:S(2)}, u32[]{:S(2)}) collective-permute-start(bf16[512,512]{1,0:T(8,128)(2,1)S(1)} %get-tuple-element.27.refs_0_), channel_id=1, source_target_pairs={{0,192},{64,0},{128,64},{192,128},{1,193},{65,1},{129,65},{193,129... | collective-permute-start | bytes 1572872 | tf_op jit(solution)/shard_map/ppermute | solution.py:365
  98.5 13.4 %collective-permute-start.11 = (bf16[128,1024]{1,0:T(8,128)(2,1)S(1)}, bf16[128,1024]{1,0:T(8,128)(2,1)S(1)}, u32[]{:S(2)}, u32[]{:S(2)}) collective-permute-start(bf16[128,1024]{1,0:T(8,128)(2,1)S(1)} %constant_dynamic-update-slice_fusion), channel_id=1, source_target_pairs={{0,5},{8,13},{16,21},{24,29},{32,37},{40,45},{48,53},{56,61},{64,6... | collective-permute-start | bytes 786440 | tf_op jit(solution)/shard_map/ppermute | solution.py:354
  107.2 6.0 %collective-permute-start.12 = (bf16[128,1024]{1,0:T(8,128)(2,1)S(1)}, bf16[128,1024]{1,0:T(8,128)(2,1)S(1)}, u32[]{:S(2)}, u32[]{:S(2)}) collective-permute-start(bf16[128,1024]{1,0:T(8,128)(2,1)S(1)} %constant_dynamic-update-slice_fusion), channel_id=1, source_target_pairs={{0,3},{8,11},{16,19},{24,27},{32,35},{40,43},{48,51},{56,59},{64,6... | collective-permute-start | bytes 786440 | tf_op jit(solution)/shard_map/ppermute | solution.py:353
  108.5 15.9 %collective-permute-start.17 = (bf16[512,512]{1,0:T(8,128)(2,1)S(1)}, bf16[512,512]{1,0:T(8,128)(2,1)S(1)}, u32[]{:S(2)}, u32[]{:S(2)}) collective-permute-start(bf16[512,512]{1,0:T(8,128)(2,1)S(1)} %get-tuple-element.27.refs_0_), channel_id=1, source_target_pairs={{0,64},{64,128},{128,192},{192,0},{1,65},{65,129},{129,193},{193,1... | collective-permute-start | bytes 1572872 | tf_op jit(solution)/shard_map/ppermute | solution.py:368
  111.9 14.9 %collective-permute-start.18 = (bf16[512,512]{1,0:T(8,128)(2,1)S(1)}, bf16[512,512]{1,0:T(8,128)(2,1)S(1)}, u32[]{:S(2)}, u32[]{:S(2)}) collective-permute-start(bf16[512,512]{1,0:T(8,128)(2,1)S(1)} %get-tuple-element.26.refs_1_), channel_id=1, source_target_pairs={{0,192},{64,0},{128,64},{192,128},{1,193},{65,1},{129,65},{193,129... | collective-permute-start | bytes 1572872 | tf_op jit(solution)/shard_map/ppermute | solution.py:369
  113.3 10.6 %collective-permute-start.15 = (bf16[128,1024]{1,0:T(8,128)(2,1)S(1)}, bf16[128,1024]{1,0:T(8,128)(2,1)S(1)}, u32[]{:S(2)}, u32[]{:S(2)}) collective-permute-start(bf16[128,1024]{1,0:T(8,128)(2,1)S(1)} %select_select_fusion.2), channel_id=1, source_target_pairs={{0,7},{3,2},{8,15},{11,10},{16,23},{19,18},{24,31},{27,26},{32,39}... | collective-permute-start | bytes 786440 | tf_op jit(solution)/shard_map/ppermute | solution.py:354
  120.5 15.0 %collective-permute-start.22 = (bf16[512,512]{1,0:T(8,128)(2,1)}, bf16[512,512]{1,0:T(8,128)(2,1)}, u32[]{:S(2)}, u32[]{:S(2)}) collective-permute-start(bf16[512,512]{1,0:T(8,128)(2,1)} %collective-permute-done.14.refs_4_), channel_id=1, source_target_pairs={{0,192},{64,0},{128,64},{192,128},{1,193},{65,1},{129,65},{193,129... | collective-permute-start | bytes 1572872 | tf_op jit(solution)/shard_map/ppermute | solution.py:373
  123.8 11.6 %collective-permute-start.23 = (bf16[512,512]{1,0:T(8,128)(2,1)}, bf16[512,512]{1,0:T(8,128)(2,1)}, u32[]{:S(2)}, u32[]{:S(2)}) collective-permute-start(bf16[512,512]{1,0:T(8,128)(2,1)} %collective-permute-done.13.refs_3_), channel_id=1, source_target_pairs={{0,64},{64,128},{128,192},{192,0},{1,65},{65,129},{129,193},{193,1... | collective-permute-start | bytes 1572872 | tf_op jit(solution)/shard_map/ppermute | solution.py:374
  127.6 7.9 %collective-permute-start.21 = (bf16[128,1024]{1,0:T(8,128)(2,1)S(1)}, bf16[128,1024]{1,0:T(8,128)(2,1)S(1)}, u32[]{:S(2)}, u32[]{:S(2)}) collective-permute-start(bf16[128,1024]{1,0:T(8,128)(2,1)S(1)} %select_select_fusion.refs_0_), channel_id=1, source_target_pairs={{0,32},{8,40},{32,0},{40,8},{1,33},{9,41},{33,1},{41,9},{2,34},{10... | collective-permute-start | bytes 786440 | tf_op jit(solution)/shard_map/ppermute | solution.py:375
  128.7 9.2 %collective-permute-start.19 = (bf16[128,1024]{1,0:T(8,128)(2,1)S(1)}, bf16[128,1024]{1,0:T(8,128)(2,1)S(1)}, u32[]{:S(2)}, u32[]{:S(2)}) collective-permute-start(bf16[128,1024]{1,0:T(8,128)(2,1)S(1)} %select_select_fusion.refs_0_), channel_id=1, source_target_pairs={{0,8},{8,32},{32,40},{40,0},{1,9},{9,33},{33,41},{41,1},{2,10},{10... | collective-permute-start | bytes 786440 | tf_op jit(solution)/shard_map/ppermute | solution.py:371
  131.6 6.7 %collective-permute-start.20 = (bf16[128,1024]{1,0:T(8,128)(2,1)S(1)}, bf16[128,1024]{1,0:T(8,128)(2,1)S(1)}, u32[]{:S(2)}, u32[]{:S(2)}) collective-permute-start(bf16[128,1024]{1,0:T(8,128)(2,1)S(1)} %select_select_fusion.refs_0_), channel_id=1, source_target_pairs={{0,40},{8,0},{32,8},{40,32},{1,41},{9,1},{33,9},{41,33},{2,42},{10... | collective-permute-start | bytes 786440 | tf_op jit(solution)/shard_map/ppermute | solution.py:372
  (11 other events, 110.6 us)

commit v7 on v6

--- a/solution.py
+++ b/solution.py
@@ -116,10 +116,12 @@
 
         @pl.when((xl == 0) & (i == 0))
         def _():
-            for copy in slabs[0] + slabs[1]:
+            for copy in slabs[0]:
                 copy.start()
             for copy in slabs[0]:
                 copy.wait()
+            for copy in slabs[1]:
+                copy.start()
 
         @pl.when((xl == 1) & (i == 0))
         def _():

time: 210 us -> 210 us (level)
  no operation moved by 1% of the time
where the time goes in v7:
time: 210 us; the launch traced here: 208 us
  starting transfers between devices  62.5 us (30%)
  blocking collectives  54.4 us (26%)
  waiting for transfers between devices  51.4 us (24%)
  Pallas kernels  29 us (14%)
  local copies, waits for them, and re-layouts  9.03 us (4%)
    all_to_all x1, blocking collectives, exchange(): return lax.all_to_all(block, axes, split_axis=0, concat_axis=0, tiled=True)  54.4 us
    ppermute x3, waiting for transfers between devices, per_device(): low = lax.ppermute(low, 'z', shift('z', 1))  24.7 us
    ppermute x2, starting transfers between devices, reach(): lax.ppermute(held, 'z', [(i, (i - step) % DEPTH) for i in sources[1]])  14.6 us
    all_to_all x2, starting transfers between devices, exchange(): return lax.all_to_all(block, axes, split_axis=0, concat_axis=0, tiled=True)  13.2 us
    ppermute x3, starting transfers between devices, per_device(): high = lax.ppermute(high, 'z', shift('z', -1))  10.5 us
    pallas_call x1, Pallas kernels, encode(): pl.pallas_call(body, out_shape=(jax.ShapeDtypeStruct((total, mine), jnp.f...  9.41 us
    pallas_call x1, Pallas kernels, gram(): pl.pallas_call(body, out_shape=jax.ShapeDtypeStruct((2 * CORES, XLO, 2 *...  8.73 us
    unnamed x17, local copies, waits for them, and re-layouts  5.99 us
  transfers between devices with their start and end apart: 27, of which 15 were waited for; matrix products, arithmetic and copies ran while one was open for 1% of the time, Pallas kernels for 4%

profile of v7, /device:TPU:2, one launch (start us, length us, event | category | flops | bytes accessed | tf_op | source)
XLA Modules:
  0.0 208.2 jit_solution(12645376456132627260)
XLA Ops:
  4.7 7.5 %all-to-all-start = ((bf16[16,8,1792]{2,1,0:T(8,128)(2,1)}), bf16[16,8,1792]{2,1,0:T(8,128)(2,1)S(1)}, u32[]{:S(2)}, u32[]{:S(2)}) async-start(bf16[16,8,1792]{2,1,0:T(8,128)(2,1)} %broadcast_in_dim.2), calls=%async_computation | async-start | bytes 917504 | tf_op jit(solution)/shard_map/all_to_all | solution.py:37
  12.2 4.7 %shard_map.47 = bf16[16,224,512]{2,1,0:T(8,128)(2,1)} custom-call(bf16[224,8192]{1,0:T(8,128)(2,1)} %in_ref.1), custom_call_target="tpu_custom_call" | custom-call | bytes 7340032 | tf_op jit(solution)/shard_map/pallas_call | solution.py:58
  16.9 5.0 %all-to-all-done = bf16[16,8,1792]{2,1,0:T(8,128)(2,1)S(1)} async-done(((bf16[16,8,1792]{2,1,0:T(8,128)(2,1)}), bf16[16,8,1792]{2,1,0:T(8,128)(2,1)S(1)}, u32[]{:S(2)}, u32[]{:S(2)}) %all-to-all-start) | async-done | bytes 458784 | tf_op jit(solution)/shard_map/all_to_all | solution.py:37
  21.9 5.7 %all-to-all-start.1 = ((bf16[16,224,512]{2,1,0:T(8,128)(2,1)}), bf16[16,224,512]{2,1,0:T(8,128)(2,1)}, u32[]{:S(2)}, u32[]{:S(2)}) async-start(bf16[16,224,512]{2,1,0:T(8,128)(2,1)} %shard_map.47), calls=%async_computation.1 | async-start | bytes 7340032 | tf_op jit(solution)/shard_map/all_to_all | solution.py:37
  29.6 4.0 %collective-permute-start.2 = (bf16[128,1792]{1,0:T(8,128)(2,1)S(1)}, bf16[128,1792]{1,0:T(8,128)(2,1)S(1)}, u32[]{:S(2)}, u32[]{:S(2)}) collective-permute-start(bf16[128,1792]{1,0:T(8,128)(2,1)S(1)} %bitcast.22), channel_id=1, source_target_pairs={{0,7},{1,0},{2,1},{3,2},{4,3},{5,4},{6,5},{7,6},{8,15},{9,8},{10,9... | collective-permute-start | bytes 1376264 | tf_op jit(solution)/shard_map/ppermute | solution.py:333
  33.6 9.0 %collective-permute-done.1.refs_1_ = bf16[128,1792]{1,0:T(8,128)(2,1)S(1)} collective-permute-done((bf16[128,1792]{1,0:T(8,128)(2,1)S(1)}, bf16[128,1792]{1,0:T(8,128)(2,1)S(1)}, u32[]{:S(2)}, u32[]{:S(2)}) %collective-permute-start.1) | collective-permute-done | bytes 458784 | tf_op jit(solution)/shard_map/ppermute | solution.py:332
  42.6 3.2 %collective-permute-start.4 = (bf16[128,1792]{1,0:T(8,128)(2,1)S(1)}, bf16[128,1792]{1,0:T(8,128)(2,1)S(1)}, u32[]{:S(2)}, u32[]{:S(2)}) collective-permute-start(bf16[128,1792]{1,0:T(8,128)(2,1)S(1)} %collective-permute-done.2.refs_2_), channel_id=1, source_target_pairs={{0,7},{1,0},{2,1},{3,2},{4,3},{5,4},{6,5},{7,6},{8,15},{9,8},{10,9... | collective-permute-start | bytes 1376264 | tf_op jit(solution)/shard_map/ppermute | solution.py:333
  45.8 8.3 %collective-permute-done.3.refs_3_ = bf16[128,1792]{1,0:T(8,128)(2,1)S(1)} collective-permute-done((bf16[128,1792]{1,0:T(8,128)(2,1)S(1)}, bf16[128,1792]{1,0:T(8,128)(2,1)S(1)}, u32[]{:S(2)}, u32[]{:S(2)}) %collective-permute-start.3) | collective-permute-done | bytes 458784 | tf_op jit(solution)/shard_map/ppermute | solution.py:332
  54.1 3.2 %collective-permute-start.6 = (bf16[128,1792]{1,0:T(8,128)(2,1)S(1)}, bf16[128,1792]{1,0:T(8,128)(2,1)S(1)}, u32[]{:S(2)}, u32[]{:S(2)}) collective-permute-start(bf16[128,1792]{1,0:T(8,128)(2,1)S(1)} %collective-permute-done.4.refs_4_), channel_id=1, source_target_pairs={{0,7},{1,0},{2,1},{3,2},{4,3},{5,4},{6,5},{7,6},{8,15},{9,8},{10,9... | collective-permute-start | bytes 1376264 | tf_op jit(solution)/shard_map/ppermute | solution.py:333
  57.3 7.4 %collective-permute-done.5.refs_5_ = bf16[128,1792]{1,0:T(8,128)(2,1)S(1)} collective-permute-done((bf16[128,1792]{1,0:T(8,128)(2,1)S(1)}, bf16[128,1792]{1,0:T(8,128)(2,1)S(1)}, u32[]{:S(2)}, u32[]{:S(2)}) %collective-permute-start.5) | collective-permute-done | bytes 458784 | tf_op jit(solution)/shard_map/ppermute | solution.py:332
  64.9 3.3 %collective-permute-start.8 = (bf16[64,1792]{1,0:T(8,128)(2,1)S(1)}, bf16[64,1792]{1,0:T(8,128)(2,1)S(1)}, u32[]{:S(2)}, u32[]{:S(2)}) collective-permute-start(bf16[64,1792]{1,0:T(8,128)(2,1)S(1)} %slice.23), channel_id=1, source_target_pairs={{0,7},{1,0},{2,1},{3,2},{4,3},{5,4},{6,5},{7,6},{8,15},{9,8},{10,9... | collective-permute-start | bytes 688136 | tf_op jit(solution)/shard_map/ppermute | solution.py:337
  68.2 3.9 %collective-permute-done.7.refs_7_ = bf16[64,1792]{1,0:T(8,128)(2,1)S(1)} collective-permute-done((bf16[64,1792]{1,0:T(8,128)(2,1)S(1)}, bf16[64,1792]{1,0:T(8,128)(2,1)S(1)}, u32[]{:S(2)}, u32[]{:S(2)}) %collective-permute-start.7) | collective-permute-done | bytes 229408 | tf_op jit(solution)/shard_map/ppermute | solution.py:336
  72.1 2.8 %shard_map.46.batch_ref = bf16[1024,1792]{1,0:T(8,128)(2,1)S(1)} custom-call(s32[1]{0:T(128)} %bitcast.2.z_ref, bf16[128,1792]{1,0:T(8,128)(2,1)S(1)} %bitcast.23, bf16[128,1792]{1,0:T(8,128)(2,1)S(1)} %collective-permute-done.1.refs_1_, bf16[128,1792]{1,0:T(8,128)(2,1)S(1)} %collective-permute-done.2.refs_2_, ...), custom_call_target="tpu_custom_call" | custom-call | bytes 7340032 | tf_op jit(solution)/shard_map/pallas_call | solution.py:85
  76.7 9.4 %shard_map.48 = (f32[1024,512]{1,0:T(8,128)}, f32[1024,512]{1,0:T(8,128)}) custom-call(s32[1]{0:T(128)} %bitcast.core_ref, bf16[1024,1792]{1,0:T(8,128)(2,1)} %copy-done.1, bf16[16,224,512]{2,1,0:T(8,128)(2,1)} %all-to-all-done.1.weight_ref), custom_call_target="tpu_custom_call" | custom-call | flops 3758096384 | bytes 11534336 | tf_op jit(solution)/shard_map/pallas_call | solution.py:141
  87.0 4.2 %collective-permute-start.10 = (f32[2,128]{1,0:T(2,128)S(1)}, f32[2,128]{1,0:T(2,128)S(1)}, u32[]{:S(2)}, u32[]{:S(2)}) collective-permute-start(f32[2,128]{1,0:T(2,128)S(1)} %bitcast.28), channel_id=1, source_target_pairs={{0,8},{8,0},{1,9},{9,1},{2,10},{10,2},{3,11},{11,3},{4,12},{12,4},... | collective-permute-start | bytes 3080 | tf_op jit(solution)/shard_map/ppermute | solution.py:345
  95.6 2.8 %collective-permute-start.14 = (bf16[512,512]{1,0:T(8,128)(2,1)S(1)}, bf16[512,512]{1,0:T(8,128)(2,1)}, u32[]{:S(2)}, u32[]{:S(2)}) collective-permute-start(bf16[512,512]{1,0:T(8,128)(2,1)S(1)} %get-tuple-element.27.refs_0_), channel_id=1, source_target_pairs={{0,192},{64,0},{128,64},{192,128},{1,193},{65,1},{129,65},{193,129... | collective-permute-start | bytes 1572872 | tf_op jit(solution)/shard_map/ppermute | solution.py:367
  98.5 8.7 %collective-permute-start.11 = (bf16[128,1024]{1,0:T(8,128)(2,1)S(1)}, bf16[128,1024]{1,0:T(8,128)(2,1)S(1)}, u32[]{:S(2)}, u32[]{:S(2)}) collective-permute-start(bf16[128,1024]{1,0:T(8,128)(2,1)S(1)} %constant_dynamic-update-slice_fusion), channel_id=1, source_target_pairs={{0,5},{8,13},{16,21},{24,29},{32,37},{40,45},{48,53},{56,61},{64,6... | collective-permute-start | bytes 786440 | tf_op jit(solution)/shard_map/ppermute | solution.py:356
  108.6 3.3 %collective-permute-done.11 = bf16[128,1024]{1,0:T(8,128)(2,1)S(1)} collective-permute-done((bf16[128,1024]{1,0:T(8,128)(2,1)S(1)}, bf16[128,1024]{1,0:T(8,128)(2,1)S(1)}, u32[]{:S(2)}, u32[]{:S(2)}) %collective-permute-start.11) | collective-permute-done | bytes 262176 | tf_op jit(solution)/shard_map/ppermute | solution.py:356
  113.3 5.9 %collective-permute-start.15 = (bf16[128,1024]{1,0:T(8,128)(2,1)S(1)}, bf16[128,1024]{1,0:T(8,128)(2,1)S(1)}, u32[]{:S(2)}, u32[]{:S(2)}) collective-permute-start(bf16[128,1024]{1,0:T(8,128)(2,1)S(1)} %select_select_fusion.2), channel_id=1, source_target_pairs={{0,7},{3,2},{8,15},{11,10},{16,23},{19,18},{24,31},{27,26},{32,39}... | collective-permute-start | bytes 786440 | tf_op jit(solution)/shard_map/ppermute | solution.py:356
  120.5 3.3 %collective-permute-start.22 = (bf16[512,512]{1,0:T(8,128)(2,1)}, bf16[512,512]{1,0:T(8,128)(2,1)}, u32[]{:S(2)}, u32[]{:S(2)}) collective-permute-start(bf16[512,512]{1,0:T(8,128)(2,1)} %collective-permute-done.14.refs_4_), channel_id=1, source_target_pairs={{0,192},{64,0},{128,64},{192,128},{1,193},{65,1},{129,65},{193,129... | collective-permute-start | bytes 1572872 | tf_op jit(solution)/shard_map/ppermute | solution.py:375
  128.7 2.9 %collective-permute-start.19 = (bf16[128,1024]{1,0:T(8,128)(2,1)S(1)}, bf16[128,1024]{1,0:T(8,128)(2,1)S(1)}, u32[]{:S(2)}, u32[]{:S(2)}) collective-permute-start(bf16[128,1024]{1,0:T(8,128)(2,1)S(1)} %select_select_fusion.refs_0_), channel_id=1, source_target_pairs={{0,8},{8,32},{32,40},{40,0},{1,9},{9,33},{33,41},{41,1},{2,10},{10... | collective-permute-start | bytes 786440 | tf_op jit(solution)/shard_map/ppermute | solution.py:373
  131.6 3.9 %collective-permute-done.21.refs_3_ = bf16[128,1024]{1,0:T(8,128)(2,1)S(1)} collective-permute-done((bf16[128,1024]{1,0:T(8,128)(2,1)S(1)}, bf16[128,1024]{1,0:T(8,128)(2,1)S(1)}, u32[]{:S(2)}, u32[]{:S(2)}) %collective-permute-start.21) | collective-permute-done | bytes 262176 | tf_op jit(solution)/shard_map/ppermute | solution.py:377
  142.1 8.7 %shard_map.51 = bf16[4,2,8,256,128]{4,3,2,1,0:T(8,128)(2,1)} custom-call(s32[1]{0:T(128)} %bitcast.core_ref, bf16[4,128,1024]{2,1,0:T(8,128)(2,1)} %copy-done.2, bf16[4,128,1024]{2,1,0:T(8,128)(2,1)} %copy-done.5, bf16[512,512]{1,0:T(8,128)(2,1)} %copy-done.3, bf16[512,512]{1,0:T(8,128)(2,1)} %copy-done.4, bf16[512,512]{1,0:T(8,128)(2,1)} %copy-done.6, ...), custom_call_target="tpu_custom_call" | custom-call | flops 4294967296 | bytes 10485760 | tf_op jit(solution)/shard_map/pallas_call | solution.py:248
  150.9 54.4 %all_to_all.15.in_ref = bf16[8,8,256,128]{3,2,1,0:T(8,128)(2,1)S(1)} all-to-all(bf16[8,8,256,128]{3,2,1,0:T(8,128)(2,1)} %bitcast.25), channel_id=1, replica_groups=mesh['y'=4,'xh'=2,'c'=2,'xl'=2,'z'=8] {'xh','c','xl'}, dimensions={0} | all-to-all | bytes 8388608 | tf_op jit(solution)/shard_map/all_to_all | solution.py:37
  (71 shorter events, 32.0 us)
Async XLA Ops:
  4.7 17.2 %all-to-all-start = ((bf16[16,8,1792]{2,1,0:T(8,128)(2,1)}), bf16[16,8,1792]{2,1,0:T(8,128)(2,1)S(1)}, u32[]{:S(2)}, u32[]{:S(2)}) async-start(bf16[16,8,1792]{2,1,0:T(8,128)(2,1)} %broadcast_in_dim.2), calls=%async_computation | async-start | bytes 917504 | tf_op jit(solution)/shard_map/all_to_all | solution.py:37
  21.9 54.8 %all-to-all-start.1 = ((bf16[16,224,512]{2,1,0:T(8,128)(2,1)}), bf16[16,224,512]{2,1,0:T(8,128)(2,1)}, u32[]{:S(2)}, u32[]{:S(2)}) async-start(bf16[16,224,512]{2,1,0:T(8,128)(2,1)} %shard_map.47), calls=%async_computation.1 | async-start | bytes 7340032 | tf_op jit(solution)/shard_map/all_to_all | solution.py:37
  27.6 14.9 %collective-permute-start.1 = (bf16[128,1792]{1,0:T(8,128)(2,1)S(1)}, bf16[128,1792]{1,0:T(8,128)(2,1)S(1)}, u32[]{:S(2)}, u32[]{:S(2)}) collective-permute-start(bf16[128,1792]{1,0:T(8,128)(2,1)S(1)} %bitcast.21), channel_id=1, source_target_pairs={{0,1},{1,2},{2,3},{3,4},{4,5},{5,6},{6,7},{7,0},{8,9},{9,10},{10,1... | collective-permute-start | bytes 1376264 | tf_op jit(solution)/shard_map/ppermute | solution.py:332
  29.6 13.0 %collective-permute-start.2 = (bf16[128,1792]{1,0:T(8,128)(2,1)S(1)}, bf16[128,1792]{1,0:T(8,128)(2,1)S(1)}, u32[]{:S(2)}, u32[]{:S(2)}) collective-permute-start(bf16[128,1792]{1,0:T(8,128)(2,1)S(1)} %bitcast.22), channel_id=1, source_target_pairs={{0,7},{1,0},{2,1},{3,2},{4,3},{5,4},{6,5},{7,6},{8,15},{9,8},{10,9... | collective-permute-start | bytes 1376264 | tf_op jit(solution)/shard_map/ppermute | solution.py:333
  42.6 11.5 %collective-permute-start.3 = (bf16[128,1792]{1,0:T(8,128)(2,1)S(1)}, bf16[128,1792]{1,0:T(8,128)(2,1)S(1)}, u32[]{:S(2)}, u32[]{:S(2)}) collective-permute-start(bf16[128,1792]{1,0:T(8,128)(2,1)S(1)} %collective-permute-done.1.refs_1_), channel_id=1, source_target_pairs={{0,1},{1,2},{2,3},{3,4},{4,5},{5,6},{6,7},{7,0},{8,9},{9,10},{10,1... | collective-permute-start | bytes 1376264 | tf_op jit(solution)/shard_map/ppermute | solution.py:332
  42.6 11.5 %collective-permute-start.4 = (bf16[128,1792]{1,0:T(8,128)(2,1)S(1)}, bf16[128,1792]{1,0:T(8,128)(2,1)S(1)}, u32[]{:S(2)}, u32[]{:S(2)}) collective-permute-start(bf16[128,1792]{1,0:T(8,128)(2,1)S(1)} %collective-permute-done.2.refs_2_), channel_id=1, source_target_pairs={{0,7},{1,0},{2,1},{3,2},{4,3},{5,4},{6,5},{7,6},{8,15},{9,8},{10,9... | collective-permute-start | bytes 1376264 | tf_op jit(solution)/shard_map/ppermute | solution.py:333
  54.1 10.7 %collective-permute-start.5 = (bf16[128,1792]{1,0:T(8,128)(2,1)S(1)}, bf16[128,1792]{1,0:T(8,128)(2,1)S(1)}, u32[]{:S(2)}, u32[]{:S(2)}) collective-permute-start(bf16[128,1792]{1,0:T(8,128)(2,1)S(1)} %collective-permute-done.3.refs_3_), channel_id=1, source_target_pairs={{0,1},{1,2},{2,3},{3,4},{4,5},{5,6},{6,7},{7,0},{8,9},{9,10},{10,1... | collective-permute-start | bytes 1376264 | tf_op jit(solution)/shard_map/ppermute | solution.py:332
  54.1 10.8 %collective-permute-start.6 = (bf16[128,1792]{1,0:T(8,128)(2,1)S(1)}, bf16[128,1792]{1,0:T(8,128)(2,1)S(1)}, u32[]{:S(2)}, u32[]{:S(2)}) collective-permute-start(bf16[128,1792]{1,0:T(8,128)(2,1)S(1)} %collective-permute-done.4.refs_4_), channel_id=1, source_target_pairs={{0,7},{1,0},{2,1},{3,2},{4,3},{5,4},{6,5},{7,6},{8,15},{9,8},{10,9... | collective-permute-start | bytes 1376264 | tf_op jit(solution)/shard_map/ppermute | solution.py:333
  64.8 7.3 %collective-permute-start.7 = (bf16[64,1792]{1,0:T(8,128)(2,1)S(1)}, bf16[64,1792]{1,0:T(8,128)(2,1)S(1)}, u32[]{:S(2)}, u32[]{:S(2)}) collective-permute-start(bf16[64,1792]{1,0:T(8,128)(2,1)S(1)} %slice.22), channel_id=1, source_target_pairs={{0,1},{1,2},{2,3},{3,4},{4,5},{5,6},{6,7},{7,0},{8,9},{9,10},{10,1... | collective-permute-start | bytes 688136 | tf_op jit(solution)/shard_map/ppermute | solution.py:336
  64.9 7.2 %collective-permute-start.8 = (bf16[64,1792]{1,0:T(8,128)(2,1)S(1)}, bf16[64,1792]{1,0:T(8,128)(2,1)S(1)}, u32[]{:S(2)}, u32[]{:S(2)}) collective-permute-start(bf16[64,1792]{1,0:T(8,128)(2,1)S(1)} %slice.23), channel_id=1, source_target_pairs={{0,7},{1,0},{2,1},{3,2},{4,3},{5,4},{6,5},{7,6},{8,15},{9,8},{10,9... | collective-permute-start | bytes 688136 | tf_op jit(solution)/shard_map/ppermute | solution.py:337
  86.1 6.7 %collective-permute-start.9 = (f32[1024,512]{1,0:T(8,128)}, f32[1024,512]{1,0:T(8,128)S(1)}, u32[]{:S(2)}, u32[]{:S(2)}) collective-permute-start(f32[1024,512]{1,0:T(8,128)} %get-tuple-element.23), channel_id=1, source_target_pairs={{0,16},{16,0},{1,17},{17,1},{2,18},{18,2},{3,19},{19,3},{4,20},{20... | collective-permute-start | bytes 6291464 | tf_op jit(solution)/shard_map/ppermute | solution.py:350
  87.0 5.8 %collective-permute-start.10 = (f32[2,128]{1,0:T(2,128)S(1)}, f32[2,128]{1,0:T(2,128)S(1)}, u32[]{:S(2)}, u32[]{:S(2)}) collective-permute-start(f32[2,128]{1,0:T(2,128)S(1)} %bitcast.28), channel_id=1, source_target_pairs={{0,8},{8,0},{1,9},{9,1},{2,10},{10,2},{3,11},{11,3},{4,12},{12,4},... | collective-permute-start | bytes 3080 | tf_op jit(solution)/shard_map/ppermute | solution.py:345
  95.0 18.3 %collective-permute-start.13 = (bf16[512,512]{1,0:T(8,128)(2,1)S(1)}, bf16[512,512]{1,0:T(8,128)(2,1)}, u32[]{:S(2)}, u32[]{:S(2)}) collective-permute-start(bf16[512,512]{1,0:T(8,128)(2,1)S(1)} %get-tuple-element.26.refs_1_), channel_id=1, source_target_pairs={{0,64},{64,128},{128,192},{192,0},{1,65},{65,129},{129,193},{193,1... | collective-permute-start | bytes 1572872 | tf_op jit(solution)/shard_map/ppermute | solution.py:366
  95.6 17.6 %collective-permute-start.14 = (bf16[512,512]{1,0:T(8,128)(2,1)S(1)}, bf16[512,512]{1,0:T(8,128)(2,1)}, u32[]{:S(2)}, u32[]{:S(2)}) collective-permute-start(bf16[512,512]{1,0:T(8,128)(2,1)S(1)} %get-tuple-element.27.refs_0_), channel_id=1, source_target_pairs={{0,192},{64,0},{128,64},{192,128},{1,193},{65,1},{129,65},{193,129... | collective-permute-start | bytes 1572872 | tf_op jit(solution)/shard_map/ppermute | solution.py:367
  98.5 13.4 %collective-permute-start.11 = (bf16[128,1024]{1,0:T(8,128)(2,1)S(1)}, bf16[128,1024]{1,0:T(8,128)(2,1)S(1)}, u32[]{:S(2)}, u32[]{:S(2)}) collective-permute-start(bf16[128,1024]{1,0:T(8,128)(2,1)S(1)} %constant_dynamic-update-slice_fusion), channel_id=1, source_target_pairs={{0,5},{8,13},{16,21},{24,29},{32,37},{40,45},{48,53},{56,61},{64,6... | collective-permute-start | bytes 786440 | tf_op jit(solution)/shard_map/ppermute | solution.py:356
  107.2 6.0 %collective-permute-start.12 = (bf16[128,1024]{1,0:T(8,128)(2,1)S(1)}, bf16[128,1024]{1,0:T(8,128)(2,1)S(1)}, u32[]{:S(2)}, u32[]{:S(2)}) collective-permute-start(bf16[128,1024]{1,0:T(8,128)(2,1)S(1)} %constant_dynamic-update-slice_fusion), channel_id=1, source_target_pairs={{0,3},{8,11},{16,19},{24,27},{32,35},{40,43},{48,51},{56,59},{64,6... | collective-permute-start | bytes 786440 | tf_op jit(solution)/shard_map/ppermute | solution.py:355
  108.5 15.9 %collective-permute-start.17 = (bf16[512,512]{1,0:T(8,128)(2,1)S(1)}, bf16[512,512]{1,0:T(8,128)(2,1)S(1)}, u32[]{:S(2)}, u32[]{:S(2)}) collective-permute-start(bf16[512,512]{1,0:T(8,128)(2,1)S(1)} %get-tuple-element.27.refs_0_), channel_id=1, source_target_pairs={{0,64},{64,128},{128,192},{192,0},{1,65},{65,129},{129,193},{193,1... | collective-permute-start | bytes 1572872 | tf_op jit(solution)/shard_map/ppermute | solution.py:370
  111.9 14.9 %collective-permute-start.18 = (bf16[512,512]{1,0:T(8,128)(2,1)S(1)}, bf16[512,512]{1,0:T(8,128)(2,1)S(1)}, u32[]{:S(2)}, u32[]{:S(2)}) collective-permute-start(bf16[512,512]{1,0:T(8,128)(2,1)S(1)} %get-tuple-element.26.refs_1_), channel_id=1, source_target_pairs={{0,192},{64,0},{128,64},{192,128},{1,193},{65,1},{129,65},{193,129... | collective-permute-start | bytes 1572872 | tf_op jit(solution)/shard_map/ppermute | solution.py:371
  113.3 10.6 %collective-permute-start.15 = (bf16[128,1024]{1,0:T(8,128)(2,1)S(1)}, bf16[128,1024]{1,0:T(8,128)(2,1)S(1)}, u32[]{:S(2)}, u32[]{:S(2)}) collective-permute-start(bf16[128,1024]{1,0:T(8,128)(2,1)S(1)} %select_select_fusion.2), channel_id=1, source_target_pairs={{0,7},{3,2},{8,15},{11,10},{16,23},{19,18},{24,31},{27,26},{32,39}... | collective-permute-start | bytes 786440 | tf_op jit(solution)/shard_map/ppermute | solution.py:356
  120.5 15.0 %collective-permute-start.22 = (bf16[512,512]{1,0:T(8,128)(2,1)}, bf16[512,512]{1,0:T(8,128)(2,1)}, u32[]{:S(2)}, u32[]{:S(2)}) collective-permute-start(bf16[512,512]{1,0:T(8,128)(2,1)} %collective-permute-done.14.refs_4_), channel_id=1, source_target_pairs={{0,192},{64,0},{128,64},{192,128},{1,193},{65,1},{129,65},{193,129... | collective-permute-start | bytes 1572872 | tf_op jit(solution)/shard_map/ppermute | solution.py:375
  123.8 11.7 %collective-permute-start.23 = (bf16[512,512]{1,0:T(8,128)(2,1)}, bf16[512,512]{1,0:T(8,128)(2,1)}, u32[]{:S(2)}, u32[]{:S(2)}) collective-permute-start(bf16[512,512]{1,0:T(8,128)(2,1)} %collective-permute-done.13.refs_3_), channel_id=1, source_target_pairs={{0,64},{64,128},{128,192},{192,0},{1,65},{65,129},{129,193},{193,1... | collective-permute-start | bytes 1572872 | tf_op jit(solution)/shard_map/ppermute | solution.py:376
  127.6 7.9 %collective-permute-start.21 = (bf16[128,1024]{1,0:T(8,128)(2,1)S(1)}, bf16[128,1024]{1,0:T(8,128)(2,1)S(1)}, u32[]{:S(2)}, u32[]{:S(2)}) collective-permute-start(bf16[128,1024]{1,0:T(8,128)(2,1)S(1)} %select_select_fusion.refs_0_), channel_id=1, source_target_pairs={{0,32},{8,40},{32,0},{40,8},{1,33},{9,41},{33,1},{41,9},{2,34},{10... | collective-permute-start | bytes 786440 | tf_op jit(solution)/shard_map/ppermute | solution.py:377
  128.7 9.2 %collective-permute-start.19 = (bf16[128,1024]{1,0:T(8,128)(2,1)S(1)}, bf16[128,1024]{1,0:T(8,128)(2,1)S(1)}, u32[]{:S(2)}, u32[]{:S(2)}) collective-permute-start(bf16[128,1024]{1,0:T(8,128)(2,1)S(1)} %select_select_fusion.refs_0_), channel_id=1, source_target_pairs={{0,8},{8,32},{32,40},{40,0},{1,9},{9,33},{33,41},{41,1},{2,10},{10... | collective-permute-start | bytes 786440 | tf_op jit(solution)/shard_map/ppermute | solution.py:373
  131.6 6.7 %collective-permute-start.20 = (bf16[128,1024]{1,0:T(8,128)(2,1)S(1)}, bf16[128,1024]{1,0:T(8,128)(2,1)S(1)}, u32[]{:S(2)}, u32[]{:S(2)}) collective-permute-start(bf16[128,1024]{1,0:T(8,128)(2,1)S(1)} %select_select_fusion.refs_0_), channel_id=1, source_target_pairs={{0,40},{8,0},{32,8},{40,32},{1,41},{9,1},{33,9},{41,33},{2,42},{10... | collective-permute-start | bytes 786440 | tf_op jit(solution)/shard_map/ppermute | solution.py:374
  (11 other events, 110.6 us)
